TPU v7x, 32 devices: a whole 2x2x4 slice. The times are simulated.
32 devices in a mesh: groups: 2 (over y), seq: 4 (over x, core), tensor: 4 (over z).
Axes of the slice: x: 2, y: 2, z: 4, core: 2. Of those that a mesh axis runs over, the one named last changes fastest.
Arguments:
- layer_input: bfloat16 [4096, 4096], P(('groups', 'seq'), 'tensor'), parts along dimension 0, may hold values from -6 to 6
- out_grad: bfloat16 [4096, 4096], P(('groups', 'seq'), 'tensor'), parts along dimension 0, may hold values from -6 to 6
- gate_pre: bfloat16 [4096, 14336], P(('groups', 'seq'), 'tensor'), parts along dimension 0, may hold values from -6 to 6
- up_pre: bfloat16 [4096, 14336], P(('groups', 'seq'), 'tensor'), parts along dimension 0, may hold values from -6 to 6
- w_down: bfloat16 [14336, 4096], P('tensor', 'seq'), may hold values from -0.046875 to 0.046875
- proj_in: bfloat16 [4096, 128], P('tensor'), may hold values from -0.09375 to 0.09375
- proj_ff: bfloat16 [14336, 192], P('tensor'), may hold values from -0.046875 to 0.046875
- proj_down: bfloat16 [4096, 64], replicated, may hold values from -0.09375 to 0.09375
- lengths: int32 [8], P('groups'), parts along dimension 0, may hold values from 1 to 1024, 2048 in all
- slots: int32 [8], P('groups'), parts along dimension 0, may hold values from 0 to 3, each once
Outputs:
- owned_sketches: float32 [8, 3, 64, 64], P('groups', None, 'tensor', 'seq'), parts along dimension 0
There are 2 independent parts, one for each index of `groups`. A program takes and returns all parts, laid end to end along the dimension named above; an argument that names none is the same for every part. Nothing has to cross between parts.
Inputs may be any that keep to these rules, and one draw needn't show every extreme that they name: The lengths of the 4 sequences sum to 2048; the longest is exactly 1024. `slots`: A permutation of the 4 output rows.
All inputs are finite; a program needn't handle non-finite values.
Results may differ from a plain program's by a relative error of at most 0.0029.
Values may be sent and summed in bfloat16 or wider, within the bound.
No kernel may reach another device: no remote copies, remote signals or barrier semaphores. Data moves between devices by JAX's collectives and lax.ppermute only.
A program may use at most 128 MiB of HBM per device.

v0:
```python
import jax
import jax.numpy as jnp
from jax import lax
from jax.sharding import PartitionSpec as P


def silu_pair(gates):
    sigma = jax.nn.sigmoid(gates)
    return (gates * sigma, sigma * (1.0 + gates * (1.0 - sigma)))


def local(
    layer_input, out_grad, gate_pre, up_pre, w_down, proj_in, proj_ff, proj_down, lengths, slots
):
    tokens_here = layer_input.shape[0]
    tensor_count = lax.axis_size("tensor")
    share = 64 // tensor_count
    whole_down = lax.all_gather(w_down, "seq", axis=1, tiled=True)
    piece = lax.all_gather(out_grad, "tensor", axis=1, tiled=True)
    grad_total = lax.dot_general(
        piece, whole_down, (((1,), (1,)), ((), ())), preferred_element_type=jnp.float32
    )
    right_total = jnp.dot(piece, proj_down, preferred_element_type=jnp.float32)
    gate_value = gate_pre.astype(jnp.float32)
    upper_value = up_pre.astype(jnp.float32)
    activated, slope = silu_pair(gate_value)
    hidden = (activated * upper_value).astype(jnp.bfloat16)
    gate_grad = (grad_total * upper_value * slope).astype(jnp.bfloat16)
    up_grad = (grad_total * activated).astype(jnp.bfloat16)
    in_side = jnp.dot(layer_input, proj_in, preferred_element_type=jnp.float32)
    down_left = jnp.dot(hidden, proj_ff[:, 128:192], preferred_element_type=jnp.float32)
    gate_right = jnp.dot(gate_grad, proj_ff[:, 0:64], preferred_element_type=jnp.float32)
    up_right = jnp.dot(up_grad, proj_ff[:, 64:128], preferred_element_type=jnp.float32)
    left_local = jnp.concatenate([in_side, down_left], axis=1)
    right_local = jnp.concatenate([gate_right, up_right], axis=1)
    tensor_place = lax.axis_index("tensor")
    left_full, right_summed = lax.psum((left_local, right_local), "tensor")
    left_mine = lax.dynamic_slice_in_dim(
        left_full.reshape(tokens_here, 3, 64), tensor_place * share, share, 2
    )
    right_all = jnp.concatenate([right_summed, right_total], axis=1).reshape(tokens_here, 3, 64)
    examples = lengths.shape[0]
    positions = lax.axis_index("seq") * tokens_here + jnp.arange(tokens_here, dtype=jnp.int32)
    ends = jnp.cumsum(lengths)
    starts = ends - lengths
    member = (
        (positions[:, None] >= starts[None, :]) & (positions[:, None] < ends[None, :])
    ).astype(jnp.float32)
    scale = lax.rsqrt(lengths.astype(jnp.float32))
    sketches = []
    for linear in range(3):
        weighted = (member[:, :, None] * left_mine[:, None, linear, :]).reshape(
            tokens_here, examples * share
        )
        sketch = lax.dot_general(
            weighted,
            right_all[:, linear, :],
            (((0,), (0,)), ((), ())),
            precision=lax.Precision.HIGHEST,
            preferred_element_type=jnp.float32,
        )
        sketches.append(sketch.reshape(examples, share * 64))
    stacked = jnp.stack(sketches, axis=1) * scale[:, None, None]
    placing = (slots[None, :] == jnp.arange(examples, dtype=jnp.int32)[:, None]).astype(jnp.float32)
    placed = jnp.dot(
        placing,
        stacked.reshape(examples, 3 * share * 64),
        precision=lax.Precision.HIGHEST,
        preferred_element_type=jnp.float32,
    )
    owned = lax.psum_scatter(
        placed.reshape(examples, 3, share, 64), "seq", scatter_dimension=3, tiled=True
    )
    return owned


def solution(mesh):
    placed = (
        P(("groups", "seq"), "tensor"),
        P(("groups", "seq"), "tensor"),
        P(("groups", "seq"), "tensor"),
        P(("groups", "seq"), "tensor"),
        P("tensor", "seq"),
        P("tensor", None),
        P("tensor", None),
        P(),
        P("groups"),
        P("groups"),
    )
    return jax.shard_map(
        local,
        mesh=mesh,
        in_specs=placed,
        out_specs=P("groups", None, "tensor", "seq"),
        check_vma=False,
    )
```

profile of v0, /device:TPU:0, one launch (start us, length us, event | category | flops | bytes accessed | tf_op | source)
XLA Modules:
  0.0 379.1 jit_solution(14335009822136997091)
XLA Ops:
  6.6 0.7 all-gather.3.cloned.1.call-update
  7.3 0.7 all-gather.5.cloned.1.call-update
  8.3 0.5 fusion.27
  8.8 4.6 %fusion.9 = f32[512,64]{0,1:T(8,128)S(1)} fusion(bf16[512,3584]{1,0:T(8,128)(2,1)} %param.13, bf16[512,3584]{1,0:T(8,128)(2,1)} %param.12, bf16[3584,192]{0,1:T(8,128)(2,1)S(1)} %copy-done.5), kind=kOutput, calls=%fused_computation.15 | convolution fusion | flops 249561088 | bytes 7929856 | tf_op jit(solution)/shard_map/dot_general | solution.py:31
  13.3 0.8 pad_maximum_fusion
  14.1 78.3 %all-gather.3.cloned.1.call-done = bf16[512,4096]{1,0:T(8,128)(2,1)} async-done(((bf16[512,1024]{1,0:T(8,128)(2,1)}), bf16[512,4096]{1,0:T(8,128)(2,1)}) %all-gather.3.cloned.1.call-update) | async-done | bytes 4194320 | tf_op jit(solution)/shard_map/all_gather | solution.py:19
  92.4 178.1 %all-gather.5.cloned.1.call-done = bf16[3584,4096]{1,0:T(8,128)(2,1)} async-done(((bf16[3584,1024]{1,0:T(8,128)(2,1)}), bf16[3584,4096]{1,0:T(8,128)(2,1)}) %all-gather.5.cloned.1.call-update) | async-done | bytes 29360144 | tf_op jit(solution)/shard_map/all_gather | solution.py:18
  270.6 23.4 %fusion.28 = f32[512,3584]{1,0:T(8,128)} fusion(bf16[512,4096]{1,0:T(8,128)(2,1)} %all-gather.3.cloned.1.call-done, bf16[3584,4096]{1,0:T(8,128)(2,1)} %all-gather.5.cloned.1.call-done), kind=kOutput, calls=%fused_computation.50 | convolution fusion | flops 15032385536 | bytes 40894464 | tf_op jit(solution)/shard_map/dot_general | solution.py:20
  294.0 7.0 %fusion.11 = f32[512,64]{0,1:T(8,128)S(1)} fusion(f32[512,3584]{1,0:T(8,128)} %fusion.28, bf16[512,3584]{1,0:T(8,128)(2,1)} %param.13, bf16[512,3584]{1,0:T(8,128)(2,1)} %param.12, bf16[3584,192]{0,1:T(8,128)(2,1)S(1)} %copy-done.5), kind=kOutput, calls=%fused_computation.16 | convolution fusion | flops 256901120 | bytes 15269888 | tf_op jit(solution)/shard_map/dot_general | solution.py:32
  301.0 1.4 copy-done.7
  302.4 2.1 fusion.8
  304.6 0.7 pad_maximum_fusion.2
  305.6 3.6 fusion.29
  309.2 37.0 %all-reduce.3.cloned.1.call-done = (f32[512,3,64]{0,2,1:T(8,128)}, f32[512,128]{0,1:T(8,128)}) async-done(((f32[512,3,64]{0,2,1:T(8,128)}, f32[512,128]{0,1:T(8,128)}), (f32[512,3,64]{0,2,1:T(8,128)}, f32[512,128]{0,1:T(8,128)})) %all-reduce.3.cloned.1.call-update) | async-done | bytes 655376 | tf_op jit(solution)/shard_map/psum | solution.py:37
  346.2 1.0 pad_maximum_fusion.1
  347.2 0.8 dynamic-slice_bitcast_fusion.2
  348.1 0.3 fusion.18
  348.4 0.3 fusion.17
  348.8 0.3 fusion.16
  349.5 0.8 copy.20
  350.3 1.3 reshape.138
  351.6 19.0 %reduce-scatter.4.cloned.1.call-done = f32[16,192]{1,0:T(8,128)} async-done(((f32[64,192]{1,0:T(8,128)}), f32[16,192]{1,0:T(8,128)}) %reduce-scatter.4.cloned.1.call-update) | async-done | bytes 12304
  370.6 0.9 reshape.139
  371.6 1.0 copy.18
  (34 shorter events, 1.4 us)
Async XLA Ops:
  6.5 1.7 copy-start
  6.5 1.5 copy-start.6
  6.5 1.7 copy-start.2
  6.5 2.2 copy-start.5
  6.5 85.9 %all-gather.3.cloned.1.call-start = ((), (), s32[]{:S(2)}) async-start(), calls=%async_computation.1 | async-start | bytes 5242880 | tf_op jit(solution)/shard_map/all_gather | solution.py:19
  7.3 263.3 %all-gather.5.cloned.1.call-start = ((), (), s32[]{:S(2)}) async-start(), calls=%async_computation.2 | async-start | bytes 36700160 | tf_op jit(solution)/shard_map/all_gather | solution.py:18
  8.0 338.2 %all-reduce.3.cloned.1.call-start = ((), (), s32[]{:S(2)}) async-start(), calls=%async_computation.4 | async-start | bytes 1310720 | tf_op jit(solution)/shard_map/psum | solution.py:37
  294.0 7.1 %copy-start.4 = (bf16[512,3584]{1,0:T(8,128)(2,1)S(1)}, bf16[512,3584]{1,0:T(8,128)(2,1)}, u32[]{:S(2)}) copy-start(bf16[512,3584]{1,0:T(8,128)(2,1)} %param.12) | copy-start | bytes 11010052
  294.0 8.4 %copy-start.7 = (f32[512,3584]{1,0:T(8,128)S(1)}, f32[512,3584]{1,0:T(8,128)}, u32[]{:S(2)}) copy-start(f32[512,3584]{1,0:T(8,128)} %fusion.28) | copy-start | bytes 22020100
  302.4 3.2 copy-start.1
  304.6 44.7 %copy-start.3 = (s32[4]{0:T(128)S(1)}, s32[4]{0:T(128)}, u32[]{:S(2)}) copy-start(s32[4]{0:T(128)} %param.19) | copy-start | bytes 52
  305.3 65.3 %reduce-scatter.4.cloned.1.call-start = ((), (), s32[]{:S(2)}) async-start(), calls=%async_computation.3 | async-start | bytes 81920
Sparse Core Ops, SparseCore 0:
  8.9 83.4 all-gather.2
  94.0 176.5 all-gather.4
  305.4 40.7 all-reduce.2
  351.7 18.8 reduce-scatter.3
where the time goes:
time: 379 us
  waiting for transfers between devices  314 us (83%)
  matrix products  42.2 us (11%)
  between operations  13.3 us (4%)
  local copies, waits for them, and re-layouts  6.54 us (2%)
    all_gather x1, waiting for transfers between devices, local(): whole_down = lax.all_gather(w_down, 'seq', axis=1, tiled=True)  178 us
    all_gather x1, waiting for transfers between devices, local(): piece = lax.all_gather(out_grad, 'tensor', axis=1, tiled=True)  78.3 us
    psum x1, waiting for transfers between devices, local(): left_full, right_summed = lax.psum((left_local, right_local), 'tensor')  37 us
    dot_general x1, matrix products, local(): lax.dot_general(piece, whole_down, (((1,), (1,)), ((), ())), preferred_el...  23.4 us
    unnamed x5, waiting for transfers between devices  20.4 us
  transfers between devices with their start and end apart: 4, of which 4 were waited for; matrix products, arithmetic and copies ran while one was open for 3% of the time, Pallas kernels for 0%

commit v1 on v0

v1 whole, which is shorter than its diff:
```python
import functools
import jax
import jax.numpy as jnp
from jax import lax
from jax.experimental import pallas as pl
from jax.experimental.pallas import tpu as pltpu
from jax.sharding import PartitionSpec as P

F32 = jnp.float32
BF16 = jnp.bfloat16
TILE = 256
CHUNKS = (256, 256, 256, 256, 256, 256, 256)
CALLS = (5, 1, 1)
DEPTH = 3


def silu_pair(gates):
    sigma = jax.nn.sigmoid(gates)
    return (gates * sigma, sigma * (1.0 + gates * (1.0 - sigma)))


def general(
    layer_input, out_grad, gate_pre, up_pre, w_down, proj_in, proj_ff, proj_down, lengths, slots
):
    tokens_here = layer_input.shape[0]
    tensor_count = lax.axis_size("tensor")
    share = 64 // tensor_count
    whole_down = lax.all_gather(w_down, "seq", axis=1, tiled=True)
    piece = lax.all_gather(out_grad, "tensor", axis=1, tiled=True)
    grad_total = lax.dot_general(
        piece, whole_down, (((1,), (1,)), ((), ())), preferred_element_type=F32
    )
    right_total = jnp.dot(piece, proj_down, preferred_element_type=F32)
    upper_value = up_pre.astype(F32)
    activated, slope = silu_pair(gate_pre.astype(F32))
    hidden = (activated * upper_value).astype(BF16)
    gate_grad = (grad_total * upper_value * slope).astype(BF16)
    up_grad = (grad_total * activated).astype(BF16)
    in_side = jnp.dot(layer_input, proj_in, preferred_element_type=F32)
    down_left = jnp.dot(hidden, proj_ff[:, 128:192], preferred_element_type=F32)
    gate_right = jnp.dot(gate_grad, proj_ff[:, 0:64], preferred_element_type=F32)
    up_right = jnp.dot(up_grad, proj_ff[:, 64:128], preferred_element_type=F32)
    left_local = jnp.concatenate([in_side, down_left], axis=1)
    right_local = jnp.concatenate([gate_right, up_right], axis=1)
    tensor_place = lax.axis_index("tensor")
    left_full, right_summed = lax.psum((left_local, right_local), "tensor")
    left_mine = lax.dynamic_slice_in_dim(
        left_full.reshape(tokens_here, 3, 64), tensor_place * share, share, 2
    )
    right_all = jnp.concatenate([right_summed, right_total], axis=1).reshape(tokens_here, 3, 64)
    examples = lengths.shape[0]
    positions = lax.axis_index("seq") * tokens_here + jnp.arange(tokens_here, dtype=jnp.int32)
    ends = jnp.cumsum(lengths)
    starts = ends - lengths
    member = (
        (positions[:, None] >= starts[None, :]) & (positions[:, None] < ends[None, :])
    ).astype(F32)
    scale = lax.rsqrt(lengths.astype(F32))
    sketches = []
    for linear in range(3):
        weighted = (member[:, :, None] * left_mine[:, None, linear, :]).reshape(
            tokens_here, examples * share
        )
        sketch = lax.dot_general(
            weighted,
            right_all[:, linear, :],
            (((0,), (0,)), ((), ())),
            precision=lax.Precision.HIGHEST,
            preferred_element_type=F32,
        )
        sketches.append(sketch.reshape(examples, share * 64))
    stacked = jnp.stack(sketches, axis=1) * scale[:, None, None]
    placing = (slots[None, :] == jnp.arange(examples, dtype=jnp.int32)[:, None]).astype(F32)
    placed = jnp.dot(
        placing,
        stacked.reshape(examples, 3 * share * 64),
        precision=lax.Precision.HIGHEST,
        preferred_element_type=F32,
    )
    return lax.psum_scatter(
        placed.reshape(examples, 3, share, 64), "seq", scatter_dimension=3, tiled=True
    )


def grads_kernel(tiles, half, first, last, *refs):
    n_pairs = 1 + max(t[0] for t in tiles)
    it = iter(refs)
    take = lambda n: [next(it) for _ in range(n)]
    (scal,) = take(1)
    own, ups, downs = next(it), take(3), take(3)
    w_own, w_sib = take(2)
    pairs = [take(2) for _ in range(n_pairs)]
    gate, up, pg, pu = take(4)
    acc_in = None if first else take(2)
    if last:
        left_t, r_down, lo, hi, scale = take(5)
        keep, send = take(2)
    else:
        acc_out = take(2)
    og, wbuf, gbuf, ubuf, pbuf, acc, og_sem, sems = take(8)
    s, z, y = scal[0], scal[1], scal[2]
    n = len(tiles)

    def og_copies():
        out = [(z >= 0, own, z)]
        for k in range(1, 4):
            out.append((z >= k, ups[k - 1], z - k))
            out.append((z + k <= 3, downs[k - 1], z + k))
        return out

    for cond, ref, q in og_copies():
        @pl.when(cond)
        def _(ref=ref, q=q):
            pltpu.make_async_copy(ref, og.at[q], og_sem).start()

    def fetch(t, slot):
        for i, (pair, row, off, mine) in enumerate(tiles):
            @pl.when(t == i)
            def _(pair=pair, row=row, off=off, mine=mine):
                h = y if mine else 1 - y
                at = pl.multiple_of(h * half + off, 128)
                rows = pl.ds(at, TILE)
                here = pl.ds(row, TILE)
                a, b = pairs[pair]
                for j, src in enumerate(
                    (w_own.at[rows], w_sib.at[rows], a.at[here], b.at[here])
                ):
                    pltpu.make_async_copy(src, wbuf.at[slot, j], sems.at[slot]).start()
                pltpu.make_async_copy(gate.at[:, rows], gbuf.at[slot], sems.at[slot]).start()
                pltpu.make_async_copy(up.at[:, rows], ubuf.at[slot], sems.at[slot]).start()
                pltpu.make_async_copy(pg.at[rows], pbuf.at[slot, 0], sems.at[slot]).start()
                pltpu.make_async_copy(pu.at[rows], pbuf.at[slot, 1], sems.at[slot]).start()

    def arrive(slot):
        rows = pl.ds(0, TILE)
        for j in range(4):
            pltpu.make_async_copy(w_own.at[rows], wbuf.at[slot, j], sems.at[slot]).wait()
        pltpu.make_async_copy(gate.at[:, rows], gbuf.at[slot], sems.at[slot]).wait()
        pltpu.make_async_copy(up.at[:, rows], ubuf.at[slot], sems.at[slot]).wait()
        pltpu.make_async_copy(pg.at[rows], pbuf.at[slot, 0], sems.at[slot]).wait()
        pltpu.make_async_copy(pu.at[rows], pbuf.at[slot, 1], sems.at[slot]).wait()

    fetch(jnp.int32(0), 0)
    if first:
        acc[...] = jnp.zeros_like(acc)
    else:
        acc[0] = acc_in[0][...]
        acc[1] = acc_in[1][...]
    for q in range(4):
        pltpu.make_async_copy(own, og.at[q], og_sem).wait()

    @pl.loop(0, n)
    def _(t):
        slot = lax.rem(t, 2)
        @pl.when(t + 1 < n)
        def _():
            fetch(t + 1, 1 - slot)
        arrive(slot)
        for m in range(2):
            toks = pl.ds(m * 256, 256)
            total = None
            for j in range(4):
                part = lax.dot_general(
                    og[s ^ j, toks, :],
                    wbuf[slot, j],
                    (((1,), (1,)), ((), ())),
                    preferred_element_type=F32,
                )
                total = part if total is None else total + part
            activated, slope = silu_pair(gbuf[slot, toks, :].astype(F32))
            gate_grad = (total * ubuf[slot, toks, :].astype(F32) * slope).astype(BF16)
            up_grad = (total * activated).astype(BF16)
            acc[0, toks, :] += jnp.dot(gate_grad, pbuf[slot, 0], preferred_element_type=F32)
            acc[1, toks, :] += jnp.dot(up_grad, pbuf[slot, 1], preferred_element_type=F32)

    if not last:
        acc_out[0][...] = acc[0]
        acc_out[1][...] = acc[1]
        return
    tokens = acc.shape[1]
    where = s * tokens + lax.broadcasted_iota(jnp.int32, (tokens, 256), 0)
    weight = jnp.where((where >= lo[...]) & (where < hi[...]), scale[...], 0.0)
    for l in range(3):
        right = (r_down[...] if l == 2 else acc[l]) * weight
        m = jnp.dot(
            left_t[pl.ds(64 * l, 64), :],
            right,
            precision=lax.Precision.HIGHEST,
            preferred_element_type=F32,
        )
        even = lax.rem(s, 2) == 0
        keep[l] = jnp.where(even, m[:, :128], m[:, 128:])
        send[l] = jnp.where(even, m[:, 128:], m[:, :128])


def grads_call(tiles, half, scal, og_parts, weights, pairs, streams, acc, tail):
    tokens, depth = og_parts[0].shape
    first, last = acc is None, tail is not None
    any_spec = pl.BlockSpec(memory_space=pl.ANY)
    vmem = pl.BlockSpec(memory_space=pltpu.VMEM)
    args = [scal, *og_parts, *weights, *[a for p in pairs for a in p], *streams]
    specs = [pl.BlockSpec(memory_space=pltpu.SMEM)] + [any_spec] * (len(args) - 1)
    if not first:
        args += list(acc)
        specs += [vmem] * 2
    if last:
        args += list(tail)
        specs += [vmem] * len(tail)
        outs = [jax.ShapeDtypeStruct((3, 64, 128), F32)] * 2
    else:
        outs = [jax.ShapeDtypeStruct((tokens, 256), F32)] * 2
    flops = 2 * len(tiles) * TILE * tokens * (4 * depth + 512)
    return pl.pallas_call(
        functools.partial(grads_kernel, tiles, half, first, last),
        out_shape=outs,
        in_specs=specs,
        out_specs=[vmem] * 2,
        scratch_shapes=[
            pltpu.VMEM((4, tokens, depth), BF16),
            pltpu.VMEM((2, 4, TILE, depth), BF16),
            pltpu.VMEM((2, tokens, TILE), BF16),
            pltpu.VMEM((2, tokens, TILE), BF16),
            pltpu.VMEM((2, 2, TILE, 256), BF16),
            pltpu.VMEM((2, tokens, 256), F32),
            pltpu.SemaphoreType.DMA,
            pltpu.SemaphoreType.DMA((2,)),
        ],
        compiler_params=pltpu.CompilerParams(vmem_limit_bytes=40 * 1024 * 1024),
        cost_estimate=pl.CostEstimate(
            flops=flops,
            bytes_accessed=2 * (4 * tokens * depth + len(tiles) * TILE * (4 * depth + 2 * tokens)),
            transcendentals=len(tiles) * TILE * tokens,
        ),
    )(*args)


def local(
    layer_input, out_grad, gate_pre, up_pre, w_down, proj_in, proj_ff, proj_down, lengths, slots
):
    tokens = layer_input.shape[0]
    depth = out_grad.shape[1]
    units = w_down.shape[0]
    half = units // 2
    y, s, z = (lax.axis_index(a) for a in ("groups", "seq", "tensor"))
    scal = jnp.stack([s, z, y]).astype(jnp.int32)

    over_x = lambda a: lax.ppermute(a, "seq", [(i, i ^ 2) for i in range(4)])
    over_c = lambda a: lax.ppermute(a, "seq", [(i, i ^ 1) for i in range(4)])
    over_y = lambda a: lax.ppermute(a, "groups", [(0, 1), (1, 0)])
    over_z = lambda a, k: lax.ppermute(a, "tensor", [(i, i ^ k) for i in range(4)])

    count = len(CHUNKS)
    offs = [sum(CHUNKS[:k]) for k in range(count)]
    srcs = [
        lax.dynamic_slice_in_dim(w_down, y * half + offs[k], CHUNKS[k], 0) for k in range(count)
    ]
    r, rc, ry, yc = ([None] * count for _ in range(4))
    for k in range(DEPTH):
        r[k] = over_x(srcs[k])
    w_sib = over_c(w_down)

    ups, downs = [], []
    rise = fall = out_grad
    z_at = {1: 1, 3: 2, 5: 3}

    def z_step(k, rise, fall):
        rise = lax.ppermute(rise, "tensor", [(i, i + 1) for i in range(k - 1, 3)])
        fall = lax.ppermute(fall, "tensor", [(i + 1, i) for i in range(0, 4 - k)])
        return rise, fall

    rise, fall = z_step(1, rise, fall)

    upper = up_pre.astype(F32)
    activated, _ = silu_pair(gate_pre.astype(F32))
    hidden = (activated * upper).astype(BF16)
    in_side = jnp.dot(layer_input, proj_in, preferred_element_type=F32)
    down_left = jnp.dot(hidden, proj_ff[:, 128:192], preferred_element_type=F32)
    left_t = lax.psum(jnp.concatenate([in_side, down_left], axis=1).T, "tensor")

    column = jnp.arange(64, dtype=jnp.int32)[:, None]
    lane = jnp.arange(256, dtype=jnp.int32)[None, :]
    source = (2 * ((lane // 64) % 2) + lane // 128) * 16 + lane % 16
    spread = (column == source).astype(BF16)
    expand = lambda a: jnp.dot(a, spread, preferred_element_type=F32).astype(BF16)
    pg, pu = expand(proj_ff[:, 0:64]), expand(proj_ff[:, 64:128])
    down_rows = lax.dynamic_slice_in_dim(proj_down, z * depth, depth, 0)
    r_down = jnp.dot(out_grad, expand(down_rows), preferred_element_type=F32)
    ends = jnp.cumsum(lengths)
    pick = slots[:, None] == (lane // 16) % 4
    by_lane = lambda a: jnp.sum(jnp.where(pick, a[:, None], jnp.zeros((), a.dtype)), 0, keepdims=True)
    lo, hi = by_lane(ends - lengths), by_lane(ends)
    scale = by_lane(lax.rsqrt(lengths.astype(F32)))

    for k in range(count):
        items = {"r": r[k]}
        if k >= 2:
            items["y"] = ry[k - 2]
        if k + DEPTH < count:
            items["w"] = srcs[k + DEPTH]
        if k in z_at:
            items["z"] = (rise, fall)
        items = lax.optimization_barrier(items)
        r[k] = items["r"]
        ry[k] = over_y(r[k])
        rc[k] = over_c(r[k])
        if k >= 2:
            ry[k - 2] = items["y"]
            yc[k - 2] = over_c(ry[k - 2])
        if k + DEPTH < count:
            r[k + DEPTH] = over_x(items["w"])
        if k in z_at:
            rise, fall = items["z"]
            ups.append(rise)
            downs.append(fall)
            if z_at[k] < 3:
                rise, fall = z_step(z_at[k] + 1, rise, fall)
    for k in (count - 2, count - 1):
        yc[k] = over_c(ry[k])

    acc = None
    begin = 0
    for c, n in enumerate(CALLS):
        pairs, tiles = [], []
        for k in range(begin, begin + n):
            for mine in (True, False):
                for row in range(0, CHUNKS[k], TILE):
                    tiles.append((len(pairs), row, offs[k] + row, mine))
                pairs.append((r[k], rc[k]) if mine else (ry[k], yc[k]))
        begin += n
        last = c == len(CALLS) - 1
        acc = grads_call(
            tuple(tiles), half, scal, (out_grad, *ups, *downs), (w_down, w_sib), pairs,
            (gate_pre, up_pre, pg, pu), acc,
            (left_t, r_down, lo, hi, scale) if last else None,
        )
    keep, send = acc
    x = s // 2
    total = (keep + over_c(send)).reshape(3, 64, 2, 64)
    part = lambda a, axis, at: lax.dynamic_index_in_dim(a, at, axis, keepdims=False)
    total = part(total, 2, x) + over_x(part(total, 2, 1 - x))
    total = total.reshape(3, 2, 32, 64)
    total = part(total, 1, z // 2) + over_z(part(total, 1, 1 - z // 2), 2)
    total = total.reshape(3, 2, 16, 64)
    total = part(total, 1, z % 2) + over_z(part(total, 1, 1 - z % 2), 1)
    return total.reshape(3, 16, 4, 16).transpose(2, 0, 1, 3)


def solution(mesh):
    placed = (
        P(("groups", "seq"), "tensor"),
        P(("groups", "seq"), "tensor"),
        P(("groups", "seq"), "tensor"),
        P(("groups", "seq"), "tensor"),
        P("tensor", "seq"),
        P("tensor", None),
        P("tensor", None),
        P(),
        P("groups"),
        P("groups"),
    )
    small = (mesh.shape["groups"], mesh.shape["seq"], mesh.shape["tensor"]) == (2, 4, 4)
    return jax.shard_map(
        local if small else general,
        mesh=mesh,
        in_specs=placed,
        out_specs=P("groups", None, "tensor", "seq"),
        check_vma=False,
    )
```

time: 379 us -> 257 us (0.68)
  waiting for transfers between devices: 314 us -> 110 us
  Pallas kernels: 0 us -> 49.4 us
  starting transfers between devices: 0.33 us -> 35.7 us
  matrix products: 42.2 us -> 13.2 us
  local copies, waits for them, and re-layouts: 6.54 us -> 32.8 us
    all_gather x2 -> x0, waiting for transfers between devices: 256 us -> none  [the longest x1 178 us: local(): whole_down = lax.all_gather(w_down, 'seq', axis=1, tiled=True)]
    ppermute x0 -> x39, waiting for transfers between devices: none -> 110 us  [the longest x8 56.5 us: local(): over_x = lambda a: lax.ppermute(a, 'seq', [(i, i ^ 2) for i in range(4)])]
    pallas_call x0 -> x3, Pallas kernels: none -> 49.4 us  [grads_call(): pl.pallas_call(functools.partial(grads_kernel, tiles, half, first, last),...]
    psum x1, waiting for transfers between devices: 37 us -> 0.01 us  [local(): left_t = lax.psum(jnp.concatenate([in_side, down_left], axis=1).T, 'tensor')]
    ppermute x0 -> x39, starting transfers between devices: none -> 35.7 us  [the longest x8 12.5 us: local(): over_x = lambda a: lax.ppermute(a, 'seq', [(i, i ^ 2) for i in range(4)])]
    dot_general x10 -> x5, matrix products: 42.2 us -> 13.2 us  [the longest x2 6.08 us: local(): jnp.dot(a, spread, preferred_element_type=F32).astype(BF16)]
    unnamed x19 -> x88, local copies, waits for them, and re-layouts: 4.34 us -> 28.3 us
    unnamed x5 -> x1, waiting for transfers between devices: 20.4 us -> 0.02 us
  transfers between devices with their start and end apart: 4 -> 40, of which waited for: 4 -> 18; matrix products, arithmetic and copies ran while one was open for 3% -> 7% of each run, Pallas kernels for 0% -> 15%
where the time goes in v1:
time: 257 us; the launch traced here: 256 us
  waiting for transfers between devices  110 us (43%)
  Pallas kernels  49.4 us (19%)
  starting transfers between devices  35.7 us (14%)
  local copies, waits for them, and re-layouts  32.8 us (13%)
  between operations  13.8 us (5%)
  matrix products  13.2 us (5%)
    ppermute x8, waiting for transfers between devices, local(): over_x = lambda a: lax.ppermute(a, 'seq', [(i, i ^ 2) for i in range(4)])  56.5 us
    pallas_call x3, Pallas kernels, grads_call(): pl.pallas_call(functools.partial(grads_kernel, tiles, half, first, last),...  49.4 us
    unnamed x88, local copies, waits for them, and re-layouts  28.3 us
    ppermute x7, waiting for transfers between devices, local(): over_y = lambda a: lax.ppermute(a, 'groups', [(0, 1), (1, 0)])  23.5 us
    ppermute x3, waiting for transfers between devices, z_step(): fall = lax.ppermute(fall, 'tensor', [(i + 1, i) for i in range(0, 4 - k)])  20.2 us
    ppermute x8, starting transfers between devices, local(): over_x = lambda a: lax.ppermute(a, 'seq', [(i, i ^ 2) for i in range(4)])  12.5 us
    ppermute x7, starting transfers between devices, local(): over_y = lambda a: lax.ppermute(a, 'groups', [(0, 1), (1, 0)])  9.53 us
    ppermute x2, waiting for transfers between devices, local(): lax.ppermute(a, 'tensor', [(i, i ^ k) for i in range(4)])  8.76 us
  transfers between devices with their start and end apart: 40, of which 18 were waited for; matrix products, arithmetic and copies ran while one was open for 7% of the time, Pallas kernels for 15%

profile of v1, /device:TPU:0, one launch (start us, length us, event | category | flops | bytes accessed | tf_op | source)
XLA Modules:
  0.0 256.3 jit_solution(8002252903289091365)
XLA Ops:
  7.0 3.4 %constant_dynamic-slice_fusion.2 = (bf16[256,1024]{1,0:T(8,128)(2,1)S(1)}, bf16[256,1024]{1,0:T(8,128)(2,1)S(1)}, bf16[256,1024]{1,0:T(8,128)(2,1)}, bf16[256,10...) fusion(bf16[3584,1024]{1,0:T(8,128)(2,1)} %refs_8_.5, ...), kind=kLoop, calls=%fused_computation.43 | loop fusion | bytes 7340060 | tf_op jit(solution)/shard_map/dynamic_slice | solution.py:255
  12.9 4.0 %collective-permute-start.1 = (bf16[512,1024]{1,0:T(8,128)(2,1)S(1)}, bf16[512,1024]{1,0:T(8,128)(2,1)S(1)}, u32[]{:S(2)}, u32[]{:S(2)}) collective-permute-start(bf16[512,1024]{1,0:T(8,128)(2,1)S(1)} %copy-done.2), channel_id=1, source_target_pairs={{0,1},{1,2},{2,3},{4,5},{5,6},{6,7},{8,9},{9,10},{10,11},{12,13},{... | collective-permute-start | bytes 3145736 | tf_op jit(solution)/shard_map/ppermute | solution.py:267
  18.3 7.4 %collective-permute-done.3.refs_10_ = bf16[256,1024]{1,0:T(8,128)(2,1)S(1)} collective-permute-done((bf16[256,1024]{1,0:T(8,128)(2,1)S(1)}, bf16[256,1024]{1,0:T(8,128)(2,1)S(1)}, u32[]{:S(2)}, u32[]{:S(2)}) %collective-permute-start.3) | collective-permute-done | bytes 524320 | tf_op jit(solution)/shard_map/ppermute | solution.py:247
  27.6 9.3 %collective-permute-done.8.refs_18_ = bf16[256,1024]{1,0:T(8,128)(2,1)S(1)} collective-permute-done((bf16[256,1024]{1,0:T(8,128)(2,1)S(1)}, bf16[256,1024]{1,0:T(8,128)(2,1)S(1)}, u32[]{:S(2)}, u32[]{:S(2)}) %collective-permute-start.8) | collective-permute-done | bytes 524320 | tf_op jit(solution)/shard_map/ppermute | solution.py:247
  38.9 9.2 %collective-permute-done.refs_14_ = bf16[256,1024]{1,0:T(8,128)(2,1)} collective-permute-done((bf16[256,1024]{1,0:T(8,128)(2,1)S(1)}, bf16[256,1024]{1,0:T(8,128)(2,1)}, u32[]{:S(2)}, u32[]{:S(2)}) %collective-permute-start) | collective-permute-done | bytes 524320 | tf_op jit(solution)/shard_map/ppermute | solution.py:247
  54.4 8.6 %collective-permute-done.4.refs_22_ = bf16[256,1024]{1,0:T(8,128)(2,1)} collective-permute-done((bf16[256,1024]{1,0:T(8,128)(2,1)S(1)}, bf16[256,1024]{1,0:T(8,128)(2,1)}, u32[]{:S(2)}, u32[]{:S(2)}) %collective-permute-start.4) | collective-permute-done | bytes 524320 | tf_op jit(solution)/shard_map/ppermute | solution.py:247
  68.6 4.5 %collective-permute-done.16.refs_26_ = bf16[256,1024]{1,0:T(8,128)(2,1)} collective-permute-done((bf16[256,1024]{1,0:T(8,128)(2,1)S(1)}, bf16[256,1024]{1,0:T(8,128)(2,1)}, u32[]{:S(2)}, u32[]{:S(2)}) %collective-permute-start.16) | collective-permute-done | bytes 524320 | tf_op jit(solution)/shard_map/ppermute | solution.py:247
  74.7 4.8 %collective-permute-done.5.refs_16_ = bf16[256,1024]{1,0:T(8,128)(2,1)S(1)} collective-permute-done((bf16[256,1024]{1,0:T(8,128)(2,1)}, bf16[256,1024]{1,0:T(8,128)(2,1)S(1)}, u32[]{:S(2)}, u32[]{:S(2)}) %collective-permute-start.5) | collective-permute-done | bytes 524320 | tf_op jit(solution)/shard_map/ppermute | solution.py:249
  80.3 5.7 %collective-permute-done.10.refs_10_ = bf16[256,1024]{1,0:T(8,128)(2,1)S(1)} collective-permute-done((bf16[256,1024]{1,0:T(8,128)(2,1)S(1)}, bf16[256,1024]{1,0:T(8,128)(2,1)S(1)}, u32[]{:S(2)}, u32[]{:S(2)}) %collective-permute-start.10) | collective-permute-done | bytes 524320 | tf_op jit(solution)/shard_map/ppermute | solution.py:247
  87.4 5.3 %collective-permute-done.7.refs_6_ = bf16[512,1024]{1,0:T(8,128)(2,1)} collective-permute-done((bf16[512,1024]{1,0:T(8,128)(2,1)S(1)}, bf16[512,1024]{1,0:T(8,128)(2,1)}, u32[]{:S(2)}, u32[]{:S(2)}) %collective-permute-start.7) | collective-permute-done | bytes 1048608 | tf_op jit(solution)/shard_map/ppermute | solution.py:268
  94.2 4.1 %fusion.7 = f32[512,64]{0,1:T(8,128)S(1)} fusion(bf16[512,3584]{1,0:T(8,128)(2,1)} %refs_15_.3, bf16[512,3584]{1,0:T(8,128)(2,1)S(1)} %copy-done.40, bf16[3584,192]{0,1:T(8,128)(2,1)} %param.16), kind=kOutput, calls=%fused_computation.11 | convolution fusion | flops 249561088 | bytes 7929856 | tf_op jit(solution)/shard_map/dot_general | solution.py:277
  106.5 8.4 %collective-permute-done.15.refs_10_ = bf16[256,1024]{1,0:T(8,128)(2,1)} collective-permute-done((bf16[256,1024]{1,0:T(8,128)(2,1)}, bf16[256,1024]{1,0:T(8,128)(2,1)}, u32[]{:S(2)}, u32[]{:S(2)}) %collective-permute-start.15) | collective-permute-done | bytes 524320 | tf_op jit(solution)/shard_map/ppermute | solution.py:247
  116.5 14.9 %collective-permute-done.13.refs_7_ = bf16[512,1024]{1,0:T(8,128)(2,1)} collective-permute-done((bf16[512,1024]{1,0:T(8,128)(2,1)}, bf16[512,1024]{1,0:T(8,128)(2,1)}, u32[]{:S(2)}, u32[]{:S(2)}) %collective-permute-start.13) | collective-permute-done | bytes 1048608 | tf_op jit(solution)/shard_map/ppermute | solution.py:268
  131.7 2.9 %fusion.5.refs_32_.refs_16_ = bf16[3584,256]{1,0:T(8,128)(2,1)} fusion(bf16[3584,192]{0,1:T(8,128)(2,1)} %param.16, s32[256]{0:T(256)S(1)} %fusion.27), kind=kOutput, calls=%fused_computation.9 | convolution fusion | flops 118374400 | bytes 2294784 | tf_op jit(solution)/shard_map/dot_general | solution.py:284
  137.3 2.6 fusion.10.refs_21_
  139.9 3.1 %fusion.6.refs_33_.refs_17_ = bf16[3584,256]{1,0:T(8,128)(2,1)} fusion(bf16[3584,192]{0,1:T(8,128)(2,1)} %param.16, s32[256]{0:T(256)S(1)} %fusion.27), kind=kOutput, calls=%fused_computation.10 | convolution fusion | flops 118374400 | bytes 2294784 | tf_op jit(solution)/shard_map/dot_general | solution.py:284
  143.2 7.1 %collective-permute-done.20.refs_12_ = bf16[256,1024]{1,0:T(8,128)(2,1)} collective-permute-done((bf16[256,1024]{1,0:T(8,128)(2,1)}, bf16[256,1024]{1,0:T(8,128)(2,1)}, u32[]{:S(2)}, u32[]{:S(2)}) %collective-permute-start.20) | collective-permute-done | bytes 524320 | tf_op jit(solution)/shard_map/ppermute | solution.py:249
  150.8 9.8 %collective-permute-done.23.refs_12_ = bf16[256,1024]{1,0:T(8,128)(2,1)} collective-permute-done((bf16[256,1024]{1,0:T(8,128)(2,1)}, bf16[256,1024]{1,0:T(8,128)(2,1)}, u32[]{:S(2)}, u32[]{:S(2)}) %collective-permute-start.23) | collective-permute-done | bytes 524320 | tf_op jit(solution)/shard_map/ppermute | solution.py:249
  172.5 31.1 %shard_map.100 = (f32[512,256]{1,0:T(8,128)S(1)}, f32[512,256]{1,0:T(8,128)S(1)}) custom-call(s32[3]{0:T(128)S(1)} %pad_add_fusion.refs_0_, bf16[512,1024]{1,0:T(8,128)(2,1)S(1)} %copy-done.3, bf16[512,1024]{1,0:T(8,128)(2,1)S(1)} %copy-done.6, bf16[512,1024]{1,0:T(8,128)(2,1)} %copy-done.11, bf16[512,1024]{1,0:T(8,128)(2,1)} %collective-permute-done.12.refs_4_, ...), custom_call_target="tpu_custom_call" | custom-call | flops 12079595520 | bytes 30408704 | tf_op jit(solution)/shard_map/pallas_call | solution.py:213
  203.7 8.3 %shard_map.101 = (f32[512,256]{1,0:T(8,128)S(1)}, f32[512,256]{1,0:T(8,128)S(1)}) custom-call(s32[3]{0:T(128)S(1)} %pad_add_fusion.refs_0_, bf16[512,1024]{1,0:T(8,128)(2,1)S(1)} %copy-done.3, bf16[512,1024]{1,0:T(8,128)(2,1)S(1)} %copy-done.6, bf16[512,1024]{1,0:T(8,128)(2,1)S(1)} %copy-done.12, bf16[512,1024]{1,0:T(8,128)(2,1)} %collective-permute-done.12.refs_4_, ...), custom_call_target="tpu_custom_call" | custom-call | flops 2415919104 | bytes 9437184 | tf_op jit(solution)/shard_map/pallas_call | solution.py:213
  222.7 10.0 %shard_map.102 = (f32[3,64,128]{2,1,0:T(8,128)S(1)}, f32[3,64,128]{2,1,0:T(8,128)S(1)}) custom-call(s32[3]{0:T(128)S(1)} %pad_add_fusion.refs_0_, bf16[512,1024]{1,0:T(8,128)(2,1)S(1)} %copy-done.4, bf16[512,1024]{1,0:T(8,128)(2,1)S(1)} %copy-done.7, bf16[512,1024]{1,0:T(8,128)(2,1)S(1)} %copy-done.13, bf16[512,1024]{1,0:T(8,128)(2,1)} %collective-permute-done.12.refs_4_, ...), custom_call_target="tpu_custom_call" | custom-call | flops 2415919104 | bytes 9437184 | tf_op jit(solution)/shard_map/pallas_call | solution.py:213
  236.1 3.5 %collective-permute-done.36 = f32[3,64,64]{2,1,0:T(8,128)S(1)} collective-permute-done((f32[3,64,64]{2,1,0:T(8,128)S(1)}, f32[3,64,64]{2,1,0:T(8,128)S(1)}, u32[]{:S(2)}, u32[]{:S(2)}) %collective-permute-start.36) | collective-permute-done | bytes 49184 | tf_op jit(solution)/shard_map/ppermute | solution.py:247
  239.8 5.0 %collective-permute-done.37 = f32[3,32,64]{2,1,0:T(8,128)S(1)} collective-permute-done((f32[3,32,64]{2,1,0:T(8,128)S(1)}, f32[3,32,64]{2,1,0:T(8,128)S(1)}, u32[]{:S(2)}, u32[]{:S(2)}) %collective-permute-start.37) | collective-permute-done | bytes 24608 | tf_op jit(solution)/shard_map/ppermute | solution.py:250
  244.9 3.8 %collective-permute-done.38 = f32[3,16,64]{2,1,0:T(8,128)S(1)} collective-permute-done((f32[3,16,64]{2,1,0:T(8,128)S(1)}, f32[3,16,64]{2,1,0:T(8,128)S(1)}, u32[]{:S(2)}, u32[]{:S(2)}) %collective-permute-start.38) | collective-permute-done | bytes 12320 | tf_op jit(solution)/shard_map/ppermute | solution.py:250
  (173 shorter events, 65.6 us)
Async XLA Ops:
  6.5 207.1 %all-reduce.2.cloned.1.call-start = ((), (), s32[]{:S(2)}) async-start(), calls=%async_computation | async-start | bytes 786432 | tf_op jit(solution)/shard_map/psum | solution.py:278
  6.5 154.1 %collective-permute-start.14 = (bf16[3584,1024]{1,0:T(8,128)(2,1)}, bf16[3584,1024]{1,0:T(8,128)(2,1)}, u32[]{:S(2)}, u32[]{:S(2)}) collective-permute-start(bf16[3584,1024]{1,0:T(8,128)(2,1)} %refs_8_.5), channel_id=1, source_target_pairs={{0,4},{4,0},{8,12},{12,8},{1,5},{5,1},{9,13},{13,9},{2,6},{6,2},{1... | collective-permute-start | bytes 22020104 | tf_op jit(solution)/shard_map/ppermute | solution.py:248
  10.4 15.3 %collective-permute-start.3 = (bf16[256,1024]{1,0:T(8,128)(2,1)S(1)}, bf16[256,1024]{1,0:T(8,128)(2,1)S(1)}, u32[]{:S(2)}, u32[]{:S(2)}) collective-permute-start(bf16[256,1024]{1,0:T(8,128)(2,1)S(1)} %get-tuple-element.67), channel_id=1, source_target_pairs={{0,8},{4,12},{8,0},{12,4},{1,9},{5,13},{9,1},{13,5},{2,10},{6,14},... | collective-permute-start | bytes 1572872 | tf_op jit(solution)/shard_map/ppermute | solution.py:247
  12.9 24.0 %collective-permute-start.8 = (bf16[256,1024]{1,0:T(8,128)(2,1)S(1)}, bf16[256,1024]{1,0:T(8,128)(2,1)S(1)}, u32[]{:S(2)}, u32[]{:S(2)}) collective-permute-start(bf16[256,1024]{1,0:T(8,128)(2,1)S(1)} %get-tuple-element.64), channel_id=1, source_target_pairs={{0,8},{4,12},{8,0},{12,4},{1,9},{5,13},{9,1},{13,5},{2,10},{6,14},... | collective-permute-start | bytes 1572872 | tf_op jit(solution)/shard_map/ppermute | solution.py:247
  12.9 38.3 %collective-permute-start.1 = (bf16[512,1024]{1,0:T(8,128)(2,1)S(1)}, bf16[512,1024]{1,0:T(8,128)(2,1)S(1)}, u32[]{:S(2)}, u32[]{:S(2)}) collective-permute-start(bf16[512,1024]{1,0:T(8,128)(2,1)S(1)} %copy-done.2), channel_id=1, source_target_pairs={{0,1},{1,2},{2,3},{4,5},{5,6},{6,7},{8,9},{9,10},{10,11},{12,13},{... | collective-permute-start | bytes 3145736 | tf_op jit(solution)/shard_map/ppermute | solution.py:267
  17.0 35.8 %collective-permute-start.2 = (bf16[512,1024]{1,0:T(8,128)(2,1)S(1)}, bf16[512,1024]{1,0:T(8,128)(2,1)S(1)}, u32[]{:S(2)}, u32[]{:S(2)}) collective-permute-start(bf16[512,1024]{1,0:T(8,128)(2,1)S(1)} %copy-done.2), channel_id=1, source_target_pairs={{1,0},{2,1},{3,2},{5,4},{6,5},{7,6},{9,8},{10,9},{11,10},{13,12},{... | collective-permute-start | bytes 3145736 | tf_op jit(solution)/shard_map/ppermute | solution.py:268
  25.7 22.4 %collective-permute-start = (bf16[256,1024]{1,0:T(8,128)(2,1)S(1)}, bf16[256,1024]{1,0:T(8,128)(2,1)}, u32[]{:S(2)}, u32[]{:S(2)}) collective-permute-start(bf16[256,1024]{1,0:T(8,128)(2,1)S(1)} %get-tuple-element.69), channel_id=1, source_target_pairs={{0,8},{4,12},{8,0},{12,4},{1,9},{5,13},{9,1},{13,5},{2,10},{6,14},... | collective-permute-start | bytes 1572872 | tf_op jit(solution)/shard_map/ppermute | solution.py:247
  51.2 15.5 %collective-permute-start.17 = (bf16[256,1024]{1,0:T(8,128)(2,1)S(1)}, bf16[256,1024]{1,0:T(8,128)(2,1)}, u32[]{:S(2)}, u32[]{:S(2)}) collective-permute-start(bf16[256,1024]{1,0:T(8,128)(2,1)S(1)} %collective-permute-done.8.refs_18_), channel_id=1, source_target_pairs={{0,16},{16,0},{1,17},{17,1},{2,18},{18,2},{3,19},{19,3},{4,20},{20... | collective-permute-start | bytes 1572872 | tf_op jit(solution)/shard_map/ppermute | solution.py:249
  52.8 20.3 %collective-permute-start.16 = (bf16[256,1024]{1,0:T(8,128)(2,1)S(1)}, bf16[256,1024]{1,0:T(8,128)(2,1)}, u32[]{:S(2)}, u32[]{:S(2)}) collective-permute-start(bf16[256,1024]{1,0:T(8,128)(2,1)S(1)} %get-tuple-element.45), channel_id=1, source_target_pairs={{0,8},{4,12},{8,0},{12,4},{1,9},{5,13},{9,1},{13,5},{2,10},{6,14},... | collective-permute-start | bytes 1572872 | tf_op jit(solution)/shard_map/ppermute | solution.py:247
  63.0 23.0 %collective-permute-start.6 = (bf16[512,1024]{1,0:T(8,128)(2,1)S(1)}, bf16[512,1024]{1,0:T(8,128)(2,1)S(1)}, u32[]{:S(2)}, u32[]{:S(2)}) collective-permute-start(bf16[512,1024]{1,0:T(8,128)(2,1)S(1)} %collective-permute-done.1.refs_2_), channel_id=1, source_target_pairs={{1,2},{2,3},{5,6},{6,7},{9,10},{10,11},{13,14},{14,15},{17,18},{18... | collective-permute-start | bytes 3145736 | tf_op jit(solution)/shard_map/ppermute | solution.py:267
  65.4 27.2 %collective-permute-start.7 = (bf16[512,1024]{1,0:T(8,128)(2,1)S(1)}, bf16[512,1024]{1,0:T(8,128)(2,1)}, u32[]{:S(2)}, u32[]{:S(2)}) collective-permute-start(bf16[512,1024]{1,0:T(8,128)(2,1)S(1)} %collective-permute-done.2.refs_5_), channel_id=1, source_target_pairs={{1,0},{2,1},{5,4},{6,5},{9,8},{10,9},{13,12},{14,13},{17,16},{18,1... | collective-permute-start | bytes 3145736 | tf_op jit(solution)/shard_map/ppermute | solution.py:268
  79.4 21.3 %collective-permute-start.29 = (bf16[256,1024]{1,0:T(8,128)(2,1)S(1)}, bf16[256,1024]{1,0:T(8,128)(2,1)S(1)}, u32[]{:S(2)}, u32[]{:S(2)}) collective-permute-start(bf16[256,1024]{1,0:T(8,128)(2,1)S(1)} %collective-permute-done.8.refs_18_), channel_id=1, source_target_pairs={{0,4},{4,0},{8,12},{12,8},{1,5},{5,1},{9,13},{13,9},{2,6},{6,2},{1... | collective-permute-start | bytes 1572872 | tf_op jit(solution)/shard_map/ppermute | solution.py:248
  86.0 18.4 %collective-permute-start.27 = (bf16[256,1024]{1,0:T(8,128)(2,1)}, bf16[256,1024]{1,0:T(8,128)(2,1)}, u32[]{:S(2)}, u32[]{:S(2)}) collective-permute-start(bf16[256,1024]{1,0:T(8,128)(2,1)} %collective-permute-done.refs_14_), channel_id=1, source_target_pairs={{0,4},{4,0},{8,12},{12,8},{1,5},{5,1},{9,13},{13,9},{2,6},{6,2},{1... | collective-permute-start | bytes 1572872 | tf_op jit(solution)/shard_map/ppermute | solution.py:248
  99.1 16.9 %collective-permute-start.12 = (bf16[512,1024]{1,0:T(8,128)(2,1)S(1)}, bf16[512,1024]{1,0:T(8,128)(2,1)}, u32[]{:S(2)}, u32[]{:S(2)}) collective-permute-start(bf16[512,1024]{1,0:T(8,128)(2,1)S(1)} %collective-permute-done.6.refs_3_), channel_id=1, source_target_pairs={{2,3},{6,7},{10,11},{14,15},{18,19},{22,23},{26,27},{30,31}} | collective-permute-start | bytes 3145736 | tf_op jit(solution)/shard_map/ppermute | solution.py:267
  101.6 29.9 %collective-permute-start.13 = (bf16[512,1024]{1,0:T(8,128)(2,1)}, bf16[512,1024]{1,0:T(8,128)(2,1)}, u32[]{:S(2)}, u32[]{:S(2)}) collective-permute-start(bf16[512,1024]{1,0:T(8,128)(2,1)} %collective-permute-done.7.refs_6_), channel_id=1, source_target_pairs={{1,0},{5,4},{9,8},{13,12},{17,16},{21,20},{25,24},{29,28}} | collective-permute-start | bytes 3145736 | tf_op jit(solution)/shard_map/ppermute | solution.py:268
  114.9 20.3 %collective-permute-start.33 = (bf16[256,1024]{1,0:T(8,128)(2,1)}, bf16[256,1024]{1,0:T(8,128)(2,1)}, u32[]{:S(2)}, u32[]{:S(2)}) collective-permute-start(bf16[256,1024]{1,0:T(8,128)(2,1)} %collective-permute-done.16.refs_26_), channel_id=1, source_target_pairs={{0,4},{4,0},{8,12},{12,8},{1,5},{5,1},{9,13},{13,9},{2,6},{6,2},{1... | collective-permute-start | bytes 1572872 | tf_op jit(solution)/shard_map/ppermute | solution.py:248
  116.0 18.7 %collective-permute-start.30 = (bf16[256,1024]{1,0:T(8,128)(2,1)}, bf16[256,1024]{1,0:T(8,128)(2,1)}, u32[]{:S(2)}, u32[]{:S(2)}) collective-permute-start(bf16[256,1024]{1,0:T(8,128)(2,1)} %collective-permute-done.17.refs_20_), channel_id=1, source_target_pairs={{0,4},{4,0},{8,12},{12,8},{1,5},{5,1},{9,13},{13,9},{2,6},{6,2},{1... | collective-permute-start | bytes 1572872 | tf_op jit(solution)/shard_map/ppermute | solution.py:248
  116.0 19.7 %collective-permute-start.31 = (bf16[256,1024]{1,0:T(8,128)(2,1)}, bf16[256,1024]{1,0:T(8,128)(2,1)S(1)}, u32[]{:S(2)}, u32[]{:S(2)}) collective-permute-start(bf16[256,1024]{1,0:T(8,128)(2,1)} %collective-permute-done.4.refs_22_), channel_id=1, source_target_pairs={{0,4},{4,0},{8,12},{12,8},{1,5},{5,1},{9,13},{13,9},{2,6},{6,2},{1... | collective-permute-start | bytes 1572872 | tf_op jit(solution)/shard_map/ppermute | solution.py:248
  135.2 15.1 %collective-permute-start.20 = (bf16[256,1024]{1,0:T(8,128)(2,1)}, bf16[256,1024]{1,0:T(8,128)(2,1)}, u32[]{:S(2)}, u32[]{:S(2)}) collective-permute-start(bf16[256,1024]{1,0:T(8,128)(2,1)} %collective-permute-done.15.refs_10_), channel_id=1, source_target_pairs={{0,16},{16,0},{1,17},{17,1},{2,18},{18,2},{3,19},{19,3},{4,20},{20... | collective-permute-start | bytes 1572872 | tf_op jit(solution)/shard_map/ppermute | solution.py:249
  135.7 24.9 %collective-permute-start.23 = (bf16[256,1024]{1,0:T(8,128)(2,1)}, bf16[256,1024]{1,0:T(8,128)(2,1)}, u32[]{:S(2)}, u32[]{:S(2)}) collective-permute-start(bf16[256,1024]{1,0:T(8,128)(2,1)} %copy-done.14), channel_id=1, source_target_pairs={{0,16},{16,0},{1,17},{17,1},{2,18},{18,2},{3,19},{19,3},{4,20},{20... | collective-permute-start | bytes 1572872 | tf_op jit(solution)/shard_map/ppermute | solution.py:249
  143.0 70.6 %collective-permute-start.19 = (bf16[256,1024]{1,0:T(8,128)(2,1)}, bf16[256,1024]{1,0:T(8,128)(2,1)}, u32[]{:S(2)}, u32[]{:S(2)}) collective-permute-start(bf16[256,1024]{1,0:T(8,128)(2,1)} %collective-permute-done.15.refs_10_), channel_id=1, source_target_pairs={{0,4},{4,0},{8,12},{12,8},{1,5},{5,1},{9,13},{13,9},{2,6},{6,2},{1... | collective-permute-start | bytes 1572872 | tf_op jit(solution)/shard_map/ppermute | solution.py:248
  150.3 53.3 %collective-permute-start.22 = (bf16[256,1024]{1,0:T(8,128)(2,1)S(1)}, bf16[256,1024]{1,0:T(8,128)(2,1)S(1)}, u32[]{:S(2)}, u32[]{:S(2)}) collective-permute-start(bf16[256,1024]{1,0:T(8,128)(2,1)S(1)} %copy-done.15), channel_id=1, source_target_pairs={{0,4},{4,0},{8,12},{12,8},{1,5},{5,1},{9,13},{13,9},{2,6},{6,2},{1... | collective-permute-start | bytes 1572872 | tf_op jit(solution)/shard_map/ppermute | solution.py:248
  150.3 63.3 %collective-permute-start.21 = (bf16[256,1024]{1,0:T(8,128)(2,1)}, bf16[256,1024]{1,0:T(8,128)(2,1)}, u32[]{:S(2)}, u32[]{:S(2)}) collective-permute-start(bf16[256,1024]{1,0:T(8,128)(2,1)} %collective-permute-done.20.refs_12_), channel_id=1, source_target_pairs={{0,4},{4,0},{8,12},{12,8},{1,5},{5,1},{9,13},{13,9},{2,6},{6,2},{1... | collective-permute-start | bytes 1572872 | tf_op jit(solution)/shard_map/ppermute | solution.py:248
  160.6 43.0 %collective-permute-start.24 = (bf16[256,1024]{1,0:T(8,128)(2,1)}, bf16[256,1024]{1,0:T(8,128)(2,1)S(1)}, u32[]{:S(2)}, u32[]{:S(2)}) collective-permute-start(bf16[256,1024]{1,0:T(8,128)(2,1)} %collective-permute-done.23.refs_12_), channel_id=1, source_target_pairs={{0,4},{4,0},{8,12},{12,8},{1,5},{5,1},{9,13},{13,9},{2,6},{6,2},{1... | collective-permute-start | bytes 1572872 | tf_op jit(solution)/shard_map/ppermute | solution.py:248
  (60 other events, 862.5 us)
Sparse Core Ops, SparseCore 0:
  104.3 38.3 all-reduce.1

commit v2 on v1

v2 whole, which is shorter than its diff:
```python
import functools
import jax
import jax.numpy as jnp
from jax import lax
from jax.experimental import pallas as pl
from jax.experimental.pallas import tpu as pltpu
from jax.sharding import PartitionSpec as P

F32 = jnp.float32
BF16 = jnp.bfloat16
TILE = 256
CHUNKS = (256, 256, 256, 256, 256, 256, 256)


def silu_pair(gates):
    sigma = jax.nn.sigmoid(gates)
    return (gates * sigma, sigma * (1.0 + gates * (1.0 - sigma)))


def general(
    layer_input, out_grad, gate_pre, up_pre, w_down, proj_in, proj_ff, proj_down, lengths, slots
):
    tokens_here = layer_input.shape[0]
    tensor_count = lax.axis_size("tensor")
    share = 64 // tensor_count
    whole_down = lax.all_gather(w_down, "seq", axis=1, tiled=True)
    piece = lax.all_gather(out_grad, "tensor", axis=1, tiled=True)
    grad_total = lax.dot_general(
        piece, whole_down, (((1,), (1,)), ((), ())), preferred_element_type=F32
    )
    right_total = jnp.dot(piece, proj_down, preferred_element_type=F32)
    upper_value = up_pre.astype(F32)
    activated, slope = silu_pair(gate_pre.astype(F32))
    hidden = (activated * upper_value).astype(BF16)
    gate_grad = (grad_total * upper_value * slope).astype(BF16)
    up_grad = (grad_total * activated).astype(BF16)
    in_side = jnp.dot(layer_input, proj_in, preferred_element_type=F32)
    down_left = jnp.dot(hidden, proj_ff[:, 128:192], preferred_element_type=F32)
    gate_right = jnp.dot(gate_grad, proj_ff[:, 0:64], preferred_element_type=F32)
    up_right = jnp.dot(up_grad, proj_ff[:, 64:128], preferred_element_type=F32)
    left_local = jnp.concatenate([in_side, down_left], axis=1)
    right_local = jnp.concatenate([gate_right, up_right], axis=1)
    tensor_place = lax.axis_index("tensor")
    left_full, right_summed = lax.psum((left_local, right_local), "tensor")
    left_mine = lax.dynamic_slice_in_dim(
        left_full.reshape(tokens_here, 3, 64), tensor_place * share, share, 2
    )
    right_all = jnp.concatenate([right_summed, right_total], axis=1).reshape(tokens_here, 3, 64)
    examples = lengths.shape[0]
    positions = lax.axis_index("seq") * tokens_here + jnp.arange(tokens_here, dtype=jnp.int32)
    ends = jnp.cumsum(lengths)
    starts = ends - lengths
    member = (
        (positions[:, None] >= starts[None, :]) & (positions[:, None] < ends[None, :])
    ).astype(F32)
    scale = lax.rsqrt(lengths.astype(F32))
    sketches = []
    for linear in range(3):
        weighted = (member[:, :, None] * left_mine[:, None, linear, :]).reshape(
            tokens_here, examples * share
        )
        sketch = lax.dot_general(
            weighted,
            right_all[:, linear, :],
            (((0,), (0,)), ((), ())),
            precision=lax.Precision.HIGHEST,
            preferred_element_type=F32,
        )
        sketches.append(sketch.reshape(examples, share * 64))
    stacked = jnp.stack(sketches, axis=1) * scale[:, None, None]
    placing = (slots[None, :] == jnp.arange(examples, dtype=jnp.int32)[:, None]).astype(F32)
    placed = jnp.dot(
        placing,
        stacked.reshape(examples, 3 * share * 64),
        precision=lax.Precision.HIGHEST,
        preferred_element_type=F32,
    )
    return lax.psum_scatter(
        placed.reshape(examples, 3, share, 64), "seq", scatter_dimension=3, tiled=True
    )


def move_kernel(moves, n_in, *refs):
    scal, ins, refs = refs[0], refs[1 : 1 + n_in], refs[1 + n_in :]
    outs, (buf, sem) = refs[:-2], refs[-2:]
    y, at, steps = scal[2], 0, []
    for i, (src, lead, row, dst, to, rows) in enumerate(moves):
        a = ins[src].at[y, pl.ds(row, rows)] if lead else ins[src].at[pl.ds(row, rows)]
        mid = buf.at[pl.ds(at, rows)]
        steps.append(
            (
                pltpu.make_async_copy(a, mid, sem.at[0, i]),
                pltpu.make_async_copy(mid, outs[dst].at[pl.ds(to, rows)], sem.at[1, i]),
            )
        )
        at += rows
    for a, _ in steps:
        a.start()
    for a, b in steps:
        a.wait()
        b.start()
    for _, b in steps:
        b.wait()


def move(scal, ins, moves, out_rows):
    width, kind = ins[0].shape[-1], ins[0].dtype
    hbm = pl.BlockSpec(memory_space=pltpu.HBM)
    total = sum(m[-1] for m in moves)
    return pl.pallas_call(
        functools.partial(move_kernel, tuple(moves), len(ins)),
        out_shape=[jax.ShapeDtypeStruct((rows, width), kind) for rows in out_rows],
        in_specs=[pl.BlockSpec(memory_space=pltpu.SMEM)] + [hbm] * len(ins),
        out_specs=[hbm] * len(out_rows),
        scratch_shapes=[
            pltpu.VMEM((total, width), kind),
            pltpu.SemaphoreType.DMA((2, len(moves))),
        ],
        compiler_params=pltpu.CompilerParams(vmem_limit_bytes=60 * 1024 * 1024),
        cost_estimate=pl.CostEstimate(
            flops=0, bytes_accessed=4 * total * width, transcendentals=0
        ),
    )(scal, *ins)


def join(scal, pieces):
    moves, at = [], 0
    for i, piece in enumerate(pieces):
        moves.append((i, False, 0, 0, at, piece.shape[0]))
        at += piece.shape[0]
    return move(scal, pieces, moves, [at])[0]


def grads_kernel(tiles, half, first, last, *refs):
    n_pairs = 1 + max(t[0] for t in tiles)
    it = iter(refs)
    take = lambda n: [next(it) for _ in range(n)]
    (scal,) = take(1)
    (gathered,) = take(1)
    w_own, w_sib = take(2)
    pairs = [take(2) for _ in range(n_pairs)]
    gate, up, pg, pu = take(4)
    acc_in = None if first else take(2)
    if last:
        left_t, r_down, lo, hi, scale = take(5)
        keep, send = take(2)
    else:
        acc_out = take(2)
    og, wbuf, gbuf, ubuf, pbuf, grads, og_sem, sems, p_sem = take(9)
    s, y = scal[0], scal[2]
    n = len(tiles)

    def fetch(t, slot, with_grad=False):
        for i, (pair, row, off, mine) in enumerate(tiles):
            if with_grad and i:
                break

            @pl.when(t == i)
            def _(pair=pair, row=row, off=off, mine=mine, i=i):
                h = y if mine else 1 - y
                at = pl.multiple_of(h * half + off, 128)
                rows = pl.ds(at, TILE)
                here = pl.ds(row, TILE)
                a, b = pairs[pair]
                for j, src in enumerate(
                    (w_own.at[rows], w_sib.at[rows], a.at[here], b.at[here])
                ):
                    if with_grad:
                        pltpu.make_async_copy(gathered.at[s ^ j], og.at[s ^ j], og_sem.at[j]).start()
                    pltpu.make_async_copy(src, wbuf.at[slot, j], sems.at[slot, j]).start()
                pltpu.make_async_copy(gate.at[:, rows], gbuf.at[slot], sems.at[slot, 4]).start()
                pltpu.make_async_copy(up.at[:, rows], ubuf.at[slot], sems.at[slot, 5]).start()
                mine_p = pl.ds(i * TILE, TILE)
                pltpu.make_async_copy(pg.at[rows], pbuf.at[0, mine_p], p_sem).start()
                pltpu.make_async_copy(pu.at[rows], pbuf.at[1, mine_p], p_sem).start()

    def weights_arrive(slot, j):
        pltpu.make_async_copy(w_own.at[pl.ds(0, TILE)], wbuf.at[slot, j], sems.at[slot, j]).wait()

    def dots(slot, before):
        total = None
        for j in range(4):
            before(j)
            part = lax.dot_general(
                og[s ^ j],
                wbuf[slot, j],
                (((1,), (1,)), ((), ())),
                preferred_element_type=F32,
            )
            total = part if total is None else total + part
        return total

    def finish(t, slot, total):
        activated, slope = silu_pair(gbuf[slot].astype(F32))
        columns = pl.ds(pl.multiple_of(t * TILE, 128), TILE)
        grads[0, :, columns] = (total * ubuf[slot].astype(F32) * slope).astype(BF16)
        grads[1, :, columns] = (total * activated).astype(BF16)

    def streams_arrive(slot):
        rows = pl.ds(0, TILE)
        pltpu.make_async_copy(gate.at[:, rows], gbuf.at[slot], sems.at[slot, 4]).wait()
        pltpu.make_async_copy(up.at[:, rows], ubuf.at[slot], sems.at[slot, 5]).wait()

    def first_quarter(j):
        weights_arrive(0, j)
        pltpu.make_async_copy(gathered.at[j], og.at[j], og_sem.at[j]).wait()

    fetch(jnp.int32(0), 0, True)
    if n > 1:
        fetch(jnp.int32(1), 1)
    total = dots(0, first_quarter)
    streams_arrive(0)
    finish(0, 0, total)

    @pl.loop(1, n)
    def _(t):
        slot = lax.rem(t, 2)
        @pl.when(t + 1 < n)
        def _():
            fetch(t + 1, 1 - slot)
        for j in range(4):
            weights_arrive(slot, j)
        streams_arrive(slot)
        finish(t, slot, dots(slot, lambda j: None))

    every = pl.ds(0, n * TILE)
    pltpu.make_async_copy(pg.at[every], pbuf.at[0], p_sem).wait()
    pltpu.make_async_copy(pu.at[every], pbuf.at[1], p_sem).wait()
    acc = [jnp.dot(grads[i], pbuf[i], preferred_element_type=F32) for i in range(2)]
    if not first:
        acc = [a + b[...] for a, b in zip(acc, acc_in)]
    if not last:
        acc_out[0][...] = acc[0]
        acc_out[1][...] = acc[1]
        return
    tokens = acc[0].shape[0]
    where = s * tokens + lax.broadcasted_iota(jnp.int32, (tokens, 256), 0)
    weight = jnp.where((where >= lo[...]) & (where < hi[...]), scale[...], 0.0)
    for l in range(3):
        right = (r_down[...] if l == 2 else acc[l]) * weight
        m = jnp.dot(
            left_t[pl.ds(64 * l, 64), :],
            right,
            precision=lax.Precision.HIGHEST,
            preferred_element_type=F32,
        )
        even = lax.rem(s, 2) == 0
        keep[l] = jnp.where(even, m[:, :128], m[:, 128:])
        send[l] = jnp.where(even, m[:, 128:], m[:, :128])


def grads_call(tiles, half, scal, gathered, weights, pairs, streams, acc, tail):
    _, tokens, depth = gathered.shape
    first, last = acc is None, tail is not None
    hbm = pl.BlockSpec(memory_space=pltpu.HBM)
    vmem = pl.BlockSpec(memory_space=pltpu.VMEM)
    args = [scal, gathered, *weights, *[a for p in pairs for a in p], *streams]
    specs = [pl.BlockSpec(memory_space=pltpu.SMEM)] + [hbm] * (len(args) - 1)
    if not first:
        args += list(acc)
        specs += [vmem] * 2
    if last:
        args += list(tail)
        specs += [vmem] * len(tail)
        outs = [jax.ShapeDtypeStruct((3, 64, 128), F32)] * 2
    else:
        outs = [jax.ShapeDtypeStruct((tokens, 256), F32)] * 2
    units = len(tiles) * TILE
    return pl.pallas_call(
        functools.partial(grads_kernel, tiles, half, first, last),
        out_shape=outs,
        in_specs=specs,
        out_specs=[vmem] * 2,
        scratch_shapes=[
            pltpu.VMEM((4, tokens, depth), BF16),
            pltpu.VMEM((2, 4, TILE, depth), BF16),
            pltpu.VMEM((2, tokens, TILE), BF16),
            pltpu.VMEM((2, tokens, TILE), BF16),
            pltpu.VMEM((2, units, 256), BF16),
            pltpu.VMEM((2, tokens, units), BF16),
            pltpu.SemaphoreType.DMA((4,)),
            pltpu.SemaphoreType.DMA((2, 6)),
            pltpu.SemaphoreType.DMA,
        ],
        compiler_params=pltpu.CompilerParams(vmem_limit_bytes=60 * 1024 * 1024),
        cost_estimate=pl.CostEstimate(
            flops=2 * units * tokens * (4 * depth + 512),
            bytes_accessed=2 * (4 * tokens * depth + units * (4 * depth + 2 * tokens)),
            transcendentals=units * tokens,
        ),
    )(*args)


def local(
    layer_input, out_grad, gate_pre, up_pre, w_down, proj_in, proj_ff, proj_down, lengths, slots
):
    tokens = layer_input.shape[0]
    depth = out_grad.shape[1]
    units = w_down.shape[0]
    half = units // 2
    y, s, z = (lax.axis_index(a) for a in ("groups", "seq", "tensor"))
    scal = jnp.stack([s, z, y]).astype(jnp.int32)

    over_x = lambda a: lax.ppermute(a, "seq", [(i, i ^ 2) for i in range(4)])
    over_c = lambda a: lax.ppermute(a, "seq", [(i, i ^ 1) for i in range(4)])
    over_y = lambda a: lax.ppermute(a, "groups", [(0, 1), (1, 0)])
    over_z = lambda a, k: lax.ppermute(a, "tensor", [(i, i ^ k) for i in range(4)])

    count = len(CHUNKS)
    offs = [sum(CHUNKS[:k]) for k in range(count)]
    r, ry = [None] * count, [None] * count
    tie = lax.optimization_barrier
    halves = w_down.reshape(2, half, depth)
    cut = lambda ks: move(
        scal,
        [halves],
        [(0, True, offs[k], i, 0, CHUNKS[k]) for i, k in enumerate(ks)],
        [CHUNKS[k] for k in ks],
    )

    gathered = lax.all_gather(out_grad, "tensor", axis=0, tiled=False)
    r[0] = over_x(cut([0])[0])
    srcs = [None] + list(cut(range(1, count)))
    now = srcs[2:]
    r[1] = over_x(srcs[1])
    w_sib = over_c(w_down)

    column = jnp.arange(64, dtype=jnp.int32)[:, None]
    lane = jnp.arange(256, dtype=jnp.int32)[None, :]
    source = (2 * ((lane // 64) % 2) + lane // 128) * 16 + lane % 16
    spread = (column == source).astype(BF16)
    expand = lambda a: jnp.dot(a, spread, preferred_element_type=F32).astype(BF16)
    ends = jnp.cumsum(lengths)
    pick = slots[:, None] == (lane // 16) % 4
    by_lane = lambda a: jnp.sum(jnp.where(pick, a[:, None], jnp.zeros((), a.dtype)), 0, keepdims=True)
    lo, hi = by_lane(ends - lengths), by_lane(ends)
    scale = by_lane(lax.rsqrt(lengths.astype(F32)))

    swap_after = {
        3: ((0, 0), (0, 1), (1, 0), (1, 1), (2, 0)),
        6: ((2, 1), (3, 0), (3, 1), (4, 0), (4, 1), (5, 0), (5, 1), (6, 0)),
    }
    pairs, where = [], {}

    def swap(members):
        rows = 0
        for k, far in members:
            for row in range(0, CHUNKS[k], TILE):
                where[(k, far, row)] = (len(pairs), rows)
                rows += TILE
        got = [ry[k] if far else r[k] for k, far in members]
        got = got[0] if len(got) == 1 else join(scal, got)
        pairs.append((got, over_c(got)))

    for k in range(count):
        final = k == count - 1
        gate = {"now": now, "r": r[k]}
        if k == 0:
            gate["left"] = (layer_input, gate_pre, up_pre)
        if k == 2:
            gate["left"] = left_t
        if k == count - 2:
            gate["side"] = (proj_ff, proj_down, left_t)
        if final:
            gate["side"], gate["left"] = side, left_t
        if k == 1:
            gate["sib"] = w_sib
        if k >= 2:
            gate["y"] = ry[k - 2]
        if final:
            gate["y5"], gate["all"] = ry[k - 1], gathered
        gate = tie(gate)
        now, r[k] = gate["now"], gate["r"]
        if k + 2 < count:
            r[k + 2] = over_x(now[0])
            now = now[1:]
        if k >= 2:
            ry[k - 2] = gate["y"]
        if k == 1:
            w_sib = gate["sib"]
        ry[k] = over_y(r[k])
        if k == 0:
            tokens_in, gates, uppers = gate["left"]
            activated, _ = silu_pair(gates.astype(F32))
            hidden = (activated * uppers.astype(F32)).astype(BF16)
            in_side = jnp.dot(tokens_in, proj_in, preferred_element_type=F32)
            down_left = jnp.dot(hidden, proj_ff[:, 128:192], preferred_element_type=F32)
            left_t = jnp.concatenate([in_side, down_left], axis=1).T
        if k == 2:
            left_t = gate["left"]
        if k == count - 2:
            ff, down, left_t = gate["side"]
            left_t = (left_t, over_z(left_t.astype(BF16), 1))
            down_rows = lax.dynamic_slice_in_dim(down, z * depth, depth, 0)
            side = (
                expand(ff[:, 0:64]),
                expand(ff[:, 64:128]),
                jnp.dot(out_grad, expand(down_rows), preferred_element_type=F32),
            )
        if final:
            pg, pu, r_down = gate["side"]
            left_t = gate["left"][0] + gate["left"][1].astype(F32)
            left_t = left_t + over_z(left_t.astype(BF16), 2).astype(F32)
            ry[k - 1], gathered = gate["y5"], gate["all"]
        if k in swap_after:
            swap(swap_after[k])

    def grads(members, acc, tail=None):
        used, tiles = [], []
        for k, far in members:
            for row in range(0, CHUNKS[k], TILE):
                pair, at = where[(k, far, row)]
                if pair not in used:
                    used.append(pair)
                tiles.append((used.index(pair), at, offs[k] + row, not far))
        return grads_call(
            tuple(tiles), half, scal, gathered, (w_down, w_sib), [pairs[p] for p in used],
            (gate_pre, up_pre, pg, pu), acc, tail,
        )

    gathered, left_t = tie((gathered, left_t))
    acc = grads(swap_after[3], None)
    ry[6], acc = tie((ry[6], acc))
    swap(((6, 1),))
    acc = grads(swap_after[6] + ((6, 1),), acc, (left_t, r_down, lo, hi, scale))
    keep, send = acc
    x = s // 2
    total = (keep + over_c(send)).reshape(3, 64, 2, 64)
    part = lambda a, axis, at: lax.dynamic_index_in_dim(a, at, axis, keepdims=False)
    total = part(total, 2, x) + over_x(part(total, 2, 1 - x))
    total = total.reshape(3, 2, 32, 64)
    total = part(total, 1, z // 2) + over_z(part(total, 1, 1 - z // 2), 2)
    total = total.reshape(3, 2, 16, 64)
    total = part(total, 1, z % 2) + over_z(part(total, 1, 1 - z % 2), 1)
    return total.reshape(3, 16, 4, 16).transpose(2, 0, 1, 3)


def solution(mesh):
    placed = (
        P(("groups", "seq"), "tensor"),
        P(("groups", "seq"), "tensor"),
        P(("groups", "seq"), "tensor"),
        P(("groups", "seq"), "tensor"),
        P("tensor", "seq"),
        P("tensor", None),
        P("tensor", None),
        P(),
        P("groups"),
        P("groups"),
    )
    small = (mesh.shape["groups"], mesh.shape["seq"], mesh.shape["tensor"]) == (2, 4, 4)
    return jax.shard_map(
        local if small else general,
        mesh=mesh,
        in_specs=placed,
        out_specs=P("groups", None, "tensor", "seq"),
        check_vma=False,
    )
```

time: 257 us -> 183 us (0.71)
  waiting for transfers between devices: 110 us -> 65.5 us
  local copies, waits for them, and re-layouts: 32.8 us -> 1.96 us
  starting transfers between devices: 35.7 us -> 32.6 us
  other arithmetic: 1.27 us -> 3.95 us
    unnamed x88 -> x24, local copies, waits for them, and re-layouts: 28.3 us -> 0.85 us
    ppermute x7, waiting for transfers between devices: 23.5 us -> 1.54 us  [local(): over_y = lambda a: lax.ppermute(a, 'groups', [(0, 1), (1, 0)])]
    ppermute x6 -> x0, waiting for transfers between devices: 20.2 us -> none  [the longest x3 20.2 us: z_step(): fall = lax.ppermute(fall, 'tensor', [(i + 1, i) for i in range(0, 4 - k)])]
    pallas_call x0 -> x4, Pallas kernels: none -> 13.6 us  [move(): pl.pallas_call(functools.partial(move_kernel, tuple(moves), len(ins)), ou...]
    pallas_call x3 -> x2, Pallas kernels: 49.4 us -> 37.7 us  [grads_call(): pl.pallas_call(functools.partial(grads_kernel, tiles, half, first, last),...]
    ppermute x6 -> x0, starting transfers between devices: 10.3 us -> none  [the longest x3 6.43 us: z_step(): rise = lax.ppermute(rise, 'tensor', [(i, i + 1) for i in range(k - 1, 3)])]
    ppermute x8, waiting for transfers between devices: 56.5 us -> 46.3 us  [local(): over_x = lambda a: lax.ppermute(a, 'seq', [(i, i ^ 2) for i in range(4)])]
    ppermute x2 -> x4, waiting for transfers between devices: 8.76 us -> 15.5 us  [local(): lax.ppermute(a, 'tensor', [(i, i ^ k) for i in range(4)])]
  transfers between devices with their start and end apart: 40 -> 25, of which waited for: 18 -> 13; matrix products, arithmetic and copies ran while one was open for 7% -> 9% of each run, Pallas kernels for 15% -> 13%
where the time goes in v2:
time: 183 us
  waiting for transfers between devices  65.5 us (36%)
  Pallas kernels  51.2 us (28%)
  starting transfers between devices  32.6 us (18%)
  between operations  13.7 us (7%)
  matrix products  13.5 us (7%)
  other arithmetic  3.95 us (2%)
  local copies, waits for them, and re-layouts  1.96 us (1%)
    ppermute x8, waiting for transfers between devices, local(): over_x = lambda a: lax.ppermute(a, 'seq', [(i, i ^ 2) for i in range(4)])  46.3 us
    pallas_call x2, Pallas kernels, grads_call(): pl.pallas_call(functools.partial(grads_kernel, tiles, half, first, last),...  37.7 us
    ppermute x4, waiting for transfers between devices, local(): lax.ppermute(a, 'tensor', [(i, i ^ k) for i in range(4)])  15.5 us
    ppermute x8, starting transfers between devices, local(): over_x = lambda a: lax.ppermute(a, 'seq', [(i, i ^ 2) for i in range(4)])  13.9 us
    pallas_call x4, Pallas kernels, move(): pl.pallas_call(functools.partial(move_kernel, tuple(moves), len(ins)), ou...  13.6 us
    ppermute x7, starting transfers between devices, local(): over_y = lambda a: lax.ppermute(a, 'groups', [(0, 1), (1, 0)])  11.8 us
    dot_general x2, matrix products, local(): jnp.dot(a, spread, preferred_element_type=F32).astype(BF16)  5.87 us
    ppermute x4, starting transfers between devices, local(): lax.ppermute(a, 'tensor', [(i, i ^ k) for i in range(4)])  5.56 us
  transfers between devices with their start and end apart: 25, of which 13 were waited for; matrix products, arithmetic and copies ran while one was open for 9% of the time, Pallas kernels for 13%

profile of v2, /device:TPU:0, one launch (start us, length us, event | category | flops | bytes accessed | tf_op | source)
XLA Modules:
  0.0 182.5 jit_solution(11854866033281129250)
XLA Ops:
  7.8 2.5 %shard_map.101 = bf16[256,1024]{1,0:T(8,128)(2,1)} custom-call(s32[3]{0:T(128)} %pad_add_fusion.refs_0_, bf16[2,1792,1024]{2,1,0:T(8,128)(2,1)} %bitcast.31), custom_call_target="tpu_custom_call" | custom-call | bytes 1048576 | tf_op jit(solution)/shard_map/pallas_call | solution.py:110
  10.4 3.0 %collective-permute-start = (bf16[256,1024]{1,0:T(8,128)(2,1)}, bf16[256,1024]{1,0:T(8,128)(2,1)S(1)}, u32[]{:S(2)}, u32[]{:S(2)}) collective-permute-start(bf16[256,1024]{1,0:T(8,128)(2,1)} %shard_map.101), channel_id=1, source_target_pairs={{0,8},{4,12},{8,0},{12,4},{1,9},{5,13},{9,1},{13,5},{2,10},{6,14},... | collective-permute-start | bytes 1572872 | tf_op jit(solution)/shard_map/ppermute | solution.py:304
  13.4 3.5 %shard_map.100 = (bf16[256,1024]{1,0:T(8,128)(2,1)}, bf16[256,1024]{1,0:T(8,128)(2,1)}, bf16[256,1024]{1,0:T(8,128)(2,1)}, bf16[256,1024]{1,0:T(8,128)(2,1)}, bf...) custom-call(s32[3]{0:T(128)} %pad_add_fusion.refs_0_, bf16[2,1792,1024]{2,1,0:T(8,128)(2,1)} %bitcast.32), custom_call_target="tpu_custom_call" | custom-call | bytes 6291456 | tf_op jit(solution)/shard_map/pallas_call | solution.py:110
  17.0 9.4 %collective-permute-done.refs_1_ = bf16[256,1024]{1,0:T(8,128)(2,1)S(1)} collective-permute-done((bf16[256,1024]{1,0:T(8,128)(2,1)}, bf16[256,1024]{1,0:T(8,128)(2,1)S(1)}, u32[]{:S(2)}, u32[]{:S(2)}) %collective-permute-start) | collective-permute-done | bytes 524320 | tf_op jit(solution)/shard_map/ppermute | solution.py:304
  26.4 2.1 %collective-permute-start.4 = (bf16[256,1024]{1,0:T(8,128)(2,1)S(1)}, bf16[256,1024]{1,0:T(8,128)(2,1)S(1)}, u32[]{:S(2)}, u32[]{:S(2)}) collective-permute-start(bf16[256,1024]{1,0:T(8,128)(2,1)S(1)} %collective-permute-done.refs_1_), channel_id=1, source_target_pairs={{0,16},{16,0},{1,17},{17,1},{2,18},{18,2},{3,19},{19,3},{4,20},{20... | collective-permute-start | bytes 1572872 | tf_op jit(solution)/shard_map/ppermute | solution.py:306
  29.9 7.7 %collective-permute-done.1.refs_3_ = bf16[256,1024]{1,0:T(8,128)(2,1)S(1)} collective-permute-done((bf16[256,1024]{1,0:T(8,128)(2,1)}, bf16[256,1024]{1,0:T(8,128)(2,1)S(1)}, u32[]{:S(2)}, u32[]{:S(2)}) %collective-permute-start.1) | collective-permute-done | bytes 524320 | tf_op jit(solution)/shard_map/ppermute | solution.py:304
  41.2 4.6 %fusion.5 = f32[512,64]{0,1:T(8,128)S(1)} fusion(bf16[512,3584]{1,0:T(8,128)(2,1)} %refs_9_.1, bf16[512,3584]{1,0:T(8,128)(2,1)} %refs_8_.1, bf16[3584,192]{0,1:T(8,128)(2,1)} %param.16), kind=kOutput, calls=%fused_computation.9 | convolution fusion | flops 249561088 | bytes 7929856 | tf_op jit(solution)/shard_map/dot_general | solution.py:387
  46.4 2.5 %collective-permute-done.3.refs_5_ = bf16[256,1024]{1,0:T(8,128)(2,1)} collective-permute-done((bf16[256,1024]{1,0:T(8,128)(2,1)}, bf16[256,1024]{1,0:T(8,128)(2,1)}, u32[]{:S(2)}, u32[]{:S(2)}) %collective-permute-start.3) | collective-permute-done | bytes 524320 | tf_op jit(solution)/shard_map/ppermute | solution.py:304
  52.5 7.5 %collective-permute-done.5.refs_2_ = bf16[256,1024]{1,0:T(8,128)(2,1)S(1)} collective-permute-done((bf16[256,1024]{1,0:T(8,128)(2,1)}, bf16[256,1024]{1,0:T(8,128)(2,1)S(1)}, u32[]{:S(2)}, u32[]{:S(2)}) %collective-permute-start.5) | collective-permute-done | bytes 524320 | tf_op jit(solution)/shard_map/ppermute | solution.py:304
  60.1 2.1 %collective-permute-start.7 = (bf16[256,1024]{1,0:T(8,128)(2,1)}, bf16[256,1024]{1,0:T(8,128)(2,1)}, u32[]{:S(2)}, u32[]{:S(2)}) collective-permute-start(bf16[256,1024]{1,0:T(8,128)(2,1)} %get-tuple-element.84), channel_id=1, source_target_pairs={{0,8},{4,12},{8,0},{12,4},{1,9},{5,13},{9,1},{13,5},{2,10},{6,14},... | collective-permute-start | bytes 1572872 | tf_op jit(solution)/shard_map/ppermute | solution.py:304
  63.7 7.7 %collective-permute-done.10.refs_4_ = bf16[256,1024]{1,0:T(8,128)(2,1)} collective-permute-done((bf16[256,1024]{1,0:T(8,128)(2,1)}, bf16[256,1024]{1,0:T(8,128)(2,1)}, u32[]{:S(2)}, u32[]{:S(2)}) %collective-permute-start.10) | collective-permute-done | bytes 524320 | tf_op jit(solution)/shard_map/ppermute | solution.py:304
  75.0 7.7 %collective-permute-done.7.refs_6_ = bf16[256,1024]{1,0:T(8,128)(2,1)} collective-permute-done((bf16[256,1024]{1,0:T(8,128)(2,1)}, bf16[256,1024]{1,0:T(8,128)(2,1)}, u32[]{:S(2)}, u32[]{:S(2)}) %collective-permute-start.7) | collective-permute-done | bytes 524320 | tf_op jit(solution)/shard_map/ppermute | solution.py:304
  86.4 2.9 %convolution_convert_fusion.refs_9_.refs_11_ = bf16[3584,256]{1,0:T(8,128)(2,1)} fusion(bf16[3584,192]{0,1:T(8,128)(2,1)} %param.16, s32[256]{0:T(256)S(1)} %fusion.26), kind=kOutput, calls=%fused_computation.7 | convolution fusion | flops 118374400 | bytes 2294784 | tf_op jit(solution)/shard_map/dot_general | solution.py:332
  89.3 3.0 %convolution_convert_fusion.1.refs_8_.refs_10_ = bf16[3584,256]{1,0:T(8,128)(2,1)} fusion(bf16[3584,192]{0,1:T(8,128)(2,1)} %param.16, s32[256]{0:T(256)S(1)} %fusion.26), kind=kOutput, calls=%fused_computation.8 | convolution fusion | flops 118374400 | bytes 2294784 | tf_op jit(solution)/shard_map/dot_general | solution.py:332
  92.3 2.6 %fusion.8.refs_15_ = f32[512,256]{1,0:T(8,128)} fusion(bf16[512,1024]{1,0:T(8,128)(2,1)S(1)} %copy-done.1, bf16[4096,64]{0,1:T(8,128)(2,1)} %param.17, s32[]{:T(128)S(6)} %select_n.127, s32[256]{0:T(256)S(1)} %fusion.26), kind=kOutput, calls=%fused_computation.12 | convolution fusion | flops 302268416 | bytes 1704964 | tf_op jit(solution)/shard_map/dot_general | solution.py:398
  96.4 4.2 %shard_map.102.refs_4_ = bf16[2048,1024]{1,0:T(8,128)(2,1)} custom-call(s32[3]{0:T(128)} %pad_add_fusion.refs_0_, bf16[256,1024]{1,0:T(8,128)(2,1)} %collective-permute-done.11.refs_1_, bf16[256,1024]{1,0:T(8,128)(2,1)} %copy-done.4, bf16[256,1024]{1,0:T(8,128)(2,1)} %collective-permute-done.8.refs_3_, bf16[256,1024]{1,0:T(8,128)(2,1)} %collective-permute-done.10.refs_4_, ...), custom_call_target="tpu_custom_call" | custom-call | bytes 8388608 | tf_op jit(solution)/shard_map/pallas_call | solution.py:110
  100.7 3.3 %shard_map.103.refs_4_ = bf16[1280,1024]{1,0:T(8,128)(2,1)} custom-call(s32[3]{0:T(128)} %pad_add_fusion.refs_0_, bf16[256,1024]{1,0:T(8,128)(2,1)} %copy-done.5, bf16[256,1024]{1,0:T(8,128)(2,1)} %copy-done.7, bf16[256,1024]{1,0:T(8,128)(2,1)} %copy-done.6, bf16[256,1024]{1,0:T(8,128)(2,1)} %copy-done.8, bf16[256,1024]{1,0:T(8,128)(2,1)} %collective-permute-done.3.refs_5_), custom_call_target="tpu_custom_call" | custom-call | bytes 5242880 | tf_op jit(solution)/shard_map/pallas_call | solution.py:110
  104.8 2.7 %collective-permute-start.15 = (bf16[192,512]{1,0:T(8,128)(2,1)S(1)}, bf16[192,512]{1,0:T(8,128)(2,1)S(1)}, u32[]{:S(2)}, u32[]{:S(2)}) collective-permute-start(bf16[192,512]{1,0:T(8,128)(2,1)S(1)} %fusion.12), channel_id=1, source_target_pairs={{0,2},{1,3},{2,0},{3,1},{4,6},{5,7},{6,4},{7,5},{8,10},{9,11},{10,... | collective-permute-start | bytes 589832 | tf_op jit(solution)/shard_map/ppermute | solution.py:307
  109.0 7.8 %collective-permute-done.15 = bf16[192,512]{1,0:T(8,128)(2,1)S(1)} collective-permute-done((bf16[192,512]{1,0:T(8,128)(2,1)S(1)}, bf16[192,512]{1,0:T(8,128)(2,1)S(1)}, u32[]{:S(2)}, u32[]{:S(2)}) %collective-permute-start.15) | collective-permute-done | bytes 196640 | tf_op jit(solution)/shard_map/ppermute | solution.py:307
  117.7 14.6 %shard_map.104 = (f32[512,256]{1,0:T(8,128)}, f32[512,256]{1,0:T(8,128)}) custom-call(s32[3]{0:T(128)} %pad_add_fusion.refs_0_, bf16[4,512,1024]{2,1,0:T(8,128)(2,1)} %bitcast.33, bf16[3584,1024]{1,0:T(8,128)(2,1)} %refs_2_.3, bf16[3584,1024]{1,0:T(8,128)(2,1)} %collective-permute-done.2.refs_3_, bf16[1280,1024]{1,0:T(8,128)(2,1)} %shard_map.103.refs_4_, ...), custom_call_target="tpu_custom_call" | custom-call | flops 6039797760 | bytes 17301504 | tf_op jit(solution)/shard_map/pallas_call | solution.py:269
  135.1 23.0 %shard_map.105 = (f32[3,64,128]{2,1,0:T(8,128)}, f32[3,64,128]{2,1,0:T(8,128)}) custom-call(s32[3]{0:T(128)} %pad_add_fusion.refs_0_, bf16[4,512,1024]{2,1,0:T(8,128)(2,1)} %bitcast.34, bf16[3584,1024]{1,0:T(8,128)(2,1)} %refs_2_.3, bf16[3584,1024]{1,0:T(8,128)(2,1)} %collective-permute-done.2.refs_3_, bf16[2048,1024]{1,0:T(8,128)(2,1)} %shard_map.102.refs_4_, ...), custom_call_target="tpu_custom_call" | custom-call | flops 10871635968 | bytes 27787264 | tf_op jit(solution)/shard_map/pallas_call | solution.py:269
  162.0 3.9 %collective-permute-done.21 = f32[3,64,64]{2,1,0:T(8,128)S(1)} collective-permute-done((f32[3,64,64]{2,1,0:T(8,128)S(1)}, f32[3,64,64]{2,1,0:T(8,128)S(1)}, u32[]{:S(2)}, u32[]{:S(2)}) %collective-permute-start.21) | collective-permute-done | bytes 49184 | tf_op jit(solution)/shard_map/ppermute | solution.py:304
  166.0 5.0 %collective-permute-done.22 = f32[3,32,64]{2,1,0:T(8,128)S(1)} collective-permute-done((f32[3,32,64]{2,1,0:T(8,128)S(1)}, f32[3,32,64]{2,1,0:T(8,128)S(1)}, u32[]{:S(2)}, u32[]{:S(2)}) %collective-permute-start.22) | collective-permute-done | bytes 24608 | tf_op jit(solution)/shard_map/ppermute | solution.py:307
  172.2 2.7 %collective-permute-done.23 = f32[3,16,64]{2,1,0:T(8,128)S(1)} collective-permute-done((f32[3,16,64]{2,1,0:T(8,128)S(1)}, f32[3,16,64]{2,1,0:T(8,128)S(1)}, u32[]{:S(2)}, u32[]{:S(2)}) %collective-permute-start.23) | collective-permute-done | bytes 12320 | tf_op jit(solution)/shard_map/ppermute | solution.py:307
  (84 shorter events, 32.9 us)
Async XLA Ops:
  6.5 88.3 %all-gather.3.cloned.1.call-start = ((), (), s32[]{:S(2)}) async-start(), calls=%async_computation | async-start | bytes 5242880 | tf_op jit(solution)/shard_map/all_gather | solution.py:321
  6.5 31.1 %collective-permute-start.2 = (bf16[3584,1024]{1,0:T(8,128)(2,1)}, bf16[3584,1024]{1,0:T(8,128)(2,1)}, u32[]{:S(2)}, u32[]{:S(2)}) collective-permute-start(bf16[3584,1024]{1,0:T(8,128)(2,1)} %refs_2_.3), channel_id=1, source_target_pairs={{0,4},{4,0},{8,12},{12,8},{1,5},{5,1},{9,13},{13,9},{2,6},{6,2},{1... | collective-permute-start | bytes 22020104 | tf_op jit(solution)/shard_map/ppermute | solution.py:305
  10.4 16.0 %collective-permute-start = (bf16[256,1024]{1,0:T(8,128)(2,1)}, bf16[256,1024]{1,0:T(8,128)(2,1)S(1)}, u32[]{:S(2)}, u32[]{:S(2)}) collective-permute-start(bf16[256,1024]{1,0:T(8,128)(2,1)} %shard_map.101), channel_id=1, source_target_pairs={{0,8},{4,12},{8,0},{12,4},{1,9},{5,13},{9,1},{13,5},{2,10},{6,14},... | collective-permute-start | bytes 1572872 | tf_op jit(solution)/shard_map/ppermute | solution.py:304
  16.9 20.7 %collective-permute-start.1 = (bf16[256,1024]{1,0:T(8,128)(2,1)}, bf16[256,1024]{1,0:T(8,128)(2,1)S(1)}, u32[]{:S(2)}, u32[]{:S(2)}) collective-permute-start(bf16[256,1024]{1,0:T(8,128)(2,1)} %get-tuple-element.74), channel_id=1, source_target_pairs={{0,8},{4,12},{8,0},{12,4},{1,9},{5,13},{9,1},{13,5},{2,10},{6,14},... | collective-permute-start | bytes 1572872 | tf_op jit(solution)/shard_map/ppermute | solution.py:304
  26.4 20.0 %collective-permute-start.4 = (bf16[256,1024]{1,0:T(8,128)(2,1)S(1)}, bf16[256,1024]{1,0:T(8,128)(2,1)S(1)}, u32[]{:S(2)}, u32[]{:S(2)}) collective-permute-start(bf16[256,1024]{1,0:T(8,128)(2,1)S(1)} %collective-permute-done.refs_1_), channel_id=1, source_target_pairs={{0,16},{16,0},{1,17},{17,1},{2,18},{18,2},{3,19},{19,3},{4,20},{20... | collective-permute-start | bytes 1572872 | tf_op jit(solution)/shard_map/ppermute | solution.py:306
  28.5 20.5 %collective-permute-start.3 = (bf16[256,1024]{1,0:T(8,128)(2,1)}, bf16[256,1024]{1,0:T(8,128)(2,1)}, u32[]{:S(2)}, u32[]{:S(2)}) collective-permute-start(bf16[256,1024]{1,0:T(8,128)(2,1)} %get-tuple-element.78), channel_id=1, source_target_pairs={{0,8},{4,12},{8,0},{12,4},{1,9},{5,13},{9,1},{13,5},{2,10},{6,14},... | collective-permute-start | bytes 1572872 | tf_op jit(solution)/shard_map/ppermute | solution.py:304
  37.6 22.5 %collective-permute-start.5 = (bf16[256,1024]{1,0:T(8,128)(2,1)}, bf16[256,1024]{1,0:T(8,128)(2,1)S(1)}, u32[]{:S(2)}, u32[]{:S(2)}) collective-permute-start(bf16[256,1024]{1,0:T(8,128)(2,1)} %get-tuple-element.82), channel_id=1, source_target_pairs={{0,8},{4,12},{8,0},{12,4},{1,9},{5,13},{9,1},{13,5},{2,10},{6,14},... | collective-permute-start | bytes 1572872 | tf_op jit(solution)/shard_map/ppermute | solution.py:304
  39.7 20.4 %collective-permute-start.6 = (bf16[256,1024]{1,0:T(8,128)(2,1)S(1)}, bf16[256,1024]{1,0:T(8,128)(2,1)S(1)}, u32[]{:S(2)}, u32[]{:S(2)}) collective-permute-start(bf16[256,1024]{1,0:T(8,128)(2,1)S(1)} %collective-permute-done.1.refs_3_), channel_id=1, source_target_pairs={{0,16},{16,0},{1,17},{17,1},{2,18},{18,2},{3,19},{19,3},{4,20},{20... | collective-permute-start | bytes 1572872 | tf_op jit(solution)/shard_map/ppermute | solution.py:306
  48.9 22.5 %collective-permute-start.10 = (bf16[256,1024]{1,0:T(8,128)(2,1)}, bf16[256,1024]{1,0:T(8,128)(2,1)}, u32[]{:S(2)}, u32[]{:S(2)}) collective-permute-start(bf16[256,1024]{1,0:T(8,128)(2,1)} %get-tuple-element.89), channel_id=1, source_target_pairs={{0,8},{4,12},{8,0},{12,4},{1,9},{5,13},{9,1},{13,5},{2,10},{6,14},... | collective-permute-start | bytes 1572872 | tf_op jit(solution)/shard_map/ppermute | solution.py:304
  51.0 20.4 %collective-permute-start.11 = (bf16[256,1024]{1,0:T(8,128)(2,1)}, bf16[256,1024]{1,0:T(8,128)(2,1)}, u32[]{:S(2)}, u32[]{:S(2)}) collective-permute-start(bf16[256,1024]{1,0:T(8,128)(2,1)} %collective-permute-done.3.refs_5_), channel_id=1, source_target_pairs={{0,16},{16,0},{1,17},{17,1},{2,18},{18,2},{3,19},{19,3},{4,20},{20... | collective-permute-start | bytes 1572872 | tf_op jit(solution)/shard_map/ppermute | solution.py:306
  60.1 22.6 %collective-permute-start.7 = (bf16[256,1024]{1,0:T(8,128)(2,1)}, bf16[256,1024]{1,0:T(8,128)(2,1)}, u32[]{:S(2)}, u32[]{:S(2)}) collective-permute-start(bf16[256,1024]{1,0:T(8,128)(2,1)} %get-tuple-element.84), channel_id=1, source_target_pairs={{0,8},{4,12},{8,0},{12,4},{1,9},{5,13},{9,1},{13,5},{2,10},{6,14},... | collective-permute-start | bytes 1572872 | tf_op jit(solution)/shard_map/ppermute | solution.py:304
  62.2 20.4 %collective-permute-start.8 = (bf16[256,1024]{1,0:T(8,128)(2,1)S(1)}, bf16[256,1024]{1,0:T(8,128)(2,1)}, u32[]{:S(2)}, u32[]{:S(2)}) collective-permute-start(bf16[256,1024]{1,0:T(8,128)(2,1)S(1)} %collective-permute-done.5.refs_2_), channel_id=1, source_target_pairs={{0,16},{16,0},{1,17},{17,1},{2,18},{18,2},{3,19},{19,3},{4,20},{20... | collective-permute-start | bytes 1572872 | tf_op jit(solution)/shard_map/ppermute | solution.py:306
  71.4 23.4 %collective-permute-start.12 = (bf16[256,1024]{1,0:T(8,128)(2,1)}, bf16[256,1024]{1,0:T(8,128)(2,1)}, u32[]{:S(2)}, u32[]{:S(2)}) collective-permute-start(bf16[256,1024]{1,0:T(8,128)(2,1)} %get-tuple-element.91), channel_id=1, source_target_pairs={{0,8},{4,12},{8,0},{12,4},{1,9},{5,13},{9,1},{13,5},{2,10},{6,14},... | collective-permute-start | bytes 1572872 | tf_op jit(solution)/shard_map/ppermute | solution.py:304
  73.5 21.4 %collective-permute-start.13 = (bf16[256,1024]{1,0:T(8,128)(2,1)}, bf16[256,1024]{1,0:T(8,128)(2,1)}, u32[]{:S(2)}, u32[]{:S(2)}) collective-permute-start(bf16[256,1024]{1,0:T(8,128)(2,1)} %collective-permute-done.10.refs_4_), channel_id=1, source_target_pairs={{0,16},{16,0},{1,17},{17,1},{2,18},{18,2},{3,19},{19,3},{4,20},{20... | collective-permute-start | bytes 1572872 | tf_op jit(solution)/shard_map/ppermute | solution.py:306
  82.6 13.7 %collective-permute-start.14 = (bf16[256,1024]{1,0:T(8,128)(2,1)}, bf16[256,1024]{1,0:T(8,128)(2,1)}, u32[]{:S(2)}, u32[]{:S(2)}) collective-permute-start(bf16[256,1024]{1,0:T(8,128)(2,1)} %collective-permute-done.7.refs_6_), channel_id=1, source_target_pairs={{0,16},{16,0},{1,17},{17,1},{2,18},{18,2},{3,19},{19,3},{4,20},{20... | collective-permute-start | bytes 1572872 | tf_op jit(solution)/shard_map/ppermute | solution.py:306
  84.8 10.1 %collective-permute-start.9 = (bf16[192,512]{1,0:T(8,128)(2,1)S(1)}, bf16[192,512]{1,0:T(8,128)(2,1)S(1)}, u32[]{:S(2)}, u32[]{:S(2)}) collective-permute-start(bf16[192,512]{1,0:T(8,128)(2,1)S(1)} %convert_element_type.37), channel_id=1, source_target_pairs={{0,1},{1,0},{2,3},{3,2},{4,5},{5,4},{6,7},{7,6},{8,9},{9,8},{10,11... | collective-permute-start | bytes 589832 | tf_op jit(solution)/shard_map/ppermute | solution.py:307
  100.7 33.7 %collective-permute-start.16 = (bf16[2048,1024]{1,0:T(8,128)(2,1)}, bf16[2048,1024]{1,0:T(8,128)(2,1)}, u32[]{:S(2)}, u32[]{:S(2)}) collective-permute-start(bf16[2048,1024]{1,0:T(8,128)(2,1)} %shard_map.102.refs_4_), channel_id=1, source_target_pairs={{0,4},{4,0},{8,12},{12,8},{1,5},{5,1},{9,13},{13,9},{2,6},{6,2},{1... | collective-permute-start | bytes 12582920 | tf_op jit(solution)/shard_map/ppermute | solution.py:305
  104.0 13.6 %collective-permute-start.18 = (bf16[1280,1024]{1,0:T(8,128)(2,1)}, bf16[1280,1024]{1,0:T(8,128)(2,1)}, u32[]{:S(2)}, u32[]{:S(2)}) collective-permute-start(bf16[1280,1024]{1,0:T(8,128)(2,1)} %shard_map.103.refs_4_), channel_id=1, source_target_pairs={{0,4},{4,0},{8,12},{12,8},{1,5},{5,1},{9,13},{13,9},{2,6},{6,2},{1... | collective-permute-start | bytes 7864328 | tf_op jit(solution)/shard_map/ppermute | solution.py:305
  104.8 12.0 %collective-permute-start.15 = (bf16[192,512]{1,0:T(8,128)(2,1)S(1)}, bf16[192,512]{1,0:T(8,128)(2,1)S(1)}, u32[]{:S(2)}, u32[]{:S(2)}) collective-permute-start(bf16[192,512]{1,0:T(8,128)(2,1)S(1)} %fusion.12), channel_id=1, source_target_pairs={{0,2},{1,3},{2,0},{3,1},{4,6},{5,7},{6,4},{7,5},{8,10},{9,11},{10,... | collective-permute-start | bytes 589832 | tf_op jit(solution)/shard_map/ppermute | solution.py:307
  107.5 24.9 %collective-permute-start.17 = (bf16[256,1024]{1,0:T(8,128)(2,1)}, bf16[256,1024]{1,0:T(8,128)(2,1)S(1)}, u32[]{:S(2)}, u32[]{:S(2)}) collective-permute-start(bf16[256,1024]{1,0:T(8,128)(2,1)} %collective-permute-done.12.refs_8_), channel_id=1, source_target_pairs={{0,16},{16,0},{1,17},{17,1},{2,18},{18,2},{3,19},{19,3},{4,20},{20... | collective-permute-start | bytes 1572872 | tf_op jit(solution)/shard_map/ppermute | solution.py:306
  132.3 2.0 %collective-permute-start.19 = (bf16[256,1024]{1,0:T(8,128)(2,1)S(1)}, bf16[256,1024]{1,0:T(8,128)(2,1)S(1)}, u32[]{:S(2)}, u32[]{:S(2)}) collective-permute-start(bf16[256,1024]{1,0:T(8,128)(2,1)S(1)} %collective-permute-done.17.refs_6_), channel_id=1, source_target_pairs={{0,4},{4,0},{8,12},{12,8},{1,5},{5,1},{9,13},{13,9},{2,6},{6,2},{1... | collective-permute-start | bytes 1572872 | tf_op jit(solution)/shard_map/ppermute | solution.py:305
  161.0 4.9 %collective-permute-start.21 = (f32[3,64,64]{2,1,0:T(8,128)S(1)}, f32[3,64,64]{2,1,0:T(8,128)S(1)}, u32[]{:S(2)}, u32[]{:S(2)}) collective-permute-start(f32[3,64,64]{2,1,0:T(8,128)S(1)} %bitcast.41), channel_id=1, source_target_pairs={{0,8},{4,12},{8,0},{12,4},{1,9},{5,13},{9,1},{13,5},{2,10},{6,14},... | collective-permute-start | bytes 147464 | tf_op jit(solution)/shard_map/ppermute | solution.py:304
  165.9 5.1 %collective-permute-start.22 = (f32[3,32,64]{2,1,0:T(8,128)S(1)}, f32[3,32,64]{2,1,0:T(8,128)S(1)}, u32[]{:S(2)}, u32[]{:S(2)}) collective-permute-start(f32[3,32,64]{2,1,0:T(8,128)S(1)} %dynamic-slice_bitcast_fusion), channel_id=1, source_target_pairs={{0,2},{1,3},{2,0},{3,1},{4,6},{5,7},{6,4},{7,5},{8,10},{9,11},{10,... | collective-permute-start | bytes 73736 | tf_op jit(solution)/shard_map/ppermute | solution.py:307
  171.0 3.9 %collective-permute-start.23 = (f32[3,16,64]{2,1,0:T(8,128)S(1)}, f32[3,16,64]{2,1,0:T(8,128)S(1)}, u32[]{:S(2)}, u32[]{:S(2)}) collective-permute-start(f32[3,16,64]{2,1,0:T(8,128)S(1)} %dynamic-slice_bitcast_fusion.1), channel_id=1, source_target_pairs={{0,1},{1,0},{2,3},{3,2},{4,5},{5,4},{6,7},{7,6},{8,9},{9,8},{10,11... | collective-permute-start | bytes 36872 | tf_op jit(solution)/shard_map/ppermute | solution.py:307
  (13 other events, 208.2 us)
Sparse Core Ops, SparseCore 0:
  8.9 83.5 all-gather.2

commit v3 on v2

--- a/solution.py
+++ b/solution.py
@@ -204,10 +204,10 @@
     def first_quarter(j):
         weights_arrive(0, j)
         pltpu.make_async_copy(gathered.at[j], og.at[j], og_sem.at[j]).wait()
+        if j == 2 and n > 1:
+            fetch(jnp.int32(1), 1)
 
     fetch(jnp.int32(0), 0, True)
-    if n > 1:
-        fetch(jnp.int32(1), 1)
     total = dots(0, first_quarter)
     streams_arrive(0)
     finish(0, 0, total)
@@ -337,9 +337,15 @@
     scale = by_lane(lax.rsqrt(lengths.astype(F32)))
 
     swap_after = {
-        3: ((0, 0), (0, 1), (1, 0), (1, 1), (2, 0)),
-        6: ((2, 1), (3, 0), (3, 1), (4, 0), (4, 1), (5, 0), (5, 1), (6, 0)),
+        1: (((0, 0),),),
+        3: (((0, 1),),),
+        6: (
+            (
+                (1, 0), (1, 1), (2, 0), (2, 1), (3, 0), (3, 1), (4, 0), (4, 1), (5, 0), (5, 1), (6, 0),
+            ),
+        ),
     }
+    swapped_by = {3: 0, 5: 1}
     pairs, where = [], {}
 
     def swap(members):
@@ -358,9 +364,11 @@
         if k == 0:
             gate["left"] = (layer_input, gate_pre, up_pre)
         if k == 2:
-            gate["left"] = left_t
+            gate["left"], gate["lanes"] = left_t, (lo, hi, scale)
         if k == count - 2:
             gate["side"] = (proj_ff, proj_down, left_t)
+        if k in swapped_by:
+            gate["c"] = pairs[swapped_by[k]]
         if final:
             gate["side"], gate["left"] = side, left_t
         if k == 1:
@@ -369,6 +377,7 @@
             gate["y"] = ry[k - 2]
         if final:
             gate["y5"], gate["all"] = ry[k - 1], gathered
+            gate["hold"] = r[1:k], ry[1 : k - 2]
         gate = tie(gate)
         now, r[k] = gate["now"], gate["r"]
         if k + 2 < count:
@@ -387,7 +396,7 @@
             down_left = jnp.dot(hidden, proj_ff[:, 128:192], preferred_element_type=F32)
             left_t = jnp.concatenate([in_side, down_left], axis=1).T
         if k == 2:
-            left_t = gate["left"]
+            left_t, (lo, hi, scale) = gate["left"], gate["lanes"]
         if k == count - 2:
             ff, down, left_t = gate["side"]
             left_t = (left_t, over_z(left_t.astype(BF16), 1))
@@ -402,8 +411,11 @@
             left_t = gate["left"][0] + gate["left"][1].astype(F32)
             left_t = left_t + over_z(left_t.astype(BF16), 2).astype(F32)
             ry[k - 1], gathered = gate["y5"], gate["all"]
-        if k in swap_after:
-            swap(swap_after[k])
+            r[1:k], ry[1 : k - 2] = gate["hold"]
+        if k in swapped_by:
+            pairs[swapped_by[k]] = gate["c"]
+        for members in swap_after.get(k, ()):
+            swap(members)
 
     def grads(members, acc, tail=None):
         used, tiles = [], []
@@ -418,11 +430,11 @@
             (gate_pre, up_pre, pg, pu), acc, tail,
         )
 
-    gathered, left_t = tie((gathered, left_t))
-    acc = grads(swap_after[3], None)
-    ry[6], acc = tie((ry[6], acc))
+    early, late = ((0, 0), (0, 1)), swap_after[6][0]
+    acc = grads(early, None)
+    ry[6], left_t, acc = tie((ry[6], left_t, acc))
     swap(((6, 1),))
-    acc = grads(swap_after[6] + ((6, 1),), acc, (left_t, r_down, lo, hi, scale))
+    acc = grads(late + ((6, 1),), acc, (left_t, r_down, lo, hi, scale))
     keep, send = acc
     x = s // 2
     total = (keep + over_c(send)).reshape(3, 64, 2, 64)

time: 183 us -> 176 us (0.962)
  waiting for transfers between devices: 65.5 us -> 57.9 us
  Pallas kernels: 51.2 us -> 48.8 us
    ppermute x4, waiting for transfers between devices: 15.5 us -> 4.85 us  [local(): lax.ppermute(a, 'tensor', [(i, i ^ k) for i in range(4)])]
    ppermute x7, waiting for transfers between devices: 1.54 us -> 5.03 us  [local(): over_y = lambda a: lax.ppermute(a, 'groups', [(0, 1), (1, 0)])]
    ppermute x4, starting transfers between devices: 5.56 us -> 8.4 us  [local(): lax.ppermute(a, 'tensor', [(i, i ^ k) for i in range(4)])]
    ppermute x8, waiting for transfers between devices: 46.3 us -> 44.4 us  [local(): over_x = lambda a: lax.ppermute(a, 'seq', [(i, i ^ 2) for i in range(4)])]
    pallas_call x4 -> x3, Pallas kernels: 13.6 us -> 11.9 us  [move(): pl.pallas_call(functools.partial(move_kernel, tuple(moves), len(ins)), ou...]
  transfers between devices with their start and end apart: 25 -> 26, of which waited for: 13 -> 12; matrix products, arithmetic and copies ran while one was open for 9% -> 10% of each run, Pallas kernels for 13% -> 9%
where the time goes in v3:
time: 176 us; the launch traced here: 175 us
  waiting for transfers between devices  57.9 us (33%)
  Pallas kernels  48.8 us (28%)
  starting transfers between devices  34.4 us (20%)
  matrix products  13.6 us (8%)
  between operations  13.6 us (8%)
  other arithmetic  4.04 us (2%)
  local copies, waits for them, and re-layouts  2.78 us (2%)
    ppermute x8, waiting for transfers between devices, local(): over_x = lambda a: lax.ppermute(a, 'seq', [(i, i ^ 2) for i in range(4)])  44.4 us
    pallas_call x2, Pallas kernels, grads_call(): pl.pallas_call(functools.partial(grads_kernel, tiles, half, first, last),...  36.9 us
    ppermute x8, starting transfers between devices, local(): over_x = lambda a: lax.ppermute(a, 'seq', [(i, i ^ 2) for i in range(4)])  13.4 us
    pallas_call x3, Pallas kernels, move(): pl.pallas_call(functools.partial(move_kernel, tuple(moves), len(ins)), ou...  11.9 us
    ppermute x7, starting transfers between devices, local(): over_y = lambda a: lax.ppermute(a, 'groups', [(0, 1), (1, 0)])  11.8 us
    ppermute x4, starting transfers between devices, local(): lax.ppermute(a, 'tensor', [(i, i ^ k) for i in range(4)])  8.4 us
    dot_general x2, matrix products, local(): jnp.dot(a, spread, preferred_element_type=F32).astype(BF16)  5.95 us
    ppermute x7, waiting for transfers between devices, local(): over_y = lambda a: lax.ppermute(a, 'groups', [(0, 1), (1, 0)])  5.03 us
  transfers between devices with their start and end apart: 26, of which 12 were waited for; matrix products, arithmetic and copies ran while one was open for 10% of the time, Pallas kernels for 9%

profile of v3, /device:TPU:0, one launch (start us, length us, event | category | flops | bytes accessed | tf_op | source)
XLA Modules:
  0.0 175.1 jit_solution(12766426367889576951)
XLA Ops:
  7.9 2.5 %shard_map.101 = bf16[256,1024]{1,0:T(8,128)(2,1)} custom-call(s32[3]{0:T(128)} %pad_add_fusion.refs_0_, bf16[2,1792,1024]{2,1,0:T(8,128)(2,1)} %bitcast.31), custom_call_target="tpu_custom_call" | custom-call | bytes 1048576 | tf_op jit(solution)/shard_map/pallas_call | solution.py:110
  10.5 3.0 %collective-permute-start = (bf16[256,1024]{1,0:T(8,128)(2,1)}, bf16[256,1024]{1,0:T(8,128)(2,1)S(1)}, u32[]{:S(2)}, u32[]{:S(2)}) collective-permute-start(bf16[256,1024]{1,0:T(8,128)(2,1)} %shard_map.101), channel_id=1, source_target_pairs={{0,8},{4,12},{8,0},{12,4},{1,9},{5,13},{9,1},{13,5},{2,10},{6,14},... | collective-permute-start | bytes 1572872 | tf_op jit(solution)/shard_map/ppermute | solution.py:304
  13.5 3.5 %shard_map.100 = (bf16[256,1024]{1,0:T(8,128)(2,1)}, bf16[256,1024]{1,0:T(8,128)(2,1)}, bf16[256,1024]{1,0:T(8,128)(2,1)}, bf16[256,1024]{1,0:T(8,128)(2,1)}, bf...) custom-call(s32[3]{0:T(128)} %pad_add_fusion.refs_0_, bf16[2,1792,1024]{2,1,0:T(8,128)(2,1)} %bitcast.32), custom_call_target="tpu_custom_call" | custom-call | bytes 6291456 | tf_op jit(solution)/shard_map/pallas_call | solution.py:110
  18.6 7.8 %collective-permute-done.refs_4_ = bf16[256,1024]{1,0:T(8,128)(2,1)S(1)} collective-permute-done((bf16[256,1024]{1,0:T(8,128)(2,1)}, bf16[256,1024]{1,0:T(8,128)(2,1)S(1)}, u32[]{:S(2)}, u32[]{:S(2)}) %collective-permute-start) | collective-permute-done | bytes 524320 | tf_op jit(solution)/shard_map/ppermute | solution.py:304
  26.5 2.1 %collective-permute-start.4 = (bf16[256,1024]{1,0:T(8,128)(2,1)S(1)}, bf16[256,1024]{1,0:T(8,128)(2,1)}, u32[]{:S(2)}, u32[]{:S(2)}) collective-permute-start(bf16[256,1024]{1,0:T(8,128)(2,1)S(1)} %collective-permute-done.refs_4_), channel_id=1, source_target_pairs={{0,16},{16,0},{1,17},{17,1},{2,18},{18,2},{3,19},{19,3},{4,20},{20... | collective-permute-start | bytes 1572872 | tf_op jit(solution)/shard_map/ppermute | solution.py:306
  30.1 7.8 %collective-permute-done.1.refs_1_ = bf16[256,1024]{1,0:T(8,128)(2,1)} collective-permute-done((bf16[256,1024]{1,0:T(8,128)(2,1)}, bf16[256,1024]{1,0:T(8,128)(2,1)}, u32[]{:S(2)}, u32[]{:S(2)}) %collective-permute-start.1) | collective-permute-done | bytes 524320 | tf_op jit(solution)/shard_map/ppermute | solution.py:304
  41.4 4.6 %fusion.5 = f32[512,64]{0,1:T(8,128)S(1)} fusion(bf16[512,3584]{1,0:T(8,128)(2,1)} %refs_9_.3, bf16[512,3584]{1,0:T(8,128)(2,1)} %refs_8_.3, bf16[3584,192]{0,1:T(8,128)(2,1)} %param.16), kind=kOutput, calls=%fused_computation.9 | convolution fusion | flops 249561088 | bytes 7929856 | tf_op jit(solution)/shard_map/dot_general | solution.py:396
  46.6 2.4 %collective-permute-done.3.refs_3_ = bf16[256,1024]{1,0:T(8,128)(2,1)} collective-permute-done((bf16[256,1024]{1,0:T(8,128)(2,1)}, bf16[256,1024]{1,0:T(8,128)(2,1)}, u32[]{:S(2)}, u32[]{:S(2)}) %collective-permute-start.3) | collective-permute-done | bytes 524320 | tf_op jit(solution)/shard_map/ppermute | solution.py:304
  53.5 6.8 %collective-permute-done.6.refs_5_ = bf16[256,1024]{1,0:T(8,128)(2,1)} collective-permute-done((bf16[256,1024]{1,0:T(8,128)(2,1)}, bf16[256,1024]{1,0:T(8,128)(2,1)}, u32[]{:S(2)}, u32[]{:S(2)}) %collective-permute-start.6) | collective-permute-done | bytes 524320 | tf_op jit(solution)/shard_map/ppermute | solution.py:304
  63.9 7.6 %collective-permute-done.8.refs_7_ = bf16[256,1024]{1,0:T(8,128)(2,1)} collective-permute-done((bf16[256,1024]{1,0:T(8,128)(2,1)}, bf16[256,1024]{1,0:T(8,128)(2,1)}, u32[]{:S(2)}, u32[]{:S(2)}) %collective-permute-start.8) | collective-permute-done | bytes 524320 | tf_op jit(solution)/shard_map/ppermute | solution.py:304
  75.1 7.6 %collective-permute-done.11.refs_9_ = bf16[256,1024]{1,0:T(8,128)(2,1)} collective-permute-done((bf16[256,1024]{1,0:T(8,128)(2,1)}, bf16[256,1024]{1,0:T(8,128)(2,1)}, u32[]{:S(2)}, u32[]{:S(2)}) %collective-permute-start.11) | collective-permute-done | bytes 524320 | tf_op jit(solution)/shard_map/ppermute | solution.py:304
  82.8 2.1 %collective-permute-start.16 = (bf16[256,1024]{1,0:T(8,128)(2,1)}, bf16[256,1024]{1,0:T(8,128)(2,1)}, u32[]{:S(2)}, u32[]{:S(2)}) collective-permute-start(bf16[256,1024]{1,0:T(8,128)(2,1)} %collective-permute-done.11.refs_9_), channel_id=1, source_target_pairs={{0,16},{16,0},{1,17},{17,1},{2,18},{18,2},{3,19},{19,3},{4,20},{20... | collective-permute-start | bytes 1572872 | tf_op jit(solution)/shard_map/ppermute | solution.py:306
  86.5 3.0 %convolution_convert_fusion.refs_11_ = bf16[3584,256]{1,0:T(8,128)(2,1)} fusion(bf16[3584,192]{0,1:T(8,128)(2,1)} %param.16, s32[256]{0:T(256)S(1)} %fusion.26), kind=kOutput, calls=%fused_computation.7 | convolution fusion | flops 118374400 | bytes 2294784 | tf_op jit(solution)/shard_map/dot_general | solution.py:332
  89.5 3.0 %convolution_convert_fusion.1.refs_10_ = bf16[3584,256]{1,0:T(8,128)(2,1)} fusion(bf16[3584,192]{0,1:T(8,128)(2,1)} %param.16, s32[256]{0:T(256)S(1)} %fusion.26), kind=kOutput, calls=%fused_computation.8 | convolution fusion | flops 118374400 | bytes 2294784 | tf_op jit(solution)/shard_map/dot_general | solution.py:332
  92.5 2.5 %fusion.8.refs_15_ = f32[512,256]{1,0:T(8,128)} fusion(bf16[512,1024]{1,0:T(8,128)(2,1)S(1)} %copy-done.1, bf16[4096,64]{0,1:T(8,128)(2,1)} %param.17, s32[]{:T(128)S(6)} %select_n.132, s32[256]{0:T(256)S(1)} %fusion.26), kind=kOutput, calls=%fused_computation.12 | convolution fusion | flops 302268416 | bytes 1704964 | tf_op jit(solution)/shard_map/dot_general | solution.py:407
  95.0 5.0 %collective-permute-done.16.refs_10_ = bf16[256,1024]{1,0:T(8,128)(2,1)} collective-permute-done((bf16[256,1024]{1,0:T(8,128)(2,1)}, bf16[256,1024]{1,0:T(8,128)(2,1)}, u32[]{:S(2)}, u32[]{:S(2)}) %collective-permute-start.16) | collective-permute-done | bytes 524320 | tf_op jit(solution)/shard_map/ppermute | solution.py:306
  100.0 5.9 %shard_map.102.refs_4_ = bf16[2816,1024]{1,0:T(8,128)(2,1)} custom-call(s32[3]{0:T(128)} %pad_add_fusion.refs_0_, bf16[256,1024]{1,0:T(8,128)(2,1)} %collective-permute-done.1.refs_1_, bf16[256,1024]{1,0:T(8,128)(2,1)} %collective-permute-done.7.refs_2_, bf16[256,1024]{1,0:T(8,128)(2,1)} %collective-permute-done.3.refs_3_, bf16[256,1024]{1,0:T(8,128)(2,1)} %copy-done.4, ...), custom_call_target="tpu_custom_call" | custom-call | bytes 11534336 | tf_op jit(solution)/shard_map/pallas_call | solution.py:110
  107.6 2.7 %collective-permute-start.19 = (bf16[192,512]{1,0:T(8,128)(2,1)S(1)}, bf16[192,512]{1,0:T(8,128)(2,1)S(1)}, u32[]{:S(2)}, u32[]{:S(2)}) collective-permute-start(bf16[192,512]{1,0:T(8,128)(2,1)S(1)} %fusion.12), channel_id=1, source_target_pairs={{0,2},{1,3},{2,0},{3,1},{4,6},{5,7},{6,4},{7,5},{8,10},{9,11},{10,... | collective-permute-start | bytes 589832 | tf_op jit(solution)/shard_map/ppermute | solution.py:307
  110.3 9.6 %shard_map.103 = (f32[512,256]{1,0:T(8,128)}, f32[512,256]{1,0:T(8,128)}) custom-call(s32[3]{0:T(128)} %pad_add_fusion.refs_0_, bf16[4,512,1024]{2,1,0:T(8,128)(2,1)} %bitcast.33, bf16[3584,1024]{1,0:T(8,128)(2,1)} %refs_2_.3, bf16[3584,1024]{1,0:T(8,128)(2,1)} %collective-permute-done.2.refs_3_, bf16[256,1024]{1,0:T(8,128)(2,1)} %copy-done.2, ...), custom_call_target="tpu_custom_call" | custom-call | flops 2415919104 | bytes 9437184 | tf_op jit(solution)/shard_map/pallas_call | solution.py:269
  123.4 27.3 %shard_map.104 = (f32[3,64,128]{2,1,0:T(8,128)}, f32[3,64,128]{2,1,0:T(8,128)}) custom-call(s32[3]{0:T(128)} %pad_add_fusion.refs_0_, bf16[4,512,1024]{2,1,0:T(8,128)(2,1)} %bitcast.34, bf16[3584,1024]{1,0:T(8,128)(2,1)} %refs_2_.3, bf16[3584,1024]{1,0:T(8,128)(2,1)} %collective-permute-done.2.refs_3_, bf16[2816,1024]{1,0:T(8,128)(2,1)} %shard_map.102.refs_4_, ...), custom_call_target="tpu_custom_call" | custom-call | flops 14495514624 | bytes 35651584 | tf_op jit(solution)/shard_map/pallas_call | solution.py:269
  154.2 4.3 %collective-permute-done.22 = f32[3,64,64]{2,1,0:T(8,128)S(1)} collective-permute-done((f32[3,64,64]{2,1,0:T(8,128)S(1)}, f32[3,64,64]{2,1,0:T(8,128)S(1)}, u32[]{:S(2)}, u32[]{:S(2)}) %collective-permute-start.22) | collective-permute-done | bytes 49184 | tf_op jit(solution)/shard_map/ppermute | solution.py:304
  158.5 2.5 %collective-permute-start.23 = (f32[3,32,64]{2,1,0:T(8,128)S(1)}, f32[3,32,64]{2,1,0:T(8,128)S(1)}, u32[]{:S(2)}, u32[]{:S(2)}) collective-permute-start(f32[3,32,64]{2,1,0:T(8,128)S(1)} %dynamic-slice_bitcast_fusion), channel_id=1, source_target_pairs={{0,2},{1,3},{2,0},{3,1},{4,6},{5,7},{6,4},{7,5},{8,10},{9,11},{10,... | collective-permute-start | bytes 73736 | tf_op jit(solution)/shard_map/ppermute | solution.py:307
  161.0 2.6 %collective-permute-done.23 = f32[3,32,64]{2,1,0:T(8,128)S(1)} collective-permute-done((f32[3,32,64]{2,1,0:T(8,128)S(1)}, f32[3,32,64]{2,1,0:T(8,128)S(1)}, u32[]{:S(2)}, u32[]{:S(2)}) %collective-permute-start.23) | collective-permute-done | bytes 24608 | tf_op jit(solution)/shard_map/ppermute | solution.py:307
  165.3 2.3 %collective-permute-done.24 = f32[3,16,64]{2,1,0:T(8,128)S(1)} collective-permute-done((f32[3,16,64]{2,1,0:T(8,128)S(1)}, f32[3,16,64]{2,1,0:T(8,128)S(1)}, u32[]{:S(2)}, u32[]{:S(2)}) %collective-permute-start.24) | collective-permute-done | bytes 12320 | tf_op jit(solution)/shard_map/ppermute | solution.py:307
  (81 shorter events, 32.9 us)
Async XLA Ops:
  6.5 88.4 %all-gather.3.cloned.1.call-start = ((), (), s32[]{:S(2)}) async-start(), calls=%async_computation | async-start | bytes 5242880 | tf_op jit(solution)/shard_map/all_gather | solution.py:321
  6.5 31.3 %collective-permute-start.2 = (bf16[3584,1024]{1,0:T(8,128)(2,1)}, bf16[3584,1024]{1,0:T(8,128)(2,1)}, u32[]{:S(2)}, u32[]{:S(2)}) collective-permute-start(bf16[3584,1024]{1,0:T(8,128)(2,1)} %refs_2_.3), channel_id=1, source_target_pairs={{0,4},{4,0},{8,12},{12,8},{1,5},{5,1},{9,13},{13,9},{2,6},{6,2},{1... | collective-permute-start | bytes 22020104 | tf_op jit(solution)/shard_map/ppermute | solution.py:305
  10.5 16.0 %collective-permute-start = (bf16[256,1024]{1,0:T(8,128)(2,1)}, bf16[256,1024]{1,0:T(8,128)(2,1)S(1)}, u32[]{:S(2)}, u32[]{:S(2)}) collective-permute-start(bf16[256,1024]{1,0:T(8,128)(2,1)} %shard_map.101), channel_id=1, source_target_pairs={{0,8},{4,12},{8,0},{12,4},{1,9},{5,13},{9,1},{13,5},{2,10},{6,14},... | collective-permute-start | bytes 1572872 | tf_op jit(solution)/shard_map/ppermute | solution.py:304
  17.0 20.8 %collective-permute-start.1 = (bf16[256,1024]{1,0:T(8,128)(2,1)}, bf16[256,1024]{1,0:T(8,128)(2,1)}, u32[]{:S(2)}, u32[]{:S(2)}) collective-permute-start(bf16[256,1024]{1,0:T(8,128)(2,1)} %get-tuple-element.85), channel_id=1, source_target_pairs={{0,8},{4,12},{8,0},{12,4},{1,9},{5,13},{9,1},{13,5},{2,10},{6,14},... | collective-permute-start | bytes 1572872 | tf_op jit(solution)/shard_map/ppermute | solution.py:304
  26.5 20.1 %collective-permute-start.4 = (bf16[256,1024]{1,0:T(8,128)(2,1)S(1)}, bf16[256,1024]{1,0:T(8,128)(2,1)}, u32[]{:S(2)}, u32[]{:S(2)}) collective-permute-start(bf16[256,1024]{1,0:T(8,128)(2,1)S(1)} %collective-permute-done.refs_4_), channel_id=1, source_target_pairs={{0,16},{16,0},{1,17},{17,1},{2,18},{18,2},{3,19},{19,3},{4,20},{20... | collective-permute-start | bytes 1572872 | tf_op jit(solution)/shard_map/ppermute | solution.py:306
  28.6 22.5 %collective-permute-start.5 = (bf16[256,1024]{1,0:T(8,128)(2,1)S(1)}, bf16[256,1024]{1,0:T(8,128)(2,1)S(1)}, u32[]{:S(2)}, u32[]{:S(2)}) collective-permute-start(bf16[256,1024]{1,0:T(8,128)(2,1)S(1)} %collective-permute-done.refs_4_), channel_id=1, source_target_pairs={{0,4},{4,0},{8,12},{12,8},{1,5},{5,1},{9,13},{13,9},{2,6},{6,2},{1... | collective-permute-start | bytes 1572872 | tf_op jit(solution)/shard_map/ppermute | solution.py:305
  28.6 20.5 %collective-permute-start.3 = (bf16[256,1024]{1,0:T(8,128)(2,1)}, bf16[256,1024]{1,0:T(8,128)(2,1)}, u32[]{:S(2)}, u32[]{:S(2)}) collective-permute-start(bf16[256,1024]{1,0:T(8,128)(2,1)} %get-tuple-element.93), channel_id=1, source_target_pairs={{0,8},{4,12},{8,0},{12,4},{1,9},{5,13},{9,1},{13,5},{2,10},{6,14},... | collective-permute-start | bytes 1572872 | tf_op jit(solution)/shard_map/ppermute | solution.py:304
  37.8 22.5 %collective-permute-start.6 = (bf16[256,1024]{1,0:T(8,128)(2,1)}, bf16[256,1024]{1,0:T(8,128)(2,1)}, u32[]{:S(2)}, u32[]{:S(2)}) collective-permute-start(bf16[256,1024]{1,0:T(8,128)(2,1)} %get-tuple-element.98), channel_id=1, source_target_pairs={{0,8},{4,12},{8,0},{12,4},{1,9},{5,13},{9,1},{13,5},{2,10},{6,14},... | collective-permute-start | bytes 1572872 | tf_op jit(solution)/shard_map/ppermute | solution.py:304
  39.9 20.4 %collective-permute-start.7 = (bf16[256,1024]{1,0:T(8,128)(2,1)}, bf16[256,1024]{1,0:T(8,128)(2,1)}, u32[]{:S(2)}, u32[]{:S(2)}) collective-permute-start(bf16[256,1024]{1,0:T(8,128)(2,1)} %collective-permute-done.1.refs_1_), channel_id=1, source_target_pairs={{0,16},{16,0},{1,17},{17,1},{2,18},{18,2},{3,19},{19,3},{4,20},{20... | collective-permute-start | bytes 1572872 | tf_op jit(solution)/shard_map/ppermute | solution.py:306
  49.0 26.1 %collective-permute-start.10 = (bf16[256,1024]{1,0:T(8,128)(2,1)}, bf16[256,1024]{1,0:T(8,128)(2,1)}, u32[]{:S(2)}, u32[]{:S(2)}) collective-permute-start(bf16[256,1024]{1,0:T(8,128)(2,1)} %collective-permute-done.4.refs_6_), channel_id=1, source_target_pairs={{0,4},{4,0},{8,12},{12,8},{1,5},{5,1},{9,13},{13,9},{2,6},{6,2},{1... | collective-permute-start | bytes 1572872 | tf_op jit(solution)/shard_map/ppermute | solution.py:305
  49.0 22.5 %collective-permute-start.8 = (bf16[256,1024]{1,0:T(8,128)(2,1)}, bf16[256,1024]{1,0:T(8,128)(2,1)}, u32[]{:S(2)}, u32[]{:S(2)}) collective-permute-start(bf16[256,1024]{1,0:T(8,128)(2,1)} %get-tuple-element.101), channel_id=1, source_target_pairs={{0,8},{4,12},{8,0},{12,4},{1,9},{5,13},{9,1},{13,5},{2,10},{6,14},... | collective-permute-start | bytes 1572872 | tf_op jit(solution)/shard_map/ppermute | solution.py:304
  51.9 19.6 %collective-permute-start.9 = (bf16[256,1024]{1,0:T(8,128)(2,1)}, bf16[256,1024]{1,0:T(8,128)(2,1)S(1)}, u32[]{:S(2)}, u32[]{:S(2)}) collective-permute-start(bf16[256,1024]{1,0:T(8,128)(2,1)} %collective-permute-done.3.refs_3_), channel_id=1, source_target_pairs={{0,16},{16,0},{1,17},{17,1},{2,18},{18,2},{3,19},{19,3},{4,20},{20... | collective-permute-start | bytes 1572872 | tf_op jit(solution)/shard_map/ppermute | solution.py:306
  60.3 22.5 %collective-permute-start.11 = (bf16[256,1024]{1,0:T(8,128)(2,1)}, bf16[256,1024]{1,0:T(8,128)(2,1)}, u32[]{:S(2)}, u32[]{:S(2)}) collective-permute-start(bf16[256,1024]{1,0:T(8,128)(2,1)} %get-tuple-element.104), channel_id=1, source_target_pairs={{0,8},{4,12},{8,0},{12,4},{1,9},{5,13},{9,1},{13,5},{2,10},{6,14},... | collective-permute-start | bytes 1572872 | tf_op jit(solution)/shard_map/ppermute | solution.py:304
  62.3 20.4 %collective-permute-start.12 = (bf16[256,1024]{1,0:T(8,128)(2,1)}, bf16[256,1024]{1,0:T(8,128)(2,1)}, u32[]{:S(2)}, u32[]{:S(2)}) collective-permute-start(bf16[256,1024]{1,0:T(8,128)(2,1)} %collective-permute-done.6.refs_5_), channel_id=1, source_target_pairs={{0,16},{16,0},{1,17},{17,1},{2,18},{18,2},{3,19},{19,3},{4,20},{20... | collective-permute-start | bytes 1572872 | tf_op jit(solution)/shard_map/ppermute | solution.py:306
  71.5 23.5 %collective-permute-start.14 = (bf16[256,1024]{1,0:T(8,128)(2,1)}, bf16[256,1024]{1,0:T(8,128)(2,1)}, u32[]{:S(2)}, u32[]{:S(2)}) collective-permute-start(bf16[256,1024]{1,0:T(8,128)(2,1)} %get-tuple-element.111), channel_id=1, source_target_pairs={{0,8},{4,12},{8,0},{12,4},{1,9},{5,13},{9,1},{13,5},{2,10},{6,14},... | collective-permute-start | bytes 1572872 | tf_op jit(solution)/shard_map/ppermute | solution.py:304
  73.6 21.4 %collective-permute-start.15 = (bf16[256,1024]{1,0:T(8,128)(2,1)}, bf16[256,1024]{1,0:T(8,128)(2,1)}, u32[]{:S(2)}, u32[]{:S(2)}) collective-permute-start(bf16[256,1024]{1,0:T(8,128)(2,1)} %collective-permute-done.8.refs_7_), channel_id=1, source_target_pairs={{0,16},{16,0},{1,17},{17,1},{2,18},{18,2},{3,19},{19,3},{4,20},{20... | collective-permute-start | bytes 1572872 | tf_op jit(solution)/shard_map/ppermute | solution.py:306
  82.8 17.3 %collective-permute-start.16 = (bf16[256,1024]{1,0:T(8,128)(2,1)}, bf16[256,1024]{1,0:T(8,128)(2,1)}, u32[]{:S(2)}, u32[]{:S(2)}) collective-permute-start(bf16[256,1024]{1,0:T(8,128)(2,1)} %collective-permute-done.11.refs_9_), channel_id=1, source_target_pairs={{0,16},{16,0},{1,17},{17,1},{2,18},{18,2},{3,19},{19,3},{4,20},{20... | collective-permute-start | bytes 1572872 | tf_op jit(solution)/shard_map/ppermute | solution.py:306
  84.9 10.1 %collective-permute-start.13 = (bf16[192,512]{1,0:T(8,128)(2,1)S(1)}, bf16[192,512]{1,0:T(8,128)(2,1)S(1)}, u32[]{:S(2)}, u32[]{:S(2)}) collective-permute-start(bf16[192,512]{1,0:T(8,128)(2,1)S(1)} %convert_element_type.38), channel_id=1, source_target_pairs={{0,1},{1,0},{2,3},{3,2},{4,5},{5,4},{6,7},{7,6},{8,9},{9,8},{10,11... | collective-permute-start | bytes 589832 | tf_op jit(solution)/shard_map/ppermute | solution.py:307
  105.9 16.7 %collective-permute-start.17 = (bf16[2816,1024]{1,0:T(8,128)(2,1)}, bf16[2816,1024]{1,0:T(8,128)(2,1)}, u32[]{:S(2)}, u32[]{:S(2)}) collective-permute-start(bf16[2816,1024]{1,0:T(8,128)(2,1)} %shard_map.102.refs_4_), channel_id=1, source_target_pairs={{0,4},{4,0},{8,12},{12,8},{1,5},{5,1},{9,13},{13,9},{2,6},{6,2},{1... | collective-permute-start | bytes 17301512 | tf_op jit(solution)/shard_map/ppermute | solution.py:305
  106.0 14.7 %collective-permute-start.18 = (bf16[256,1024]{1,0:T(8,128)(2,1)}, bf16[256,1024]{1,0:T(8,128)(2,1)S(1)}, u32[]{:S(2)}, u32[]{:S(2)}) collective-permute-start(bf16[256,1024]{1,0:T(8,128)(2,1)} %collective-permute-done.14.refs_11_), channel_id=1, source_target_pairs={{0,16},{16,0},{1,17},{17,1},{2,18},{18,2},{3,19},{19,3},{4,20},{20... | collective-permute-start | bytes 1572872 | tf_op jit(solution)/shard_map/ppermute | solution.py:306
  107.6 12.3 %collective-permute-start.19 = (bf16[192,512]{1,0:T(8,128)(2,1)S(1)}, bf16[192,512]{1,0:T(8,128)(2,1)S(1)}, u32[]{:S(2)}, u32[]{:S(2)}) collective-permute-start(bf16[192,512]{1,0:T(8,128)(2,1)S(1)} %fusion.12), channel_id=1, source_target_pairs={{0,2},{1,3},{2,0},{3,1},{4,6},{5,7},{6,4},{7,5},{8,10},{9,11},{10,... | collective-permute-start | bytes 589832 | tf_op jit(solution)/shard_map/ppermute | solution.py:307
  153.6 4.9 %collective-permute-start.22 = (f32[3,64,64]{2,1,0:T(8,128)S(1)}, f32[3,64,64]{2,1,0:T(8,128)S(1)}, u32[]{:S(2)}, u32[]{:S(2)}) collective-permute-start(f32[3,64,64]{2,1,0:T(8,128)S(1)} %bitcast.41), channel_id=1, source_target_pairs={{0,8},{4,12},{8,0},{12,4},{1,9},{5,13},{9,1},{13,5},{2,10},{6,14},... | collective-permute-start | bytes 147464 | tf_op jit(solution)/shard_map/ppermute | solution.py:304
  158.5 5.1 %collective-permute-start.23 = (f32[3,32,64]{2,1,0:T(8,128)S(1)}, f32[3,32,64]{2,1,0:T(8,128)S(1)}, u32[]{:S(2)}, u32[]{:S(2)}) collective-permute-start(f32[3,32,64]{2,1,0:T(8,128)S(1)} %dynamic-slice_bitcast_fusion), channel_id=1, source_target_pairs={{0,2},{1,3},{2,0},{3,1},{4,6},{5,7},{6,4},{7,5},{8,10},{9,11},{10,... | collective-permute-start | bytes 73736 | tf_op jit(solution)/shard_map/ppermute | solution.py:307
  163.6 3.9 %collective-permute-start.24 = (f32[3,16,64]{2,1,0:T(8,128)S(1)}, f32[3,16,64]{2,1,0:T(8,128)S(1)}, u32[]{:S(2)}, u32[]{:S(2)}) collective-permute-start(f32[3,16,64]{2,1,0:T(8,128)S(1)} %dynamic-slice_bitcast_fusion.1), channel_id=1, source_target_pairs={{0,1},{1,0},{2,3},{3,2},{4,5},{5,4},{6,7},{7,6},{8,9},{9,8},{10,11... | collective-permute-start | bytes 36872 | tf_op jit(solution)/shard_map/ppermute | solution.py:307
  (12 other events, 174.0 us)
Sparse Core Ops, SparseCore 0:
  8.9 83.5 all-gather.2

commit v4 on v3

--- a/solution.py
+++ b/solution.py
@@ -85,7 +85,8 @@
     outs, (buf, sem) = refs[:-2], refs[-2:]
     y, at, steps = scal[2], 0, []
     for i, (src, lead, row, dst, to, rows) in enumerate(moves):
-        a = ins[src].at[y, pl.ds(row, rows)] if lead else ins[src].at[pl.ds(row, rows)]
+        a = ins[src] if lead is None else ins[src].at[y if lead == "y" else lead]
+        a = a.at[pl.ds(row, rows)]
         mid = buf.at[pl.ds(at, rows)]
         steps.append(
             (
@@ -126,7 +127,7 @@
 def join(scal, pieces):
     moves, at = [], 0
     for i, piece in enumerate(pieces):
-        moves.append((i, False, 0, 0, at, piece.shape[0]))
+        moves.append((i, None, 0, 0, at, piece.shape[0]))
         at += piece.shape[0]
     return move(scal, pieces, moves, [at])[0]
 
@@ -157,7 +158,7 @@
 
             @pl.when(t == i)
             def _(pair=pair, row=row, off=off, mine=mine, i=i):
-                h = y if mine else 1 - y
+                h = (y, 1 - y, 0, 1)[mine]
                 at = pl.multiple_of(h * half + off, 128)
                 rows = pl.ds(at, TILE)
                 here = pl.ds(row, TILE)
@@ -308,19 +309,21 @@
 
     count = len(CHUNKS)
     offs = [sum(CHUNKS[:k]) for k in range(count)]
-    r, ry = [None] * count, [None] * count
+    r, ry = [None] * (count + 1), [None] * count
     tie = lax.optimization_barrier
     halves = w_down.reshape(2, half, depth)
-    cut = lambda ks: move(
+    whole = count - 1
+    sources = [("y", k) for k in range(whole)] + [(0, whole), (1, whole)]
+    cut = lambda picks: move(
         scal,
         [halves],
-        [(0, True, offs[k], i, 0, CHUNKS[k]) for i, k in enumerate(ks)],
-        [CHUNKS[k] for k in ks],
+        [(0, h, offs[k], i, 0, CHUNKS[k]) for i, (h, k) in enumerate(picks)],
+        [CHUNKS[k] for _, k in picks],
     )
 
     gathered = lax.all_gather(out_grad, "tensor", axis=0, tiled=False)
-    r[0] = over_x(cut([0])[0])
-    srcs = [None] + list(cut(range(1, count)))
+    r[0] = over_x(cut(sources[:1])[0])
+    srcs = [None] + list(cut(sources[1:]))
     now = srcs[2:]
     r[1] = over_x(srcs[1])
     w_sib = over_c(w_down)
@@ -337,26 +340,24 @@
     scale = by_lane(lax.rsqrt(lengths.astype(F32)))
 
     swap_after = {
-        1: (((0, 0),),),
-        3: (((0, 1),),),
-        6: (
-            (
-                (1, 0), (1, 1), (2, 0), (2, 1), (3, 0), (3, 1), (4, 0), (4, 1), (5, 0), (5, 1), (6, 0),
-            ),
-        ),
+        0: ((0, 0),),
+        2: ((0, 1),),
+        4: ((1, 0),),
+        5: ((1, 1), (2, 0), (2, 1), (3, 0), (3, 1), (4, 0)),
+        6: ((4, 1), (5, 0), (5, 1), (6, 0)),
     }
-    swapped_by = {3: 0, 5: 1}
+    swapped_by = {2: 0, 4: 1, 6: 2}
     pairs, where = [], {}
 
-    def swap(members):
+    def swap(members, across=True):
         rows = 0
         for k, far in members:
-            for row in range(0, CHUNKS[k], TILE):
+            for row in range(0, CHUNKS[min(k, whole)], TILE):
                 where[(k, far, row)] = (len(pairs), rows)
                 rows += TILE
         got = [ry[k] if far else r[k] for k, far in members]
         got = got[0] if len(got) == 1 else join(scal, got)
-        pairs.append((got, over_c(got)))
+        pairs.append((got, over_c(got)) if across else got)
 
     for k in range(count):
         final = k == count - 1
@@ -377,17 +378,18 @@
             gate["y"] = ry[k - 2]
         if final:
             gate["y5"], gate["all"] = ry[k - 1], gathered
-            gate["hold"] = r[1:k], ry[1 : k - 2]
+            gate["join"] = pairs[3]
         gate = tie(gate)
         now, r[k] = gate["now"], gate["r"]
-        if k + 2 < count:
+        if k + 2 <= count:
             r[k + 2] = over_x(now[0])
             now = now[1:]
         if k >= 2:
             ry[k - 2] = gate["y"]
         if k == 1:
             w_sib = gate["sib"]
-        ry[k] = over_y(r[k])
+        if not final:
+            ry[k] = over_y(r[k])
         if k == 0:
             tokens_in, gates, uppers = gate["left"]
             activated, _ = silu_pair(gates.astype(F32))
@@ -411,30 +413,33 @@
             left_t = gate["left"][0] + gate["left"][1].astype(F32)
             left_t = left_t + over_z(left_t.astype(BF16), 2).astype(F32)
             ry[k - 1], gathered = gate["y5"], gate["all"]
-            r[1:k], ry[1 : k - 2] = gate["hold"]
         if k in swapped_by:
             pairs[swapped_by[k]] = gate["c"]
-        for members in swap_after.get(k, ()):
-            swap(members)
+        if final:
+            pairs[3] = (gate["join"], over_c(gate["join"]))
+        if k in swap_after:
+            swap(swap_after[k], k != 5)
 
     def grads(members, acc, tail=None):
         used, tiles = [], []
         for k, far in members:
-            for row in range(0, CHUNKS[k], TILE):
+            at_half = min(k, whole)
+            for row in range(0, CHUNKS[at_half], TILE):
                 pair, at = where[(k, far, row)]
                 if pair not in used:
                     used.append(pair)
-                tiles.append((used.index(pair), at, offs[k] + row, not far))
+                half_of = far if k < whole else 2 + k - whole
+                tiles.append((used.index(pair), at, offs[at_half] + row, half_of))
         return grads_call(
             tuple(tiles), half, scal, gathered, (w_down, w_sib), [pairs[p] for p in used],
             (gate_pre, up_pre, pg, pu), acc, tail,
         )
 
-    early, late = ((0, 0), (0, 1)), swap_after[6][0]
+    early, late = ((0, 0), (0, 1), (1, 0)), swap_after[5] + swap_after[6]
     acc = grads(early, None)
-    ry[6], left_t, acc = tie((ry[6], left_t, acc))
-    swap(((6, 1),))
-    acc = grads(late + ((6, 1),), acc, (left_t, r_down, lo, hi, scale))
+    r[7], left_t, acc = tie((r[7], left_t, acc))
+    swap(((7, 0),))
+    acc = grads(late + ((7, 0),), acc, (left_t, r_down, lo, hi, scale))
     keep, send = acc
     x = s // 2
     total = (keep + over_c(send)).reshape(3, 64, 2, 64)

time: 176 us -> 171 us (0.972)
  waiting for transfers between devices: 57.9 us -> 54.6 us
    ppermute x7 -> x6, waiting for transfers between devices: 5.03 us -> 0.59 us  [local(): over_y = lambda a: lax.ppermute(a, 'groups', [(0, 1), (1, 0)])]
    ppermute x8 -> x9, starting transfers between devices: 13.4 us -> 15 us  [local(): over_x = lambda a: lax.ppermute(a, 'seq', [(i, i ^ 2) for i in range(4)])]
    ppermute x7 -> x6, starting transfers between devices: 11.8 us -> 10.3 us  [local(): over_y = lambda a: lax.ppermute(a, 'groups', [(0, 1), (1, 0)])]
    pallas_call x3 -> x4, Pallas kernels: 11.9 us -> 12.8 us  [move(): pl.pallas_call(functools.partial(move_kernel, tuple(moves), len(ins)), ou...]
    ppermute x8 -> x9, waiting for transfers between devices: 44.4 us -> 44.5 us  [local(): over_x = lambda a: lax.ppermute(a, 'seq', [(i, i ^ 2) for i in range(4)])]
  transfers between devices with their start and end apart: 26 -> 28, of which waited for: 12 -> 12; matrix products, arithmetic and copies ran while one was open for 10% -> 10% of each run, Pallas kernels for 9% -> 14%
where the time goes in v4:
time: 171 us; the launch traced here: 170 us
  waiting for transfers between devices  54.6 us (32%)
  Pallas kernels  48.6 us (28%)
  starting transfers between devices  33.7 us (20%)
  matrix products  13.7 us (8%)
  between operations  13.7 us (8%)
  other arithmetic  3.98 us (2%)
  local copies, waits for them, and re-layouts  1.96 us (1%)
    ppermute x9, waiting for transfers between devices, local(): over_x = lambda a: lax.ppermute(a, 'seq', [(i, i ^ 2) for i in range(4)])  44.5 us
    pallas_call x2, Pallas kernels, grads_call(): pl.pallas_call(functools.partial(grads_kernel, tiles, half, first, last),...  35.9 us
    ppermute x9, starting transfers between devices, local(): over_x = lambda a: lax.ppermute(a, 'seq', [(i, i ^ 2) for i in range(4)])  15 us
    pallas_call x4, Pallas kernels, move(): pl.pallas_call(functools.partial(move_kernel, tuple(moves), len(ins)), ou...  12.8 us
    ppermute x6, starting transfers between devices, local(): over_y = lambda a: lax.ppermute(a, 'groups', [(0, 1), (1, 0)])  10.3 us
    ppermute x4, starting transfers between devices, local(): lax.ppermute(a, 'tensor', [(i, i ^ k) for i in range(4)])  7.19 us
    dot_general x2, matrix products, local(): jnp.dot(a, spread, preferred_element_type=F32).astype(BF16)  6.04 us
    ppermute x4, waiting for transfers between devices, local(): lax.ppermute(a, 'tensor', [(i, i ^ k) for i in range(4)])  6.03 us
  transfers between devices with their start and end apart: 28, of which 12 were waited for; matrix products, arithmetic and copies ran while one was open for 10% of the time, Pallas kernels for 14%

profile of v4, /device:TPU:0, one launch (start us, length us, event | category | flops | bytes accessed | tf_op | source)
XLA Modules:
  0.0 170.4 jit_solution(13692482632409599014)
XLA Ops:
  7.9 2.5 %shard_map.101 = bf16[256,1024]{1,0:T(8,128)(2,1)} custom-call(s32[3]{0:T(128)} %pad_add_fusion.refs_0_, bf16[2,1792,1024]{2,1,0:T(8,128)(2,1)} %bitcast.31), custom_call_target="tpu_custom_call" | custom-call | bytes 1048576 | tf_op jit(solution)/shard_map/pallas_call | solution.py:111
  10.4 3.0 %collective-permute-start = (bf16[256,1024]{1,0:T(8,128)(2,1)}, bf16[256,1024]{1,0:T(8,128)(2,1)S(1)}, u32[]{:S(2)}, u32[]{:S(2)}) collective-permute-start(bf16[256,1024]{1,0:T(8,128)(2,1)} %shard_map.101), channel_id=1, source_target_pairs={{0,8},{4,12},{8,0},{12,4},{1,9},{5,13},{9,1},{13,5},{2,10},{6,14},... | collective-permute-start | bytes 1572872 | tf_op jit(solution)/shard_map/ppermute | solution.py:305
  13.4 3.7 %shard_map.100 = (bf16[256,1024]{1,0:T(8,128)(2,1)}, bf16[256,1024]{1,0:T(8,128)(2,1)}, bf16[256,1024]{1,0:T(8,128)(2,1)}, bf16[256,1024]{1,0:T(8,128)(2,1)}, bf...) custom-call(s32[3]{0:T(128)} %pad_add_fusion.refs_0_, bf16[2,1792,1024]{2,1,0:T(8,128)(2,1)} %bitcast.32), custom_call_target="tpu_custom_call" | custom-call | bytes 7340032 | tf_op jit(solution)/shard_map/pallas_call | solution.py:111
  18.7 7.7 %collective-permute-done.refs_4_ = bf16[256,1024]{1,0:T(8,128)(2,1)S(1)} collective-permute-done((bf16[256,1024]{1,0:T(8,128)(2,1)}, bf16[256,1024]{1,0:T(8,128)(2,1)S(1)}, u32[]{:S(2)}, u32[]{:S(2)}) %collective-permute-start) | collective-permute-done | bytes 524320 | tf_op jit(solution)/shard_map/ppermute | solution.py:305
  26.4 2.1 %collective-permute-start.6 = (bf16[256,1024]{1,0:T(8,128)(2,1)S(1)}, bf16[256,1024]{1,0:T(8,128)(2,1)S(1)}, u32[]{:S(2)}, u32[]{:S(2)}) collective-permute-start(bf16[256,1024]{1,0:T(8,128)(2,1)S(1)} %collective-permute-done.refs_4_), channel_id=1, source_target_pairs={{0,16},{16,0},{1,17},{17,1},{2,18},{18,2},{3,19},{19,3},{4,20},{20... | collective-permute-start | bytes 1572872 | tf_op jit(solution)/shard_map/ppermute | solution.py:307
  30.1 7.7 %collective-permute-done.1.refs_8_ = bf16[256,1024]{1,0:T(8,128)(2,1)} collective-permute-done((bf16[256,1024]{1,0:T(8,128)(2,1)}, bf16[256,1024]{1,0:T(8,128)(2,1)}, u32[]{:S(2)}, u32[]{:S(2)}) %collective-permute-start.1) | collective-permute-done | bytes 524320 | tf_op jit(solution)/shard_map/ppermute | solution.py:305
  41.3 4.6 %fusion.5 = f32[512,64]{0,1:T(8,128)S(1)} fusion(bf16[512,3584]{1,0:T(8,128)(2,1)} %refs_11_.3, bf16[512,3584]{1,0:T(8,128)(2,1)} %refs_10_.3, bf16[3584,192]{0,1:T(8,128)(2,1)} %param.16), kind=kOutput, calls=%fused_computation.9 | convolution fusion | flops 249561088 | bytes 7929856 | tf_op jit(solution)/shard_map/dot_general | solution.py:398
  46.6 2.4 %collective-permute-done.5.refs_2_ = bf16[256,1024]{1,0:T(8,128)(2,1)} collective-permute-done((bf16[256,1024]{1,0:T(8,128)(2,1)}, bf16[256,1024]{1,0:T(8,128)(2,1)}, u32[]{:S(2)}, u32[]{:S(2)}) %collective-permute-start.5) | collective-permute-done | bytes 524320 | tf_op jit(solution)/shard_map/ppermute | solution.py:305
  52.6 7.7 %collective-permute-done.7.refs_4_ = bf16[256,1024]{1,0:T(8,128)(2,1)} collective-permute-done((bf16[256,1024]{1,0:T(8,128)(2,1)}, bf16[256,1024]{1,0:T(8,128)(2,1)}, u32[]{:S(2)}, u32[]{:S(2)}) %collective-permute-start.7) | collective-permute-done | bytes 524320 | tf_op jit(solution)/shard_map/ppermute | solution.py:305
  63.8 7.6 %collective-permute-done.10.refs_6_ = bf16[256,1024]{1,0:T(8,128)(2,1)} collective-permute-done((bf16[256,1024]{1,0:T(8,128)(2,1)}, bf16[256,1024]{1,0:T(8,128)(2,1)}, u32[]{:S(2)}, u32[]{:S(2)}) %collective-permute-start.10) | collective-permute-done | bytes 524320 | tf_op jit(solution)/shard_map/ppermute | solution.py:305
  71.5 2.1 %collective-permute-start.15 = (bf16[256,1024]{1,0:T(8,128)(2,1)}, bf16[256,1024]{1,0:T(8,128)(2,1)}, u32[]{:S(2)}, u32[]{:S(2)}) collective-permute-start(bf16[256,1024]{1,0:T(8,128)(2,1)} %get-tuple-element.118), channel_id=1, source_target_pairs={{0,8},{4,12},{8,0},{12,4},{1,9},{5,13},{9,1},{13,5},{2,10},{6,14},... | collective-permute-start | bytes 1572872 | tf_op jit(solution)/shard_map/ppermute | solution.py:305
  75.1 7.6 %collective-permute-done.12.refs_2_ = bf16[256,1024]{1,0:T(8,128)(2,1)} collective-permute-done((bf16[256,1024]{1,0:T(8,128)(2,1)}, bf16[256,1024]{1,0:T(8,128)(2,1)}, u32[]{:S(2)}, u32[]{:S(2)}) %collective-permute-start.12) | collective-permute-done | bytes 524320 | tf_op jit(solution)/shard_map/ppermute | solution.py:305
  82.7 2.1 %collective-permute-start.17 = (bf16[256,1024]{1,0:T(8,128)(2,1)}, bf16[256,1024]{1,0:T(8,128)(2,1)}, u32[]{:S(2)}, u32[]{:S(2)}) collective-permute-start(bf16[256,1024]{1,0:T(8,128)(2,1)} %collective-permute-done.12.refs_2_), channel_id=1, source_target_pairs={{0,16},{16,0},{1,17},{17,1},{2,18},{18,2},{3,19},{19,3},{4,20},{20... | collective-permute-start | bytes 1572872 | tf_op jit(solution)/shard_map/ppermute | solution.py:307
  86.5 3.5 %shard_map.102.refs_4_ = bf16[1536,1024]{1,0:T(8,128)(2,1)} custom-call(s32[3]{0:T(128)} %pad_add_fusion.refs_0_, bf16[256,1024]{1,0:T(8,128)(2,1)} %collective-permute-done.8.refs_1_, bf16[256,1024]{1,0:T(8,128)(2,1)} %collective-permute-done.5.refs_2_, bf16[256,1024]{1,0:T(8,128)(2,1)} %collective-permute-done.11.refs_3_, ...), custom_call_target="tpu_custom_call" | custom-call | bytes 6291456 | tf_op jit(solution)/shard_map/pallas_call | solution.py:111
  90.0 3.1 %convolution_convert_fusion.refs_13_ = bf16[3584,256]{1,0:T(8,128)(2,1)} fusion(bf16[3584,192]{0,1:T(8,128)(2,1)} %param.16, s32[256]{0:T(256)S(1)} %fusion.26), kind=kOutput, calls=%fused_computation.7 | convolution fusion | flops 118374400 | bytes 2294784 | tf_op jit(solution)/shard_map/dot_general | solution.py:335
  93.0 3.0 %convolution_convert_fusion.1.refs_12_ = bf16[3584,256]{1,0:T(8,128)(2,1)} fusion(bf16[3584,192]{0,1:T(8,128)(2,1)} %param.16, s32[256]{0:T(256)S(1)} %fusion.26), kind=kOutput, calls=%fused_computation.8 | convolution fusion | flops 118374400 | bytes 2294784 | tf_op jit(solution)/shard_map/dot_general | solution.py:335
  96.0 2.6 %fusion.8.refs_17_ = f32[512,256]{1,0:T(8,128)} fusion(bf16[512,1024]{1,0:T(8,128)(2,1)S(1)} %copy-done.1, bf16[4096,64]{0,1:T(8,128)(2,1)} %param.17, s32[]{:T(128)S(6)} %select_n.132, s32[256]{0:T(256)S(1)} %fusion.26), kind=kOutput, calls=%fused_computation.12 | convolution fusion | flops 302268416 | bytes 1704964 | tf_op jit(solution)/shard_map/dot_general | solution.py:409
  99.2 3.1 %shard_map.103.refs_6_ = bf16[1024,1024]{1,0:T(8,128)(2,1)} custom-call(s32[3]{0:T(128)} %pad_add_fusion.refs_0_, bf16[256,1024]{1,0:T(8,128)(2,1)} %collective-permute-done.16.refs_1_, bf16[256,1024]{1,0:T(8,128)(2,1)} %collective-permute-done.12.refs_2_, bf16[256,1024]{1,0:T(8,128)(2,1)} %collective-permute-done.17.refs_3_, ...), custom_call_target="tpu_custom_call" | custom-call | bytes 4194304 | tf_op jit(solution)/shard_map/pallas_call | solution.py:111
  103.9 2.6 %collective-permute-start.21 = (bf16[192,512]{1,0:T(8,128)(2,1)S(1)}, bf16[192,512]{1,0:T(8,128)(2,1)S(1)}, u32[]{:S(2)}, u32[]{:S(2)}) collective-permute-start(bf16[192,512]{1,0:T(8,128)(2,1)S(1)} %fusion.12), channel_id=1, source_target_pairs={{0,2},{1,3},{2,0},{3,1},{4,6},{5,7},{6,4},{7,5},{8,10},{9,11},{10,... | collective-permute-start | bytes 589832 | tf_op jit(solution)/shard_map/ppermute | solution.py:308
  106.6 10.3 %shard_map.104 = (f32[512,256]{1,0:T(8,128)}, f32[512,256]{1,0:T(8,128)}) custom-call(s32[3]{0:T(128)} %pad_add_fusion.refs_0_, bf16[4,512,1024]{2,1,0:T(8,128)(2,1)} %bitcast.33, bf16[3584,1024]{1,0:T(8,128)(2,1)} %refs_2_.3, bf16[3584,1024]{1,0:T(8,128)(2,1)} %collective-permute-done.2.refs_3_, bf16[256,1024]{1,0:T(8,128)(2,1)} %copy-done.2, ...), custom_call_target="tpu_custom_call" | custom-call | flops 3623878656 | bytes 12058624 | tf_op jit(solution)/shard_map/pallas_call | solution.py:270
  120.5 25.5 %shard_map.105 = (f32[3,64,128]{2,1,0:T(8,128)}, f32[3,64,128]{2,1,0:T(8,128)}) custom-call(s32[3]{0:T(128)} %pad_add_fusion.refs_0_, bf16[4,512,1024]{2,1,0:T(8,128)(2,1)} %bitcast.34, bf16[3584,1024]{1,0:T(8,128)(2,1)} %refs_2_.3, bf16[3584,1024]{1,0:T(8,128)(2,1)} %collective-permute-done.2.refs_3_, bf16[1536,1024]{1,0:T(8,128)(2,1)} %shard_map.102.refs_4_, ...), custom_call_target="tpu_custom_call" | custom-call | flops 13287555072 | bytes 33030144 | tf_op jit(solution)/shard_map/pallas_call | solution.py:270
  150.0 3.8 %collective-permute-done.24 = f32[3,64,64]{2,1,0:T(8,128)S(1)} collective-permute-done((f32[3,64,64]{2,1,0:T(8,128)S(1)}, f32[3,64,64]{2,1,0:T(8,128)S(1)}, u32[]{:S(2)}, u32[]{:S(2)}) %collective-permute-start.24) | collective-permute-done | bytes 49184 | tf_op jit(solution)/shard_map/ppermute | solution.py:305
  155.5 3.3 %collective-permute-done.25 = f32[3,32,64]{2,1,0:T(8,128)S(1)} collective-permute-done((f32[3,32,64]{2,1,0:T(8,128)S(1)}, f32[3,32,64]{2,1,0:T(8,128)S(1)}, u32[]{:S(2)}, u32[]{:S(2)}) %collective-permute-start.25) | collective-permute-done | bytes 24608 | tf_op jit(solution)/shard_map/ppermute | solution.py:308
  160.1 2.7 %collective-permute-done.26 = f32[3,16,64]{2,1,0:T(8,128)S(1)} collective-permute-done((f32[3,16,64]{2,1,0:T(8,128)S(1)}, f32[3,16,64]{2,1,0:T(8,128)S(1)}, u32[]{:S(2)}, u32[]{:S(2)}) %collective-permute-start.26) | collective-permute-done | bytes 12320 | tf_op jit(solution)/shard_map/ppermute | solution.py:308
  (90 shorter events, 32.3 us)
Async XLA Ops:
  6.5 92.1 %all-gather.3.cloned.1.call-start = ((), (), s32[]{:S(2)}) async-start(), calls=%async_computation | async-start | bytes 5242880 | tf_op jit(solution)/shard_map/all_gather | solution.py:324
  6.5 31.2 %collective-permute-start.2 = (bf16[3584,1024]{1,0:T(8,128)(2,1)}, bf16[3584,1024]{1,0:T(8,128)(2,1)}, u32[]{:S(2)}, u32[]{:S(2)}) collective-permute-start(bf16[3584,1024]{1,0:T(8,128)(2,1)} %refs_2_.3), channel_id=1, source_target_pairs={{0,4},{4,0},{8,12},{12,8},{1,5},{5,1},{9,13},{13,9},{2,6},{6,2},{1... | collective-permute-start | bytes 22020104 | tf_op jit(solution)/shard_map/ppermute | solution.py:306
  10.4 16.0 %collective-permute-start = (bf16[256,1024]{1,0:T(8,128)(2,1)}, bf16[256,1024]{1,0:T(8,128)(2,1)S(1)}, u32[]{:S(2)}, u32[]{:S(2)}) collective-permute-start(bf16[256,1024]{1,0:T(8,128)(2,1)} %shard_map.101), channel_id=1, source_target_pairs={{0,8},{4,12},{8,0},{12,4},{1,9},{5,13},{9,1},{13,5},{2,10},{6,14},... | collective-permute-start | bytes 1572872 | tf_op jit(solution)/shard_map/ppermute | solution.py:305
  17.1 20.6 %collective-permute-start.1 = (bf16[256,1024]{1,0:T(8,128)(2,1)}, bf16[256,1024]{1,0:T(8,128)(2,1)}, u32[]{:S(2)}, u32[]{:S(2)}) collective-permute-start(bf16[256,1024]{1,0:T(8,128)(2,1)} %get-tuple-element.89), channel_id=1, source_target_pairs={{0,8},{4,12},{8,0},{12,4},{1,9},{5,13},{9,1},{13,5},{2,10},{6,14},... | collective-permute-start | bytes 1572872 | tf_op jit(solution)/shard_map/ppermute | solution.py:305
  26.4 20.1 %collective-permute-start.4 = (bf16[256,1024]{1,0:T(8,128)(2,1)S(1)}, bf16[256,1024]{1,0:T(8,128)(2,1)S(1)}, u32[]{:S(2)}, u32[]{:S(2)}) collective-permute-start(bf16[256,1024]{1,0:T(8,128)(2,1)S(1)} %collective-permute-done.refs_4_), channel_id=1, source_target_pairs={{0,4},{4,0},{8,12},{12,8},{1,5},{5,1},{9,13},{13,9},{2,6},{6,2},{1... | collective-permute-start | bytes 1572872 | tf_op jit(solution)/shard_map/ppermute | solution.py:306
  26.4 20.1 %collective-permute-start.6 = (bf16[256,1024]{1,0:T(8,128)(2,1)S(1)}, bf16[256,1024]{1,0:T(8,128)(2,1)S(1)}, u32[]{:S(2)}, u32[]{:S(2)}) collective-permute-start(bf16[256,1024]{1,0:T(8,128)(2,1)S(1)} %collective-permute-done.refs_4_), channel_id=1, source_target_pairs={{0,16},{16,0},{1,17},{17,1},{2,18},{18,2},{3,19},{19,3},{4,20},{20... | collective-permute-start | bytes 1572872 | tf_op jit(solution)/shard_map/ppermute | solution.py:307
  28.6 20.4 %collective-permute-start.5 = (bf16[256,1024]{1,0:T(8,128)(2,1)}, bf16[256,1024]{1,0:T(8,128)(2,1)}, u32[]{:S(2)}, u32[]{:S(2)}) collective-permute-start(bf16[256,1024]{1,0:T(8,128)(2,1)} %get-tuple-element.99), channel_id=1, source_target_pairs={{0,8},{4,12},{8,0},{12,4},{1,9},{5,13},{9,1},{13,5},{2,10},{6,14},... | collective-permute-start | bytes 1572872 | tf_op jit(solution)/shard_map/ppermute | solution.py:305
  37.8 22.5 %collective-permute-start.7 = (bf16[256,1024]{1,0:T(8,128)(2,1)}, bf16[256,1024]{1,0:T(8,128)(2,1)}, u32[]{:S(2)}, u32[]{:S(2)}) collective-permute-start(bf16[256,1024]{1,0:T(8,128)(2,1)} %get-tuple-element.103), channel_id=1, source_target_pairs={{0,8},{4,12},{8,0},{12,4},{1,9},{5,13},{9,1},{13,5},{2,10},{6,14},... | collective-permute-start | bytes 1572872 | tf_op jit(solution)/shard_map/ppermute | solution.py:305
  39.8 20.4 %collective-permute-start.8 = (bf16[256,1024]{1,0:T(8,128)(2,1)}, bf16[256,1024]{1,0:T(8,128)(2,1)}, u32[]{:S(2)}, u32[]{:S(2)}) collective-permute-start(bf16[256,1024]{1,0:T(8,128)(2,1)} %collective-permute-done.1.refs_8_), channel_id=1, source_target_pairs={{0,16},{16,0},{1,17},{17,1},{2,18},{18,2},{3,19},{19,3},{4,20},{20... | collective-permute-start | bytes 1572872 | tf_op jit(solution)/shard_map/ppermute | solution.py:307
  49.0 22.5 %collective-permute-start.10 = (bf16[256,1024]{1,0:T(8,128)(2,1)}, bf16[256,1024]{1,0:T(8,128)(2,1)}, u32[]{:S(2)}, u32[]{:S(2)}) collective-permute-start(bf16[256,1024]{1,0:T(8,128)(2,1)} %get-tuple-element.109), channel_id=1, source_target_pairs={{0,8},{4,12},{8,0},{12,4},{1,9},{5,13},{9,1},{13,5},{2,10},{6,14},... | collective-permute-start | bytes 1572872 | tf_op jit(solution)/shard_map/ppermute | solution.py:305
  51.0 20.4 %collective-permute-start.11 = (bf16[256,1024]{1,0:T(8,128)(2,1)}, bf16[256,1024]{1,0:T(8,128)(2,1)}, u32[]{:S(2)}, u32[]{:S(2)}) collective-permute-start(bf16[256,1024]{1,0:T(8,128)(2,1)} %collective-permute-done.5.refs_2_), channel_id=1, source_target_pairs={{0,16},{16,0},{1,17},{17,1},{2,18},{18,2},{3,19},{19,3},{4,20},{20... | collective-permute-start | bytes 1572872 | tf_op jit(solution)/shard_map/ppermute | solution.py:307
  52.6 18.9 %collective-permute-start.9 = (bf16[256,1024]{1,0:T(8,128)(2,1)S(1)}, bf16[256,1024]{1,0:T(8,128)(2,1)S(1)}, u32[]{:S(2)}, u32[]{:S(2)}) collective-permute-start(bf16[256,1024]{1,0:T(8,128)(2,1)S(1)} %collective-permute-done.6.refs_6_), channel_id=1, source_target_pairs={{0,4},{4,0},{8,12},{12,8},{1,5},{5,1},{9,13},{13,9},{2,6},{6,2},{1... | collective-permute-start | bytes 1572872 | tf_op jit(solution)/shard_map/ppermute | solution.py:306
  60.2 22.5 %collective-permute-start.12 = (bf16[256,1024]{1,0:T(8,128)(2,1)}, bf16[256,1024]{1,0:T(8,128)(2,1)}, u32[]{:S(2)}, u32[]{:S(2)}) collective-permute-start(bf16[256,1024]{1,0:T(8,128)(2,1)} %get-tuple-element.113), channel_id=1, source_target_pairs={{0,8},{4,12},{8,0},{12,4},{1,9},{5,13},{9,1},{13,5},{2,10},{6,14},... | collective-permute-start | bytes 1572872 | tf_op jit(solution)/shard_map/ppermute | solution.py:305
  62.3 20.4 %collective-permute-start.13 = (bf16[256,1024]{1,0:T(8,128)(2,1)}, bf16[256,1024]{1,0:T(8,128)(2,1)}, u32[]{:S(2)}, u32[]{:S(2)}) collective-permute-start(bf16[256,1024]{1,0:T(8,128)(2,1)} %collective-permute-done.7.refs_4_), channel_id=1, source_target_pairs={{0,16},{16,0},{1,17},{17,1},{2,18},{18,2},{3,19},{19,3},{4,20},{20... | collective-permute-start | bytes 1572872 | tf_op jit(solution)/shard_map/ppermute | solution.py:307
  71.5 27.1 %collective-permute-start.3 = (bf16[256,1024]{1,0:T(8,128)(2,1)}, bf16[256,1024]{1,0:T(8,128)(2,1)}, u32[]{:S(2)}, u32[]{:S(2)}) collective-permute-start(bf16[256,1024]{1,0:T(8,128)(2,1)} %collective-permute-done.1.refs_8_), channel_id=1, source_target_pairs={{0,4},{4,0},{8,12},{12,8},{1,5},{5,1},{9,13},{13,9},{2,6},{6,2},{1... | collective-permute-start | bytes 1572872 | tf_op jit(solution)/shard_map/ppermute | solution.py:306
  71.5 27.1 %collective-permute-start.15 = (bf16[256,1024]{1,0:T(8,128)(2,1)}, bf16[256,1024]{1,0:T(8,128)(2,1)}, u32[]{:S(2)}, u32[]{:S(2)}) collective-permute-start(bf16[256,1024]{1,0:T(8,128)(2,1)} %get-tuple-element.118), channel_id=1, source_target_pairs={{0,8},{4,12},{8,0},{12,4},{1,9},{5,13},{9,1},{13,5},{2,10},{6,14},... | collective-permute-start | bytes 1572872 | tf_op jit(solution)/shard_map/ppermute | solution.py:305
  73.6 25.0 %collective-permute-start.16 = (bf16[256,1024]{1,0:T(8,128)(2,1)}, bf16[256,1024]{1,0:T(8,128)(2,1)}, u32[]{:S(2)}, u32[]{:S(2)}) collective-permute-start(bf16[256,1024]{1,0:T(8,128)(2,1)} %collective-permute-done.10.refs_6_), channel_id=1, source_target_pairs={{0,16},{16,0},{1,17},{17,1},{2,18},{18,2},{3,19},{19,3},{4,20},{20... | collective-permute-start | bytes 1572872 | tf_op jit(solution)/shard_map/ppermute | solution.py:307
  82.7 16.5 %collective-permute-start.17 = (bf16[256,1024]{1,0:T(8,128)(2,1)}, bf16[256,1024]{1,0:T(8,128)(2,1)}, u32[]{:S(2)}, u32[]{:S(2)}) collective-permute-start(bf16[256,1024]{1,0:T(8,128)(2,1)} %collective-permute-done.12.refs_2_), channel_id=1, source_target_pairs={{0,16},{16,0},{1,17},{17,1},{2,18},{18,2},{3,19},{19,3},{4,20},{20... | collective-permute-start | bytes 1572872 | tf_op jit(solution)/shard_map/ppermute | solution.py:307
  84.8 13.8 %collective-permute-start.14 = (bf16[192,512]{1,0:T(8,128)(2,1)S(1)}, bf16[192,512]{1,0:T(8,128)(2,1)S(1)}, u32[]{:S(2)}, u32[]{:S(2)}) collective-permute-start(bf16[192,512]{1,0:T(8,128)(2,1)S(1)} %convert_element_type.38), channel_id=1, source_target_pairs={{0,1},{1,0},{2,3},{3,2},{4,5},{5,4},{6,7},{7,6},{8,9},{9,8},{10,11... | collective-permute-start | bytes 589832 | tf_op jit(solution)/shard_map/ppermute | solution.py:308
  99.2 20.5 %collective-permute-start.18 = (bf16[1536,1024]{1,0:T(8,128)(2,1)}, bf16[1536,1024]{1,0:T(8,128)(2,1)}, u32[]{:S(2)}, u32[]{:S(2)}) collective-permute-start(bf16[1536,1024]{1,0:T(8,128)(2,1)} %shard_map.102.refs_4_), channel_id=1, source_target_pairs={{0,4},{4,0},{8,12},{12,8},{1,5},{5,1},{9,13},{13,9},{2,6},{6,2},{1... | collective-permute-start | bytes 9437192 | tf_op jit(solution)/shard_map/ppermute | solution.py:306
  102.3 17.3 %collective-permute-start.19 = (bf16[1024,1024]{1,0:T(8,128)(2,1)}, bf16[1024,1024]{1,0:T(8,128)(2,1)}, u32[]{:S(2)}, u32[]{:S(2)}) collective-permute-start(bf16[1024,1024]{1,0:T(8,128)(2,1)} %shard_map.103.refs_6_), channel_id=1, source_target_pairs={{0,4},{4,0},{8,12},{12,8},{1,5},{5,1},{9,13},{13,9},{2,6},{6,2},{1... | collective-permute-start | bytes 6291464 | tf_op jit(solution)/shard_map/ppermute | solution.py:306
  102.9 14.9 %collective-permute-start.20 = (bf16[256,1024]{1,0:T(8,128)(2,1)S(1)}, bf16[256,1024]{1,0:T(8,128)(2,1)S(1)}, u32[]{:S(2)}, u32[]{:S(2)}) collective-permute-start(bf16[256,1024]{1,0:T(8,128)(2,1)S(1)} %copy-done.8), channel_id=1, source_target_pairs={{0,8},{4,12},{8,0},{12,4},{1,9},{5,13},{9,1},{13,5},{2,10},{6,14},... | collective-permute-start | bytes 1572872 | tf_op jit(solution)/shard_map/ppermute | solution.py:305
  103.9 13.0 %collective-permute-start.21 = (bf16[192,512]{1,0:T(8,128)(2,1)S(1)}, bf16[192,512]{1,0:T(8,128)(2,1)S(1)}, u32[]{:S(2)}, u32[]{:S(2)}) collective-permute-start(bf16[192,512]{1,0:T(8,128)(2,1)S(1)} %fusion.12), channel_id=1, source_target_pairs={{0,2},{1,3},{2,0},{3,1},{4,6},{5,7},{6,4},{7,5},{8,10},{9,11},{10,... | collective-permute-start | bytes 589832 | tf_op jit(solution)/shard_map/ppermute | solution.py:308
  153.8 5.1 %collective-permute-start.25 = (f32[3,32,64]{2,1,0:T(8,128)S(1)}, f32[3,32,64]{2,1,0:T(8,128)S(1)}, u32[]{:S(2)}, u32[]{:S(2)}) collective-permute-start(f32[3,32,64]{2,1,0:T(8,128)S(1)} %dynamic-slice_bitcast_fusion), channel_id=1, source_target_pairs={{0,2},{1,3},{2,0},{3,1},{4,6},{5,7},{6,4},{7,5},{8,10},{9,11},{10,... | collective-permute-start | bytes 73736 | tf_op jit(solution)/shard_map/ppermute | solution.py:308
  (16 other events, 221.8 us)
Sparse Core Ops, SparseCore 0:
  8.9 83.5 all-gather.2

commit v5 on v4

--- a/solution.py
+++ b/solution.py
@@ -147,7 +147,7 @@
         keep, send = take(2)
     else:
         acc_out = take(2)
-    og, wbuf, gbuf, ubuf, pbuf, grads, og_sem, sems, p_sem = take(9)
+    og, wbuf, gbuf, ubuf, pbuf, grads, acc, og_sem, sems, p_sem = take(10)
     s, y = scal[0], scal[2]
     n = len(tiles)
 
@@ -202,23 +202,17 @@
         pltpu.make_async_copy(gate.at[:, rows], gbuf.at[slot], sems.at[slot, 4]).wait()
         pltpu.make_async_copy(up.at[:, rows], ubuf.at[slot], sems.at[slot, 5]).wait()
 
-    def first_quarter(j):
-        weights_arrive(0, j)
+    fetch(jnp.int32(0), 0, True)
+    fetch(jnp.int32(1), 1)
+    for j in range(4):
         pltpu.make_async_copy(gathered.at[j], og.at[j], og_sem.at[j]).wait()
-        if j == 2 and n > 1:
-            fetch(jnp.int32(1), 1)
-
-    fetch(jnp.int32(0), 0, True)
-    total = dots(0, first_quarter)
-    streams_arrive(0)
-    finish(0, 0, total)
-
-    @pl.loop(1, n)
+
+    @pl.loop(0, n)
     def _(t):
-        slot = lax.rem(t, 2)
-        @pl.when(t + 1 < n)
+        slot = lax.rem(t, 3)
+        @pl.when(t + 2 < n)
         def _():
-            fetch(t + 1, 1 - slot)
+            fetch(t + 2, lax.rem(t + 2, 3))
         for j in range(4):
             weights_arrive(slot, j)
         streams_arrive(slot)
@@ -227,27 +221,44 @@
     every = pl.ds(0, n * TILE)
     pltpu.make_async_copy(pg.at[every], pbuf.at[0], p_sem).wait()
     pltpu.make_async_copy(pu.at[every], pbuf.at[1], p_sem).wait()
-    acc = [jnp.dot(grads[i], pbuf[i], preferred_element_type=F32) for i in range(2)]
+
+    @pl.loop(0, 2)
+    def _(i):
+        acc[i] = jnp.dot(grads[i], pbuf[i], preferred_element_type=F32)
+
     if not first:
-        acc = [a + b[...] for a, b in zip(acc, acc_in)]
+        acc[0] += acc_in[0][...]
+        acc[1] += acc_in[1][...]
     if not last:
         acc_out[0][...] = acc[0]
         acc_out[1][...] = acc[1]
         return
-    tokens = acc[0].shape[0]
+    acc[2] = r_down[...]
+    tokens = acc.shape[1]
     where = s * tokens + lax.broadcasted_iota(jnp.int32, (tokens, 256), 0)
     weight = jnp.where((where >= lo[...]) & (where < hi[...]), scale[...], 0.0)
-    for l in range(3):
-        right = (r_down[...] if l == 2 else acc[l]) * weight
-        m = jnp.dot(
-            left_t[pl.ds(64 * l, 64), :],
-            right,
-            precision=lax.Precision.HIGHEST,
-            preferred_element_type=F32,
-        )
-        even = lax.rem(s, 2) == 0
-        keep[l] = jnp.where(even, m[:, :128], m[:, 128:])
-        send[l] = jnp.where(even, m[:, 128:], m[:, :128])
+    even = lax.rem(s, 2) == 0
+
+    @pl.loop(0, 3)
+    def _(l):
+        right = acc[l] * weight
+        left = left_t[pl.ds(pl.multiple_of(64 * l, 64), 64), :]
+        right_high, left_high = right.astype(BF16), left.astype(BF16)
+        right_low = (right - right_high.astype(F32)).astype(BF16)
+        left_low = (left - left_high.astype(F32)).astype(BF16)
+        both = jnp.dot(
+            jnp.concatenate([left_high, left_low]), right_high, preferred_element_type=F32
+        )
+        m = both[:64] + (
+            both[64:] + jnp.dot(left_high, right_low, preferred_element_type=F32)
+        )
+        for x in range(2):
+            a, b = m[:, 64 * x : 64 * x + 64], m[:, 128 + 64 * x : 192 + 64 * x]
+            mine, other = jnp.where(even, a, b), jnp.where(even, b, a)
+            for rows in range(4):
+                part = slice(16 * rows, 16 * rows + 16)
+                keep[x, rows, l] = mine[part]
+                send[x, rows, l] = other[part]
 
 
 def grads_call(tiles, half, scal, gathered, weights, pairs, streams, acc, tail):
@@ -263,7 +274,7 @@
     if last:
         args += list(tail)
         specs += [vmem] * len(tail)
-        outs = [jax.ShapeDtypeStruct((3, 64, 128), F32)] * 2
+        outs = [jax.ShapeDtypeStruct((2, 4, 3, 16, 64), F32)] * 2
     else:
         outs = [jax.ShapeDtypeStruct((tokens, 256), F32)] * 2
     units = len(tiles) * TILE
@@ -274,13 +285,14 @@
         out_specs=[vmem] * 2,
         scratch_shapes=[
             pltpu.VMEM((4, tokens, depth), BF16),
-            pltpu.VMEM((2, 4, TILE, depth), BF16),
-            pltpu.VMEM((2, tokens, TILE), BF16),
-            pltpu.VMEM((2, tokens, TILE), BF16),
+            pltpu.VMEM((3, 4, TILE, depth), BF16),
+            pltpu.VMEM((3, tokens, TILE), BF16),
+            pltpu.VMEM((3, tokens, TILE), BF16),
             pltpu.VMEM((2, units, 256), BF16),
             pltpu.VMEM((2, tokens, units), BF16),
+            pltpu.VMEM((3, tokens, 256), F32),
             pltpu.SemaphoreType.DMA((4,)),
-            pltpu.SemaphoreType.DMA((2, 6)),
+            pltpu.SemaphoreType.DMA((3, 6)),
             pltpu.SemaphoreType.DMA,
         ],
         compiler_params=pltpu.CompilerParams(vmem_limit_bytes=60 * 1024 * 1024),
@@ -343,8 +355,8 @@
         0: ((0, 0),),
         2: ((0, 1),),
         4: ((1, 0),),
-        5: ((1, 1), (2, 0), (2, 1), (3, 0), (3, 1), (4, 0)),
-        6: ((4, 1), (5, 0), (5, 1), (6, 0)),
+        5: ((1, 1), (2, 0), (2, 1), (3, 0), (3, 1), (4, 0), (5, 0)),
+        6: ((4, 1), (5, 1), (6, 0)),
     }
     swapped_by = {2: 0, 4: 1, 6: 2}
     pairs, where = [], {}
@@ -442,13 +454,12 @@
     acc = grads(late + ((7, 0),), acc, (left_t, r_down, lo, hi, scale))
     keep, send = acc
     x = s // 2
-    total = (keep + over_c(send)).reshape(3, 64, 2, 64)
-    part = lambda a, axis, at: lax.dynamic_index_in_dim(a, at, axis, keepdims=False)
-    total = part(total, 2, x) + over_x(part(total, 2, 1 - x))
-    total = total.reshape(3, 2, 32, 64)
-    total = part(total, 1, z // 2) + over_z(part(total, 1, 1 - z // 2), 2)
-    total = total.reshape(3, 2, 16, 64)
-    total = part(total, 1, z % 2) + over_z(part(total, 1, 1 - z % 2), 1)
+    part = lambda a, at: lax.dynamic_index_in_dim(a, at, 0, keepdims=False)
+    total = keep + over_c(send)
+    total = part(total, x) + over_x(part(total, 1 - x))
+    total = total.reshape(2, 2, 3, 16, 64)
+    total = part(total, z // 2) + over_z(part(total, 1 - z // 2), 2)
+    total = part(total, z % 2) + over_z(part(total, 1 - z % 2), 1)
     return total.reshape(3, 16, 4, 16).transpose(2, 0, 1, 3)
 
 

time: 171 us -> 170 us (level)
  no operation moved by 1% of the time
where the time goes in v5:
time: 170 us
  waiting for transfers between devices  55 us (32%)
  Pallas kernels  48.4 us (28%)
  starting transfers between devices  33.5 us (20%)
  matrix products  13.7 us (8%)
  between operations  13.7 us (8%)
  other arithmetic  4.09 us (2%)
    ppermute x9, waiting for transfers between devices, local(): over_x = lambda a: lax.ppermute(a, 'seq', [(i, i ^ 2) for i in range(4)])  44.5 us
    pallas_call x2, Pallas kernels, grads_call(): pl.pallas_call(functools.partial(grads_kernel, tiles, half, first, last),...  35.5 us
    ppermute x9, starting transfers between devices, local(): over_x = lambda a: lax.ppermute(a, 'seq', [(i, i ^ 2) for i in range(4)])  15 us
    pallas_call x4, Pallas kernels, move(): pl.pallas_call(functools.partial(move_kernel, tuple(moves), len(ins)), ou...  12.9 us
    ppermute x6, starting transfers between devices, local(): over_y = lambda a: lax.ppermute(a, 'groups', [(0, 1), (1, 0)])  10.3 us
    ppermute x4, starting transfers between devices, local(): lax.ppermute(a, 'tensor', [(i, i ^ k) for i in range(4)])  6.93 us
    ppermute x4, waiting for transfers between devices, local(): lax.ppermute(a, 'tensor', [(i, i ^ k) for i in range(4)])  6.33 us
    dot_general x2, matrix products, local(): jnp.dot(a, spread, preferred_element_type=F32).astype(BF16)  6.02 us
  transfers between devices with their start and end apart: 28, of which 12 were waited for; matrix products, arithmetic and copies ran while one was open for 10% of the time, Pallas kernels for 14%

profile of v5, /device:TPU:0, one launch (start us, length us, event | category | flops | bytes accessed | tf_op | source)
XLA Modules:
  0.0 169.9 jit_solution(12839596764264571900)
XLA Ops:
  7.9 2.5 %shard_map.101 = bf16[256,1024]{1,0:T(8,128)(2,1)} custom-call(s32[3]{0:T(128)} %pad_add_fusion.refs_0_, bf16[2,1792,1024]{2,1,0:T(8,128)(2,1)} %bitcast.32), custom_call_target="tpu_custom_call" | custom-call | bytes 1048576 | tf_op jit(solution)/shard_map/pallas_call | solution.py:111
  10.5 3.0 %collective-permute-start = (bf16[256,1024]{1,0:T(8,128)(2,1)}, bf16[256,1024]{1,0:T(8,128)(2,1)S(1)}, u32[]{:S(2)}, u32[]{:S(2)}) collective-permute-start(bf16[256,1024]{1,0:T(8,128)(2,1)} %shard_map.101), channel_id=1, source_target_pairs={{0,8},{4,12},{8,0},{12,4},{1,9},{5,13},{9,1},{13,5},{2,10},{6,14},... | collective-permute-start | bytes 1572872 | tf_op jit(solution)/shard_map/ppermute | solution.py:317
  13.5 3.7 %shard_map.100 = (bf16[256,1024]{1,0:T(8,128)(2,1)}, bf16[256,1024]{1,0:T(8,128)(2,1)}, bf16[256,1024]{1,0:T(8,128)(2,1)}, bf16[256,1024]{1,0:T(8,128)(2,1)}, bf...) custom-call(s32[3]{0:T(128)} %pad_add_fusion.refs_0_, bf16[2,1792,1024]{2,1,0:T(8,128)(2,1)} %bitcast.33), custom_call_target="tpu_custom_call" | custom-call | bytes 7340032 | tf_op jit(solution)/shard_map/pallas_call | solution.py:111
  18.8 7.6 %collective-permute-done.refs_4_ = bf16[256,1024]{1,0:T(8,128)(2,1)S(1)} collective-permute-done((bf16[256,1024]{1,0:T(8,128)(2,1)}, bf16[256,1024]{1,0:T(8,128)(2,1)S(1)}, u32[]{:S(2)}, u32[]{:S(2)}) %collective-permute-start) | collective-permute-done | bytes 524320 | tf_op jit(solution)/shard_map/ppermute | solution.py:317
  26.4 2.1 %collective-permute-start.6 = (bf16[256,1024]{1,0:T(8,128)(2,1)S(1)}, bf16[256,1024]{1,0:T(8,128)(2,1)S(1)}, u32[]{:S(2)}, u32[]{:S(2)}) collective-permute-start(bf16[256,1024]{1,0:T(8,128)(2,1)S(1)} %collective-permute-done.refs_4_), channel_id=1, source_target_pairs={{0,16},{16,0},{1,17},{17,1},{2,18},{18,2},{3,19},{19,3},{4,20},{20... | collective-permute-start | bytes 1572872 | tf_op jit(solution)/shard_map/ppermute | solution.py:319
  30.1 7.7 %collective-permute-done.1.refs_8_ = bf16[256,1024]{1,0:T(8,128)(2,1)} collective-permute-done((bf16[256,1024]{1,0:T(8,128)(2,1)}, bf16[256,1024]{1,0:T(8,128)(2,1)}, u32[]{:S(2)}, u32[]{:S(2)}) %collective-permute-start.1) | collective-permute-done | bytes 524320 | tf_op jit(solution)/shard_map/ppermute | solution.py:317
  41.3 4.6 %fusion.5 = f32[512,64]{0,1:T(8,128)S(1)} fusion(bf16[512,3584]{1,0:T(8,128)(2,1)} %refs_11_.3, bf16[512,3584]{1,0:T(8,128)(2,1)} %refs_10_.3, bf16[3584,192]{0,1:T(8,128)(2,1)} %param.16), kind=kOutput, calls=%fused_computation.9 | convolution fusion | flops 249561088 | bytes 7929856 | tf_op jit(solution)/shard_map/dot_general | solution.py:410
  46.6 2.4 %collective-permute-done.5.refs_2_ = bf16[256,1024]{1,0:T(8,128)(2,1)} collective-permute-done((bf16[256,1024]{1,0:T(8,128)(2,1)}, bf16[256,1024]{1,0:T(8,128)(2,1)}, u32[]{:S(2)}, u32[]{:S(2)}) %collective-permute-start.5) | collective-permute-done | bytes 524320 | tf_op jit(solution)/shard_map/ppermute | solution.py:317
  52.6 7.7 %collective-permute-done.7.refs_4_ = bf16[256,1024]{1,0:T(8,128)(2,1)} collective-permute-done((bf16[256,1024]{1,0:T(8,128)(2,1)}, bf16[256,1024]{1,0:T(8,128)(2,1)}, u32[]{:S(2)}, u32[]{:S(2)}) %collective-permute-start.7) | collective-permute-done | bytes 524320 | tf_op jit(solution)/shard_map/ppermute | solution.py:317
  63.8 7.6 %collective-permute-done.10.refs_6_ = bf16[256,1024]{1,0:T(8,128)(2,1)} collective-permute-done((bf16[256,1024]{1,0:T(8,128)(2,1)}, bf16[256,1024]{1,0:T(8,128)(2,1)}, u32[]{:S(2)}, u32[]{:S(2)}) %collective-permute-start.10) | collective-permute-done | bytes 524320 | tf_op jit(solution)/shard_map/ppermute | solution.py:317
  71.5 2.1 %collective-permute-start.15 = (bf16[256,1024]{1,0:T(8,128)(2,1)}, bf16[256,1024]{1,0:T(8,128)(2,1)}, u32[]{:S(2)}, u32[]{:S(2)}) collective-permute-start(bf16[256,1024]{1,0:T(8,128)(2,1)} %get-tuple-element.119), channel_id=1, source_target_pairs={{0,8},{4,12},{8,0},{12,4},{1,9},{5,13},{9,1},{13,5},{2,10},{6,14},... | collective-permute-start | bytes 1572872 | tf_op jit(solution)/shard_map/ppermute | solution.py:317
  75.1 7.6 %collective-permute-done.12.refs_7_ = bf16[256,1024]{1,0:T(8,128)(2,1)} collective-permute-done((bf16[256,1024]{1,0:T(8,128)(2,1)}, bf16[256,1024]{1,0:T(8,128)(2,1)}, u32[]{:S(2)}, u32[]{:S(2)}) %collective-permute-start.12) | collective-permute-done | bytes 524320 | tf_op jit(solution)/shard_map/ppermute | solution.py:317
  82.7 2.1 %collective-permute-start.17 = (bf16[256,1024]{1,0:T(8,128)(2,1)}, bf16[256,1024]{1,0:T(8,128)(2,1)}, u32[]{:S(2)}, u32[]{:S(2)}) collective-permute-start(bf16[256,1024]{1,0:T(8,128)(2,1)} %collective-permute-done.12.refs_7_), channel_id=1, source_target_pairs={{0,16},{16,0},{1,17},{17,1},{2,18},{18,2},{3,19},{19,3},{4,20},{20... | collective-permute-start | bytes 1572872 | tf_op jit(solution)/shard_map/ppermute | solution.py:319
  86.5 3.7 %shard_map.102.refs_4_ = bf16[1792,1024]{1,0:T(8,128)(2,1)} custom-call(s32[3]{0:T(128)} %pad_add_fusion.refs_0_, bf16[256,1024]{1,0:T(8,128)(2,1)} %collective-permute-done.8.refs_1_, bf16[256,1024]{1,0:T(8,128)(2,1)} %collective-permute-done.5.refs_2_, bf16[256,1024]{1,0:T(8,128)(2,1)} %collective-permute-done.11.refs_3_, ...), custom_call_target="tpu_custom_call" | custom-call | bytes 7340032 | tf_op jit(solution)/shard_map/pallas_call | solution.py:111
  90.2 3.0 %convolution_convert_fusion.refs_13_ = bf16[3584,256]{1,0:T(8,128)(2,1)} fusion(bf16[3584,192]{0,1:T(8,128)(2,1)} %param.16, s32[256]{0:T(256)S(1)} %fusion.26), kind=kOutput, calls=%fused_computation.7 | convolution fusion | flops 118374400 | bytes 2294784 | tf_op jit(solution)/shard_map/dot_general | solution.py:347
  93.2 3.0 %convolution_convert_fusion.1.refs_12_ = bf16[3584,256]{1,0:T(8,128)(2,1)} fusion(bf16[3584,192]{0,1:T(8,128)(2,1)} %param.16, s32[256]{0:T(256)S(1)} %fusion.26), kind=kOutput, calls=%fused_computation.8 | convolution fusion | flops 118374400 | bytes 2294784 | tf_op jit(solution)/shard_map/dot_general | solution.py:347
  96.2 2.5 %fusion.8.refs_17_ = f32[512,256]{1,0:T(8,128)} fusion(bf16[512,1024]{1,0:T(8,128)(2,1)S(1)} %copy-done.1, bf16[4096,64]{0,1:T(8,128)(2,1)} %param.17, s32[]{:T(128)S(6)} %select_n.132, s32[256]{0:T(256)S(1)} %fusion.26), kind=kOutput, calls=%fused_computation.12 | convolution fusion | flops 302268416 | bytes 1704964 | tf_op jit(solution)/shard_map/dot_general | solution.py:421
  99.2 2.9 %shard_map.103.refs_6_ = bf16[768,1024]{1,0:T(8,128)(2,1)} custom-call(s32[3]{0:T(128)} %pad_add_fusion.refs_0_, bf16[256,1024]{1,0:T(8,128)(2,1)} %collective-permute-done.16.refs_1_, bf16[256,1024]{1,0:T(8,128)(2,1)} %collective-permute-done.17.refs_2_, bf16[256,1024]{1,0:T(8,128)(2,1)} %collective-permute-done.15.refs_3_), custom_call_target="tpu_custom_call" | custom-call | bytes 3145728 | tf_op jit(solution)/shard_map/pallas_call | solution.py:111
  103.9 2.7 %collective-permute-start.21 = (bf16[192,512]{1,0:T(8,128)(2,1)S(1)}, bf16[192,512]{1,0:T(8,128)(2,1)S(1)}, u32[]{:S(2)}, u32[]{:S(2)}) collective-permute-start(bf16[192,512]{1,0:T(8,128)(2,1)S(1)} %fusion.12), channel_id=1, source_target_pairs={{0,2},{1,3},{2,0},{3,1},{4,6},{5,7},{6,4},{7,5},{8,10},{9,11},{10,... | collective-permute-start | bytes 589832 | tf_op jit(solution)/shard_map/ppermute | solution.py:320
  106.5 10.4 %shard_map.104 = (f32[512,256]{1,0:T(8,128)}, f32[512,256]{1,0:T(8,128)}) custom-call(s32[3]{0:T(128)} %pad_add_fusion.refs_0_, bf16[4,512,1024]{2,1,0:T(8,128)(2,1)} %bitcast.34, bf16[3584,1024]{1,0:T(8,128)(2,1)} %refs_2_.3, bf16[3584,1024]{1,0:T(8,128)(2,1)} %collective-permute-done.2.refs_3_, bf16[256,1024]{1,0:T(8,128)(2,1)} %copy-done.2, ...), custom_call_target="tpu_custom_call" | custom-call | flops 3623878656 | bytes 12058624 | tf_op jit(solution)/shard_map/pallas_call | solution.py:281
  120.5 25.1 %shard_map.105 = (f32[2,4,3,16,64]{4,3,2,1,0:T(8,128)}, f32[2,4,3,16,64]{4,3,2,1,0:T(8,128)}) custom-call(s32[3]{0:T(128)} %pad_add_fusion.refs_0_, bf16[4,512,1024]{2,1,0:T(8,128)(2,1)} %bitcast.35, bf16[3584,1024]{1,0:T(8,128)(2,1)} %refs_2_.3, bf16[3584,1024]{1,0:T(8,128)(2,1)} %collective-permute-done.2.refs_3_, bf16[1792,1024]{1,0:T(8,128)(2,1)} %shard_map.102.refs_4_, ...), custom_call_target="tpu_custom_call" | custom-call | flops 13287555072 | bytes 33030144 | tf_op jit(solution)/shard_map/pallas_call | solution.py:281
  149.3 3.9 %collective-permute-done.24 = f32[4,3,16,64]{3,2,1,0:T(8,128)S(1)} collective-permute-done((f32[4,3,16,64]{3,2,1,0:T(8,128)S(1)}, f32[4,3,16,64]{3,2,1,0:T(8,128)S(1)}, u32[]{:S(2)}, u32[]{:S(2)}) %collective-permute-start.24) | collective-permute-done | bytes 49184 | tf_op jit(solution)/shard_map/ppermute | solution.py:317
  154.7 3.6 %collective-permute-done.25 = f32[2,3,16,64]{3,2,1,0:T(8,128)S(1)} collective-permute-done((f32[2,3,16,64]{3,2,1,0:T(8,128)S(1)}, f32[2,3,16,64]{3,2,1,0:T(8,128)S(1)}, u32[]{:S(2)}, u32[]{:S(2)}) %collective-permute-start.25) | collective-permute-done | bytes 24608 | tf_op jit(solution)/shard_map/ppermute | solution.py:320
  159.5 2.7 %collective-permute-done.26 = f32[3,16,64]{2,1,0:T(8,128)S(1)} collective-permute-done((f32[3,16,64]{2,1,0:T(8,128)S(1)}, f32[3,16,64]{2,1,0:T(8,128)S(1)}, u32[]{:S(2)}, u32[]{:S(2)}) %collective-permute-start.26) | collective-permute-done | bytes 12320 | tf_op jit(solution)/shard_map/ppermute | solution.py:320
  (89 shorter events, 31.8 us)
Async XLA Ops:
  6.5 92.2 %all-gather.3.cloned.1.call-start = ((), (), s32[]{:S(2)}) async-start(), calls=%async_computation | async-start | bytes 5242880 | tf_op jit(solution)/shard_map/all_gather | solution.py:336
  6.5 31.2 %collective-permute-start.2 = (bf16[3584,1024]{1,0:T(8,128)(2,1)}, bf16[3584,1024]{1,0:T(8,128)(2,1)}, u32[]{:S(2)}, u32[]{:S(2)}) collective-permute-start(bf16[3584,1024]{1,0:T(8,128)(2,1)} %refs_2_.3), channel_id=1, source_target_pairs={{0,4},{4,0},{8,12},{12,8},{1,5},{5,1},{9,13},{13,9},{2,6},{6,2},{1... | collective-permute-start | bytes 22020104 | tf_op jit(solution)/shard_map/ppermute | solution.py:318
  10.5 16.0 %collective-permute-start = (bf16[256,1024]{1,0:T(8,128)(2,1)}, bf16[256,1024]{1,0:T(8,128)(2,1)S(1)}, u32[]{:S(2)}, u32[]{:S(2)}) collective-permute-start(bf16[256,1024]{1,0:T(8,128)(2,1)} %shard_map.101), channel_id=1, source_target_pairs={{0,8},{4,12},{8,0},{12,4},{1,9},{5,13},{9,1},{13,5},{2,10},{6,14},... | collective-permute-start | bytes 1572872 | tf_op jit(solution)/shard_map/ppermute | solution.py:317
  17.2 20.6 %collective-permute-start.1 = (bf16[256,1024]{1,0:T(8,128)(2,1)}, bf16[256,1024]{1,0:T(8,128)(2,1)}, u32[]{:S(2)}, u32[]{:S(2)}) collective-permute-start(bf16[256,1024]{1,0:T(8,128)(2,1)} %get-tuple-element.89), channel_id=1, source_target_pairs={{0,8},{4,12},{8,0},{12,4},{1,9},{5,13},{9,1},{13,5},{2,10},{6,14},... | collective-permute-start | bytes 1572872 | tf_op jit(solution)/shard_map/ppermute | solution.py:317
  26.4 20.1 %collective-permute-start.4 = (bf16[256,1024]{1,0:T(8,128)(2,1)S(1)}, bf16[256,1024]{1,0:T(8,128)(2,1)S(1)}, u32[]{:S(2)}, u32[]{:S(2)}) collective-permute-start(bf16[256,1024]{1,0:T(8,128)(2,1)S(1)} %collective-permute-done.refs_4_), channel_id=1, source_target_pairs={{0,4},{4,0},{8,12},{12,8},{1,5},{5,1},{9,13},{13,9},{2,6},{6,2},{1... | collective-permute-start | bytes 1572872 | tf_op jit(solution)/shard_map/ppermute | solution.py:318
  26.4 20.1 %collective-permute-start.6 = (bf16[256,1024]{1,0:T(8,128)(2,1)S(1)}, bf16[256,1024]{1,0:T(8,128)(2,1)S(1)}, u32[]{:S(2)}, u32[]{:S(2)}) collective-permute-start(bf16[256,1024]{1,0:T(8,128)(2,1)S(1)} %collective-permute-done.refs_4_), channel_id=1, source_target_pairs={{0,16},{16,0},{1,17},{17,1},{2,18},{18,2},{3,19},{19,3},{4,20},{20... | collective-permute-start | bytes 1572872 | tf_op jit(solution)/shard_map/ppermute | solution.py:319
  28.6 20.4 %collective-permute-start.5 = (bf16[256,1024]{1,0:T(8,128)(2,1)}, bf16[256,1024]{1,0:T(8,128)(2,1)}, u32[]{:S(2)}, u32[]{:S(2)}) collective-permute-start(bf16[256,1024]{1,0:T(8,128)(2,1)} %get-tuple-element.99), channel_id=1, source_target_pairs={{0,8},{4,12},{8,0},{12,4},{1,9},{5,13},{9,1},{13,5},{2,10},{6,14},... | collective-permute-start | bytes 1572872 | tf_op jit(solution)/shard_map/ppermute | solution.py:317
  37.8 22.5 %collective-permute-start.7 = (bf16[256,1024]{1,0:T(8,128)(2,1)}, bf16[256,1024]{1,0:T(8,128)(2,1)}, u32[]{:S(2)}, u32[]{:S(2)}) collective-permute-start(bf16[256,1024]{1,0:T(8,128)(2,1)} %get-tuple-element.103), channel_id=1, source_target_pairs={{0,8},{4,12},{8,0},{12,4},{1,9},{5,13},{9,1},{13,5},{2,10},{6,14},... | collective-permute-start | bytes 1572872 | tf_op jit(solution)/shard_map/ppermute | solution.py:317
  39.8 20.4 %collective-permute-start.8 = (bf16[256,1024]{1,0:T(8,128)(2,1)}, bf16[256,1024]{1,0:T(8,128)(2,1)}, u32[]{:S(2)}, u32[]{:S(2)}) collective-permute-start(bf16[256,1024]{1,0:T(8,128)(2,1)} %collective-permute-done.1.refs_8_), channel_id=1, source_target_pairs={{0,16},{16,0},{1,17},{17,1},{2,18},{18,2},{3,19},{19,3},{4,20},{20... | collective-permute-start | bytes 1572872 | tf_op jit(solution)/shard_map/ppermute | solution.py:319
  49.0 22.5 %collective-permute-start.10 = (bf16[256,1024]{1,0:T(8,128)(2,1)}, bf16[256,1024]{1,0:T(8,128)(2,1)}, u32[]{:S(2)}, u32[]{:S(2)}) collective-permute-start(bf16[256,1024]{1,0:T(8,128)(2,1)} %get-tuple-element.109), channel_id=1, source_target_pairs={{0,8},{4,12},{8,0},{12,4},{1,9},{5,13},{9,1},{13,5},{2,10},{6,14},... | collective-permute-start | bytes 1572872 | tf_op jit(solution)/shard_map/ppermute | solution.py:317
  51.1 20.4 %collective-permute-start.11 = (bf16[256,1024]{1,0:T(8,128)(2,1)}, bf16[256,1024]{1,0:T(8,128)(2,1)}, u32[]{:S(2)}, u32[]{:S(2)}) collective-permute-start(bf16[256,1024]{1,0:T(8,128)(2,1)} %collective-permute-done.5.refs_2_), channel_id=1, source_target_pairs={{0,16},{16,0},{1,17},{17,1},{2,18},{18,2},{3,19},{19,3},{4,20},{20... | collective-permute-start | bytes 1572872 | tf_op jit(solution)/shard_map/ppermute | solution.py:319
  52.6 18.9 %collective-permute-start.9 = (bf16[256,1024]{1,0:T(8,128)(2,1)S(1)}, bf16[256,1024]{1,0:T(8,128)(2,1)S(1)}, u32[]{:S(2)}, u32[]{:S(2)}) collective-permute-start(bf16[256,1024]{1,0:T(8,128)(2,1)S(1)} %collective-permute-done.6.refs_6_), channel_id=1, source_target_pairs={{0,4},{4,0},{8,12},{12,8},{1,5},{5,1},{9,13},{13,9},{2,6},{6,2},{1... | collective-permute-start | bytes 1572872 | tf_op jit(solution)/shard_map/ppermute | solution.py:318
  60.2 22.5 %collective-permute-start.12 = (bf16[256,1024]{1,0:T(8,128)(2,1)}, bf16[256,1024]{1,0:T(8,128)(2,1)}, u32[]{:S(2)}, u32[]{:S(2)}) collective-permute-start(bf16[256,1024]{1,0:T(8,128)(2,1)} %get-tuple-element.113), channel_id=1, source_target_pairs={{0,8},{4,12},{8,0},{12,4},{1,9},{5,13},{9,1},{13,5},{2,10},{6,14},... | collective-permute-start | bytes 1572872 | tf_op jit(solution)/shard_map/ppermute | solution.py:317
  62.3 20.4 %collective-permute-start.13 = (bf16[256,1024]{1,0:T(8,128)(2,1)}, bf16[256,1024]{1,0:T(8,128)(2,1)}, u32[]{:S(2)}, u32[]{:S(2)}) collective-permute-start(bf16[256,1024]{1,0:T(8,128)(2,1)} %collective-permute-done.7.refs_4_), channel_id=1, source_target_pairs={{0,16},{16,0},{1,17},{17,1},{2,18},{18,2},{3,19},{19,3},{4,20},{20... | collective-permute-start | bytes 1572872 | tf_op jit(solution)/shard_map/ppermute | solution.py:319
  71.5 27.3 %collective-permute-start.3 = (bf16[256,1024]{1,0:T(8,128)(2,1)}, bf16[256,1024]{1,0:T(8,128)(2,1)}, u32[]{:S(2)}, u32[]{:S(2)}) collective-permute-start(bf16[256,1024]{1,0:T(8,128)(2,1)} %collective-permute-done.1.refs_8_), channel_id=1, source_target_pairs={{0,4},{4,0},{8,12},{12,8},{1,5},{5,1},{9,13},{13,9},{2,6},{6,2},{1... | collective-permute-start | bytes 1572872 | tf_op jit(solution)/shard_map/ppermute | solution.py:318
  71.5 27.3 %collective-permute-start.15 = (bf16[256,1024]{1,0:T(8,128)(2,1)}, bf16[256,1024]{1,0:T(8,128)(2,1)}, u32[]{:S(2)}, u32[]{:S(2)}) collective-permute-start(bf16[256,1024]{1,0:T(8,128)(2,1)} %get-tuple-element.119), channel_id=1, source_target_pairs={{0,8},{4,12},{8,0},{12,4},{1,9},{5,13},{9,1},{13,5},{2,10},{6,14},... | collective-permute-start | bytes 1572872 | tf_op jit(solution)/shard_map/ppermute | solution.py:317
  73.6 25.1 %collective-permute-start.16 = (bf16[256,1024]{1,0:T(8,128)(2,1)}, bf16[256,1024]{1,0:T(8,128)(2,1)}, u32[]{:S(2)}, u32[]{:S(2)}) collective-permute-start(bf16[256,1024]{1,0:T(8,128)(2,1)} %collective-permute-done.10.refs_6_), channel_id=1, source_target_pairs={{0,16},{16,0},{1,17},{17,1},{2,18},{18,2},{3,19},{19,3},{4,20},{20... | collective-permute-start | bytes 1572872 | tf_op jit(solution)/shard_map/ppermute | solution.py:319
  82.7 16.5 %collective-permute-start.17 = (bf16[256,1024]{1,0:T(8,128)(2,1)}, bf16[256,1024]{1,0:T(8,128)(2,1)}, u32[]{:S(2)}, u32[]{:S(2)}) collective-permute-start(bf16[256,1024]{1,0:T(8,128)(2,1)} %collective-permute-done.12.refs_7_), channel_id=1, source_target_pairs={{0,16},{16,0},{1,17},{17,1},{2,18},{18,2},{3,19},{19,3},{4,20},{20... | collective-permute-start | bytes 1572872 | tf_op jit(solution)/shard_map/ppermute | solution.py:319
  84.8 13.9 %collective-permute-start.14 = (bf16[192,512]{1,0:T(8,128)(2,1)S(1)}, bf16[192,512]{1,0:T(8,128)(2,1)S(1)}, u32[]{:S(2)}, u32[]{:S(2)}) collective-permute-start(bf16[192,512]{1,0:T(8,128)(2,1)S(1)} %convert_element_type.38), channel_id=1, source_target_pairs={{0,1},{1,0},{2,3},{3,2},{4,5},{5,4},{6,7},{7,6},{8,9},{9,8},{10,11... | collective-permute-start | bytes 589832 | tf_op jit(solution)/shard_map/ppermute | solution.py:320
  99.2 20.5 %collective-permute-start.18 = (bf16[1792,1024]{1,0:T(8,128)(2,1)}, bf16[1792,1024]{1,0:T(8,128)(2,1)}, u32[]{:S(2)}, u32[]{:S(2)}) collective-permute-start(bf16[1792,1024]{1,0:T(8,128)(2,1)} %shard_map.102.refs_4_), channel_id=1, source_target_pairs={{0,4},{4,0},{8,12},{12,8},{1,5},{5,1},{9,13},{13,9},{2,6},{6,2},{1... | collective-permute-start | bytes 11010056 | tf_op jit(solution)/shard_map/ppermute | solution.py:318
  102.1 17.6 %collective-permute-start.19 = (bf16[768,1024]{1,0:T(8,128)(2,1)}, bf16[768,1024]{1,0:T(8,128)(2,1)}, u32[]{:S(2)}, u32[]{:S(2)}) collective-permute-start(bf16[768,1024]{1,0:T(8,128)(2,1)} %shard_map.103.refs_6_), channel_id=1, source_target_pairs={{0,4},{4,0},{8,12},{12,8},{1,5},{5,1},{9,13},{13,9},{2,6},{6,2},{1... | collective-permute-start | bytes 4718600 | tf_op jit(solution)/shard_map/ppermute | solution.py:318
  102.7 15.1 %collective-permute-start.20 = (bf16[256,1024]{1,0:T(8,128)(2,1)S(1)}, bf16[256,1024]{1,0:T(8,128)(2,1)S(1)}, u32[]{:S(2)}, u32[]{:S(2)}) collective-permute-start(bf16[256,1024]{1,0:T(8,128)(2,1)S(1)} %copy-done.8), channel_id=1, source_target_pairs={{0,8},{4,12},{8,0},{12,4},{1,9},{5,13},{9,1},{13,5},{2,10},{6,14},... | collective-permute-start | bytes 1572872 | tf_op jit(solution)/shard_map/ppermute | solution.py:317
  103.9 13.1 %collective-permute-start.21 = (bf16[192,512]{1,0:T(8,128)(2,1)S(1)}, bf16[192,512]{1,0:T(8,128)(2,1)S(1)}, u32[]{:S(2)}, u32[]{:S(2)}) collective-permute-start(bf16[192,512]{1,0:T(8,128)(2,1)S(1)} %fusion.12), channel_id=1, source_target_pairs={{0,2},{1,3},{2,0},{3,1},{4,6},{5,7},{6,4},{7,5},{8,10},{9,11},{10,... | collective-permute-start | bytes 589832 | tf_op jit(solution)/shard_map/ppermute | solution.py:320
  153.3 5.1 %collective-permute-start.25 = (f32[2,3,16,64]{3,2,1,0:T(8,128)S(1)}, f32[2,3,16,64]{3,2,1,0:T(8,128)S(1)}, u32[]{:S(2)}, u32[]{:S(2)}) collective-permute-start(f32[2,3,16,64]{3,2,1,0:T(8,128)S(1)} %dynamic-slice_bitcast_fusion.1), channel_id=1, source_target_pairs={{0,2},{1,3},{2,0},{3,1},{4,6},{5,7},{6,4},{7,5},{8,10},{9,11},{10,... | collective-permute-start | bytes 73736 | tf_op jit(solution)/shard_map/ppermute | solution.py:320
  (16 other events, 221.7 us)
Sparse Core Ops, SparseCore 0:
  8.9 83.5 all-gather.2

commit v6 on v5

--- a/solution.py
+++ b/solution.py
@@ -81,9 +81,9 @@
 
 
 def move_kernel(moves, n_in, *refs):
-    scal, ins, refs = refs[0], refs[1 : 1 + n_in], refs[1 + n_in :]
+    ins, refs = refs[:n_in], refs[n_in:]
     outs, (buf, sem) = refs[:-2], refs[-2:]
-    y, at, steps = scal[2], 0, []
+    y, at, steps = lax.axis_index("groups"), 0, []
     for i, (src, lead, row, dst, to, rows) in enumerate(moves):
         a = ins[src] if lead is None else ins[src].at[y if lead == "y" else lead]
         a = a.at[pl.ds(row, rows)]
@@ -111,7 +111,7 @@
     return pl.pallas_call(
         functools.partial(move_kernel, tuple(moves), len(ins)),
         out_shape=[jax.ShapeDtypeStruct((rows, width), kind) for rows in out_rows],
-        in_specs=[pl.BlockSpec(memory_space=pltpu.SMEM)] + [hbm] * len(ins),
+        in_specs=[hbm] * len(ins),
         out_specs=[hbm] * len(out_rows),
         scratch_shapes=[
             pltpu.VMEM((total, width), kind),
@@ -121,7 +121,7 @@
         cost_estimate=pl.CostEstimate(
             flops=0, bytes_accessed=4 * total * width, transcendentals=0
         ),
-    )(scal, *ins)
+    )(*ins)
 
 
 def join(scal, pieces):

time: 170 us -> 168 us (0.988)
  Pallas kernels: 48.4 us -> 45.7 us
    pallas_call x4, Pallas kernels: 12.9 us -> 10.2 us  [move(): pl.pallas_call(functools.partial(move_kernel, tuple(moves), len(ins)), ou...]
  transfers between devices with their start and end apart: 28 -> 28, of which waited for: 12 -> 13; matrix products, arithmetic and copies ran while one was open for 10% -> 10% of each run, Pallas kernels for 14% -> 12%
where the time goes in v6:
time: 168 us
  waiting for transfers between devices  54.8 us (33%)
  Pallas kernels  45.7 us (27%)
  starting transfers between devices  34.4 us (20%)
  matrix products  13.7 us (8%)
  between operations  13.7 us (8%)
  other arithmetic  4.01 us (2%)
    ppermute x9, waiting for transfers between devices, local(): over_x = lambda a: lax.ppermute(a, 'seq', [(i, i ^ 2) for i in range(4)])  44.3 us
    pallas_call x2, Pallas kernels, grads_call(): pl.pallas_call(functools.partial(grads_kernel, tiles, half, first, last),...  35.5 us
    ppermute x9, starting transfers between devices, local(): over_x = lambda a: lax.ppermute(a, 'seq', [(i, i ^ 2) for i in range(4)])  14.4 us
    ppermute x6, starting transfers between devices, local(): over_y = lambda a: lax.ppermute(a, 'groups', [(0, 1), (1, 0)])  10.9 us
    pallas_call x4, Pallas kernels, move(): pl.pallas_call(functools.partial(move_kernel, tuple(moves), len(ins)), ou...  10.2 us
    ppermute x4, starting transfers between devices, local(): lax.ppermute(a, 'tensor', [(i, i ^ k) for i in range(4)])  7.93 us
    dot_general x2, matrix products, local(): jnp.dot(a, spread, preferred_element_type=F32).astype(BF16)  6.01 us
    ppermute x4, waiting for transfers between devices, local(): lax.ppermute(a, 'tensor', [(i, i ^ k) for i in range(4)])  5.32 us
  transfers between devices with their start and end apart: 28, of which 13 were waited for; matrix products, arithmetic and copies ran while one was open for 10% of the time, Pallas kernels for 12%

profile of v6, /device:TPU:0, one launch (start us, length us, event | category | flops | bytes accessed | tf_op | source)
XLA Modules:
  0.0 167.9 jit_solution(18399915201071077298)
XLA Ops:
  9.2 3.0 %collective-permute-start = (bf16[256,1024]{1,0:T(8,128)(2,1)}, bf16[256,1024]{1,0:T(8,128)(2,1)S(1)}, u32[]{:S(2)}, u32[]{:S(2)}) collective-permute-start(bf16[256,1024]{1,0:T(8,128)(2,1)} %shard_map.101), channel_id=1, source_target_pairs={{0,8},{4,12},{8,0},{12,4},{1,9},{5,13},{9,1},{13,5},{2,10},{6,14},... | collective-permute-start | bytes 1572872 | tf_op jit(solution)/shard_map/ppermute | solution.py:317
  12.2 3.0 %shard_map.100 = (bf16[256,1024]{1,0:T(8,128)(2,1)}, bf16[256,1024]{1,0:T(8,128)(2,1)}, bf16[256,1024]{1,0:T(8,128)(2,1)}, bf16[256,1024]{1,0:T(8,128)(2,1)}, bf...) custom-call(bf16[2,1792,1024]{2,1,0:T(8,128)(2,1)} %bitcast.33), custom_call_target="tpu_custom_call" | custom-call | bytes 7340032 | tf_op jit(solution)/shard_map/pallas_call | solution.py:111
  16.8 8.3 %collective-permute-done.refs_4_ = bf16[256,1024]{1,0:T(8,128)(2,1)S(1)} collective-permute-done((bf16[256,1024]{1,0:T(8,128)(2,1)}, bf16[256,1024]{1,0:T(8,128)(2,1)S(1)}, u32[]{:S(2)}, u32[]{:S(2)}) %collective-permute-start) | collective-permute-done | bytes 524320 | tf_op jit(solution)/shard_map/ppermute | solution.py:317
  25.2 2.1 %collective-permute-start.6 = (bf16[256,1024]{1,0:T(8,128)(2,1)S(1)}, bf16[256,1024]{1,0:T(8,128)(2,1)S(1)}, u32[]{:S(2)}, u32[]{:S(2)}) collective-permute-start(bf16[256,1024]{1,0:T(8,128)(2,1)S(1)} %collective-permute-done.refs_4_), channel_id=1, source_target_pairs={{0,16},{16,0},{1,17},{17,1},{2,18},{18,2},{3,19},{19,3},{4,20},{20... | collective-permute-start | bytes 1572872 | tf_op jit(solution)/shard_map/ppermute | solution.py:319
  28.8 7.7 %collective-permute-done.1.refs_8_ = bf16[256,1024]{1,0:T(8,128)(2,1)} collective-permute-done((bf16[256,1024]{1,0:T(8,128)(2,1)}, bf16[256,1024]{1,0:T(8,128)(2,1)}, u32[]{:S(2)}, u32[]{:S(2)}) %collective-permute-start.1) | collective-permute-done | bytes 524320 | tf_op jit(solution)/shard_map/ppermute | solution.py:317
  36.5 2.1 %collective-permute-start.8 = (bf16[256,1024]{1,0:T(8,128)(2,1)}, bf16[256,1024]{1,0:T(8,128)(2,1)}, u32[]{:S(2)}, u32[]{:S(2)}) collective-permute-start(bf16[256,1024]{1,0:T(8,128)(2,1)} %collective-permute-done.1.refs_8_), channel_id=1, source_target_pairs={{0,16},{16,0},{1,17},{17,1},{2,18},{18,2},{3,19},{19,3},{4,20},{20... | collective-permute-start | bytes 1572872 | tf_op jit(solution)/shard_map/ppermute | solution.py:319
  40.1 4.6 %fusion.5 = f32[512,64]{0,1:T(8,128)S(1)} fusion(bf16[512,3584]{1,0:T(8,128)(2,1)} %refs_11_.3, bf16[512,3584]{1,0:T(8,128)(2,1)} %refs_10_.3, bf16[3584,192]{0,1:T(8,128)(2,1)} %param.16), kind=kOutput, calls=%fused_computation.9 | convolution fusion | flops 249561088 | bytes 7929856 | tf_op jit(solution)/shard_map/dot_general | solution.py:410
  45.3 2.4 %collective-permute-done.5.refs_1_ = bf16[256,1024]{1,0:T(8,128)(2,1)} collective-permute-done((bf16[256,1024]{1,0:T(8,128)(2,1)}, bf16[256,1024]{1,0:T(8,128)(2,1)}, u32[]{:S(2)}, u32[]{:S(2)}) %collective-permute-start.5) | collective-permute-done | bytes 524320 | tf_op jit(solution)/shard_map/ppermute | solution.py:317
  51.8 7.2 %collective-permute-done.7.refs_3_ = bf16[256,1024]{1,0:T(8,128)(2,1)} collective-permute-done((bf16[256,1024]{1,0:T(8,128)(2,1)}, bf16[256,1024]{1,0:T(8,128)(2,1)}, u32[]{:S(2)}, u32[]{:S(2)}) %collective-permute-start.7) | collective-permute-done | bytes 524320 | tf_op jit(solution)/shard_map/ppermute | solution.py:317
  62.6 7.6 %collective-permute-done.10.refs_5_ = bf16[256,1024]{1,0:T(8,128)(2,1)} collective-permute-done((bf16[256,1024]{1,0:T(8,128)(2,1)}, bf16[256,1024]{1,0:T(8,128)(2,1)}, u32[]{:S(2)}, u32[]{:S(2)}) %collective-permute-start.10) | collective-permute-done | bytes 524320 | tf_op jit(solution)/shard_map/ppermute | solution.py:317
  70.2 2.1 %collective-permute-start.15 = (bf16[256,1024]{1,0:T(8,128)(2,1)}, bf16[256,1024]{1,0:T(8,128)(2,1)}, u32[]{:S(2)}, u32[]{:S(2)}) collective-permute-start(bf16[256,1024]{1,0:T(8,128)(2,1)} %get-tuple-element.119), channel_id=1, source_target_pairs={{0,8},{4,12},{8,0},{12,4},{1,9},{5,13},{9,1},{13,5},{2,10},{6,14},... | collective-permute-start | bytes 1572872 | tf_op jit(solution)/shard_map/ppermute | solution.py:317
  73.9 7.6 %collective-permute-done.12.refs_6_ = bf16[256,1024]{1,0:T(8,128)(2,1)} collective-permute-done((bf16[256,1024]{1,0:T(8,128)(2,1)}, bf16[256,1024]{1,0:T(8,128)(2,1)}, u32[]{:S(2)}, u32[]{:S(2)}) %collective-permute-start.12) | collective-permute-done | bytes 524320 | tf_op jit(solution)/shard_map/ppermute | solution.py:317
  81.5 2.1 %collective-permute-start.17 = (bf16[256,1024]{1,0:T(8,128)(2,1)}, bf16[256,1024]{1,0:T(8,128)(2,1)}, u32[]{:S(2)}, u32[]{:S(2)}) collective-permute-start(bf16[256,1024]{1,0:T(8,128)(2,1)} %collective-permute-done.12.refs_6_), channel_id=1, source_target_pairs={{0,16},{16,0},{1,17},{17,1},{2,18},{18,2},{3,19},{19,3},{4,20},{20... | collective-permute-start | bytes 1572872 | tf_op jit(solution)/shard_map/ppermute | solution.py:319
  85.2 3.0 %shard_map.102.refs_4_ = bf16[1792,1024]{1,0:T(8,128)(2,1)} custom-call(bf16[256,1024]{1,0:T(8,128)(2,1)} %collective-permute-done.8.refs_0_, bf16[256,1024]{1,0:T(8,128)(2,1)} %collective-permute-done.5.refs_1_, bf16[256,1024]{1,0:T(8,128)(2,1)} %collective-permute-done.11.refs_2_, bf16[256,1024]{1,0:T(8,128)(2,1)} %collective-permute-done.7.refs_3_, ...), custom_call_target="tpu_custom_call" | custom-call | bytes 7340032 | tf_op jit(solution)/shard_map/pallas_call | solution.py:111
  88.3 3.0 %convolution_convert_fusion.refs_13_ = bf16[3584,256]{1,0:T(8,128)(2,1)} fusion(bf16[3584,192]{0,1:T(8,128)(2,1)} %param.16, s32[256]{0:T(256)S(1)} %fusion.26), kind=kOutput, calls=%fused_computation.7 | convolution fusion | flops 118374400 | bytes 2294784 | tf_op jit(solution)/shard_map/dot_general | solution.py:347
  91.3 3.0 %convolution_convert_fusion.1.refs_12_ = bf16[3584,256]{1,0:T(8,128)(2,1)} fusion(bf16[3584,192]{0,1:T(8,128)(2,1)} %param.16, s32[256]{0:T(256)S(1)} %fusion.26), kind=kOutput, calls=%fused_computation.8 | convolution fusion | flops 118374400 | bytes 2294784 | tf_op jit(solution)/shard_map/dot_general | solution.py:347
  94.3 2.6 %fusion.8.refs_17_ = f32[512,256]{1,0:T(8,128)} fusion(bf16[512,1024]{1,0:T(8,128)(2,1)S(1)} %copy-done.1, bf16[4096,64]{0,1:T(8,128)(2,1)} %param.17, s32[]{:T(128)S(6)} %select_n.132, s32[256]{0:T(256)S(1)} %fusion.26), kind=kOutput, calls=%fused_computation.12 | convolution fusion | flops 302268416 | bytes 1704964 | tf_op jit(solution)/shard_map/dot_general | solution.py:421
  98.0 2.2 %shard_map.103.refs_6_ = bf16[768,1024]{1,0:T(8,128)(2,1)} custom-call(bf16[256,1024]{1,0:T(8,128)(2,1)} %collective-permute-done.16.refs_0_, bf16[256,1024]{1,0:T(8,128)(2,1)} %collective-permute-done.17.refs_1_, bf16[256,1024]{1,0:T(8,128)(2,1)} %collective-permute-done.15.refs_2_), custom_call_target="tpu_custom_call" | custom-call | bytes 3145728 | tf_op jit(solution)/shard_map/pallas_call | solution.py:111
  102.0 2.7 %collective-permute-start.21 = (bf16[192,512]{1,0:T(8,128)(2,1)S(1)}, bf16[192,512]{1,0:T(8,128)(2,1)S(1)}, u32[]{:S(2)}, u32[]{:S(2)}) collective-permute-start(bf16[192,512]{1,0:T(8,128)(2,1)S(1)} %fusion.12), channel_id=1, source_target_pairs={{0,2},{1,3},{2,0},{3,1},{4,6},{5,7},{6,4},{7,5},{8,10},{9,11},{10,... | collective-permute-start | bytes 589832 | tf_op jit(solution)/shard_map/ppermute | solution.py:320
  104.6 10.4 %shard_map.104 = (f32[512,256]{1,0:T(8,128)}, f32[512,256]{1,0:T(8,128)}) custom-call(s32[3]{0:T(128)} %pad_add_fusion.refs_0_, bf16[4,512,1024]{2,1,0:T(8,128)(2,1)} %bitcast.34, bf16[3584,1024]{1,0:T(8,128)(2,1)} %refs_2_.3, bf16[3584,1024]{1,0:T(8,128)(2,1)} %collective-permute-done.2.refs_3_, bf16[256,1024]{1,0:T(8,128)(2,1)} %copy-done.2, ...), custom_call_target="tpu_custom_call" | custom-call | flops 3623878656 | bytes 12058624 | tf_op jit(solution)/shard_map/pallas_call | solution.py:281
  118.6 25.1 %shard_map.105 = (f32[2,4,3,16,64]{4,3,2,1,0:T(8,128)}, f32[2,4,3,16,64]{4,3,2,1,0:T(8,128)}) custom-call(s32[3]{0:T(128)} %pad_add_fusion.refs_0_, bf16[4,512,1024]{2,1,0:T(8,128)(2,1)} %bitcast.35, bf16[3584,1024]{1,0:T(8,128)(2,1)} %refs_2_.3, bf16[3584,1024]{1,0:T(8,128)(2,1)} %collective-permute-done.2.refs_3_, bf16[1792,1024]{1,0:T(8,128)(2,1)} %shard_map.102.refs_4_, ...), custom_call_target="tpu_custom_call" | custom-call | flops 13287555072 | bytes 33030144 | tf_op jit(solution)/shard_map/pallas_call | solution.py:281
  147.9 3.4 %collective-permute-done.24 = f32[4,3,16,64]{3,2,1,0:T(8,128)S(1)} collective-permute-done((f32[4,3,16,64]{3,2,1,0:T(8,128)S(1)}, f32[4,3,16,64]{3,2,1,0:T(8,128)S(1)}, u32[]{:S(2)}, u32[]{:S(2)}) %collective-permute-start.24) | collective-permute-done | bytes 49184 | tf_op jit(solution)/shard_map/ppermute | solution.py:317
  153.3 3.1 %collective-permute-done.25 = f32[2,3,16,64]{3,2,1,0:T(8,128)S(1)} collective-permute-done((f32[2,3,16,64]{3,2,1,0:T(8,128)S(1)}, f32[2,3,16,64]{3,2,1,0:T(8,128)S(1)}, u32[]{:S(2)}, u32[]{:S(2)}) %collective-permute-start.25) | collective-permute-done | bytes 24608 | tf_op jit(solution)/shard_map/ppermute | solution.py:320
  158.1 2.3 %collective-permute-done.26 = f32[3,16,64]{2,1,0:T(8,128)S(1)} collective-permute-done((f32[3,16,64]{2,1,0:T(8,128)S(1)}, f32[3,16,64]{2,1,0:T(8,128)S(1)}, u32[]{:S(2)}, u32[]{:S(2)}) %collective-permute-start.26) | collective-permute-done | bytes 12320 | tf_op jit(solution)/shard_map/ppermute | solution.py:320
  (89 shorter events, 33.6 us)
Async XLA Ops:
  6.5 90.4 %all-gather.3.cloned.1.call-start = ((), (), s32[]{:S(2)}) async-start(), calls=%async_computation | async-start | bytes 5242880 | tf_op jit(solution)/shard_map/all_gather | solution.py:336
  6.5 30.0 %collective-permute-start.2 = (bf16[3584,1024]{1,0:T(8,128)(2,1)}, bf16[3584,1024]{1,0:T(8,128)(2,1)}, u32[]{:S(2)}, u32[]{:S(2)}) collective-permute-start(bf16[3584,1024]{1,0:T(8,128)(2,1)} %refs_2_.3), channel_id=1, source_target_pairs={{0,4},{4,0},{8,12},{12,8},{1,5},{5,1},{9,13},{13,9},{2,6},{6,2},{1... | collective-permute-start | bytes 22020104 | tf_op jit(solution)/shard_map/ppermute | solution.py:318
  9.2 16.0 %collective-permute-start = (bf16[256,1024]{1,0:T(8,128)(2,1)}, bf16[256,1024]{1,0:T(8,128)(2,1)S(1)}, u32[]{:S(2)}, u32[]{:S(2)}) collective-permute-start(bf16[256,1024]{1,0:T(8,128)(2,1)} %shard_map.101), channel_id=1, source_target_pairs={{0,8},{4,12},{8,0},{12,4},{1,9},{5,13},{9,1},{13,5},{2,10},{6,14},... | collective-permute-start | bytes 1572872 | tf_op jit(solution)/shard_map/ppermute | solution.py:317
  15.2 21.3 %collective-permute-start.1 = (bf16[256,1024]{1,0:T(8,128)(2,1)}, bf16[256,1024]{1,0:T(8,128)(2,1)}, u32[]{:S(2)}, u32[]{:S(2)}) collective-permute-start(bf16[256,1024]{1,0:T(8,128)(2,1)} %get-tuple-element.89), channel_id=1, source_target_pairs={{0,8},{4,12},{8,0},{12,4},{1,9},{5,13},{9,1},{13,5},{2,10},{6,14},... | collective-permute-start | bytes 1572872 | tf_op jit(solution)/shard_map/ppermute | solution.py:317
  25.2 20.1 %collective-permute-start.4 = (bf16[256,1024]{1,0:T(8,128)(2,1)S(1)}, bf16[256,1024]{1,0:T(8,128)(2,1)S(1)}, u32[]{:S(2)}, u32[]{:S(2)}) collective-permute-start(bf16[256,1024]{1,0:T(8,128)(2,1)S(1)} %collective-permute-done.refs_4_), channel_id=1, source_target_pairs={{0,4},{4,0},{8,12},{12,8},{1,5},{5,1},{9,13},{13,9},{2,6},{6,2},{1... | collective-permute-start | bytes 1572872 | tf_op jit(solution)/shard_map/ppermute | solution.py:318
  25.2 20.1 %collective-permute-start.6 = (bf16[256,1024]{1,0:T(8,128)(2,1)S(1)}, bf16[256,1024]{1,0:T(8,128)(2,1)S(1)}, u32[]{:S(2)}, u32[]{:S(2)}) collective-permute-start(bf16[256,1024]{1,0:T(8,128)(2,1)S(1)} %collective-permute-done.refs_4_), channel_id=1, source_target_pairs={{0,16},{16,0},{1,17},{17,1},{2,18},{18,2},{3,19},{19,3},{4,20},{20... | collective-permute-start | bytes 1572872 | tf_op jit(solution)/shard_map/ppermute | solution.py:319
  27.3 20.4 %collective-permute-start.5 = (bf16[256,1024]{1,0:T(8,128)(2,1)}, bf16[256,1024]{1,0:T(8,128)(2,1)}, u32[]{:S(2)}, u32[]{:S(2)}) collective-permute-start(bf16[256,1024]{1,0:T(8,128)(2,1)} %get-tuple-element.99), channel_id=1, source_target_pairs={{0,8},{4,12},{8,0},{12,4},{1,9},{5,13},{9,1},{13,5},{2,10},{6,14},... | collective-permute-start | bytes 1572872 | tf_op jit(solution)/shard_map/ppermute | solution.py:317
  36.5 15.2 %collective-permute-start.8 = (bf16[256,1024]{1,0:T(8,128)(2,1)}, bf16[256,1024]{1,0:T(8,128)(2,1)}, u32[]{:S(2)}, u32[]{:S(2)}) collective-permute-start(bf16[256,1024]{1,0:T(8,128)(2,1)} %collective-permute-done.1.refs_8_), channel_id=1, source_target_pairs={{0,16},{16,0},{1,17},{17,1},{2,18},{18,2},{3,19},{19,3},{4,20},{20... | collective-permute-start | bytes 1572872 | tf_op jit(solution)/shard_map/ppermute | solution.py:319
  38.6 20.4 %collective-permute-start.7 = (bf16[256,1024]{1,0:T(8,128)(2,1)}, bf16[256,1024]{1,0:T(8,128)(2,1)}, u32[]{:S(2)}, u32[]{:S(2)}) collective-permute-start(bf16[256,1024]{1,0:T(8,128)(2,1)} %get-tuple-element.103), channel_id=1, source_target_pairs={{0,8},{4,12},{8,0},{12,4},{1,9},{5,13},{9,1},{13,5},{2,10},{6,14},... | collective-permute-start | bytes 1572872 | tf_op jit(solution)/shard_map/ppermute | solution.py:317
  47.8 22.5 %collective-permute-start.10 = (bf16[256,1024]{1,0:T(8,128)(2,1)}, bf16[256,1024]{1,0:T(8,128)(2,1)}, u32[]{:S(2)}, u32[]{:S(2)}) collective-permute-start(bf16[256,1024]{1,0:T(8,128)(2,1)} %get-tuple-element.109), channel_id=1, source_target_pairs={{0,8},{4,12},{8,0},{12,4},{1,9},{5,13},{9,1},{13,5},{2,10},{6,14},... | collective-permute-start | bytes 1572872 | tf_op jit(solution)/shard_map/ppermute | solution.py:317
  49.8 20.4 %collective-permute-start.11 = (bf16[256,1024]{1,0:T(8,128)(2,1)}, bf16[256,1024]{1,0:T(8,128)(2,1)}, u32[]{:S(2)}, u32[]{:S(2)}) collective-permute-start(bf16[256,1024]{1,0:T(8,128)(2,1)} %collective-permute-done.5.refs_1_), channel_id=1, source_target_pairs={{0,16},{16,0},{1,17},{17,1},{2,18},{18,2},{3,19},{19,3},{4,20},{20... | collective-permute-start | bytes 1572872 | tf_op jit(solution)/shard_map/ppermute | solution.py:319
  51.3 18.9 %collective-permute-start.9 = (bf16[256,1024]{1,0:T(8,128)(2,1)S(1)}, bf16[256,1024]{1,0:T(8,128)(2,1)S(1)}, u32[]{:S(2)}, u32[]{:S(2)}) collective-permute-start(bf16[256,1024]{1,0:T(8,128)(2,1)S(1)} %collective-permute-done.6.refs_6_), channel_id=1, source_target_pairs={{0,4},{4,0},{8,12},{12,8},{1,5},{5,1},{9,13},{13,9},{2,6},{6,2},{1... | collective-permute-start | bytes 1572872 | tf_op jit(solution)/shard_map/ppermute | solution.py:318
  59.0 22.5 %collective-permute-start.12 = (bf16[256,1024]{1,0:T(8,128)(2,1)}, bf16[256,1024]{1,0:T(8,128)(2,1)}, u32[]{:S(2)}, u32[]{:S(2)}) collective-permute-start(bf16[256,1024]{1,0:T(8,128)(2,1)} %get-tuple-element.113), channel_id=1, source_target_pairs={{0,8},{4,12},{8,0},{12,4},{1,9},{5,13},{9,1},{13,5},{2,10},{6,14},... | collective-permute-start | bytes 1572872 | tf_op jit(solution)/shard_map/ppermute | solution.py:317
  61.0 20.4 %collective-permute-start.13 = (bf16[256,1024]{1,0:T(8,128)(2,1)}, bf16[256,1024]{1,0:T(8,128)(2,1)}, u32[]{:S(2)}, u32[]{:S(2)}) collective-permute-start(bf16[256,1024]{1,0:T(8,128)(2,1)} %collective-permute-done.7.refs_3_), channel_id=1, source_target_pairs={{0,16},{16,0},{1,17},{17,1},{2,18},{18,2},{3,19},{19,3},{4,20},{20... | collective-permute-start | bytes 1572872 | tf_op jit(solution)/shard_map/ppermute | solution.py:319
  70.2 26.7 %collective-permute-start.3 = (bf16[256,1024]{1,0:T(8,128)(2,1)}, bf16[256,1024]{1,0:T(8,128)(2,1)}, u32[]{:S(2)}, u32[]{:S(2)}) collective-permute-start(bf16[256,1024]{1,0:T(8,128)(2,1)} %collective-permute-done.1.refs_8_), channel_id=1, source_target_pairs={{0,4},{4,0},{8,12},{12,8},{1,5},{5,1},{9,13},{13,9},{2,6},{6,2},{1... | collective-permute-start | bytes 1572872 | tf_op jit(solution)/shard_map/ppermute | solution.py:318
  70.2 26.7 %collective-permute-start.15 = (bf16[256,1024]{1,0:T(8,128)(2,1)}, bf16[256,1024]{1,0:T(8,128)(2,1)}, u32[]{:S(2)}, u32[]{:S(2)}) collective-permute-start(bf16[256,1024]{1,0:T(8,128)(2,1)} %get-tuple-element.119), channel_id=1, source_target_pairs={{0,8},{4,12},{8,0},{12,4},{1,9},{5,13},{9,1},{13,5},{2,10},{6,14},... | collective-permute-start | bytes 1572872 | tf_op jit(solution)/shard_map/ppermute | solution.py:317
  72.4 24.5 %collective-permute-start.16 = (bf16[256,1024]{1,0:T(8,128)(2,1)}, bf16[256,1024]{1,0:T(8,128)(2,1)}, u32[]{:S(2)}, u32[]{:S(2)}) collective-permute-start(bf16[256,1024]{1,0:T(8,128)(2,1)} %collective-permute-done.10.refs_5_), channel_id=1, source_target_pairs={{0,16},{16,0},{1,17},{17,1},{2,18},{18,2},{3,19},{19,3},{4,20},{20... | collective-permute-start | bytes 1572872 | tf_op jit(solution)/shard_map/ppermute | solution.py:319
  81.5 16.5 %collective-permute-start.17 = (bf16[256,1024]{1,0:T(8,128)(2,1)}, bf16[256,1024]{1,0:T(8,128)(2,1)}, u32[]{:S(2)}, u32[]{:S(2)}) collective-permute-start(bf16[256,1024]{1,0:T(8,128)(2,1)} %collective-permute-done.12.refs_6_), channel_id=1, source_target_pairs={{0,16},{16,0},{1,17},{17,1},{2,18},{18,2},{3,19},{19,3},{4,20},{20... | collective-permute-start | bytes 1572872 | tf_op jit(solution)/shard_map/ppermute | solution.py:319
  83.6 13.3 %collective-permute-start.14 = (bf16[192,512]{1,0:T(8,128)(2,1)S(1)}, bf16[192,512]{1,0:T(8,128)(2,1)S(1)}, u32[]{:S(2)}, u32[]{:S(2)}) collective-permute-start(bf16[192,512]{1,0:T(8,128)(2,1)S(1)} %convert_element_type.38), channel_id=1, source_target_pairs={{0,1},{1,0},{2,3},{3,2},{4,5},{5,4},{6,7},{7,6},{8,9},{9,8},{10,11... | collective-permute-start | bytes 589832 | tf_op jit(solution)/shard_map/ppermute | solution.py:320
  98.0 19.8 %collective-permute-start.18 = (bf16[1792,1024]{1,0:T(8,128)(2,1)}, bf16[1792,1024]{1,0:T(8,128)(2,1)}, u32[]{:S(2)}, u32[]{:S(2)}) collective-permute-start(bf16[1792,1024]{1,0:T(8,128)(2,1)} %shard_map.102.refs_4_), channel_id=1, source_target_pairs={{0,4},{4,0},{8,12},{12,8},{1,5},{5,1},{9,13},{13,9},{2,6},{6,2},{1... | collective-permute-start | bytes 11010056 | tf_op jit(solution)/shard_map/ppermute | solution.py:318
  100.2 17.6 %collective-permute-start.19 = (bf16[768,1024]{1,0:T(8,128)(2,1)}, bf16[768,1024]{1,0:T(8,128)(2,1)}, u32[]{:S(2)}, u32[]{:S(2)}) collective-permute-start(bf16[768,1024]{1,0:T(8,128)(2,1)} %shard_map.103.refs_6_), channel_id=1, source_target_pairs={{0,4},{4,0},{8,12},{12,8},{1,5},{5,1},{9,13},{13,9},{2,6},{6,2},{1... | collective-permute-start | bytes 4718600 | tf_op jit(solution)/shard_map/ppermute | solution.py:318
  101.4 14.5 %collective-permute-start.20 = (bf16[256,1024]{1,0:T(8,128)(2,1)S(1)}, bf16[256,1024]{1,0:T(8,128)(2,1)S(1)}, u32[]{:S(2)}, u32[]{:S(2)}) collective-permute-start(bf16[256,1024]{1,0:T(8,128)(2,1)S(1)} %copy-done.8), channel_id=1, source_target_pairs={{0,8},{4,12},{8,0},{12,4},{1,9},{5,13},{9,1},{13,5},{2,10},{6,14},... | collective-permute-start | bytes 1572872 | tf_op jit(solution)/shard_map/ppermute | solution.py:317
  102.0 13.1 %collective-permute-start.21 = (bf16[192,512]{1,0:T(8,128)(2,1)S(1)}, bf16[192,512]{1,0:T(8,128)(2,1)S(1)}, u32[]{:S(2)}, u32[]{:S(2)}) collective-permute-start(bf16[192,512]{1,0:T(8,128)(2,1)S(1)} %fusion.12), channel_id=1, source_target_pairs={{0,2},{1,3},{2,0},{3,1},{4,6},{5,7},{6,4},{7,5},{8,10},{9,11},{10,... | collective-permute-start | bytes 589832 | tf_op jit(solution)/shard_map/ppermute | solution.py:320
  151.3 5.1 %collective-permute-start.25 = (f32[2,3,16,64]{3,2,1,0:T(8,128)S(1)}, f32[2,3,16,64]{3,2,1,0:T(8,128)S(1)}, u32[]{:S(2)}, u32[]{:S(2)}) collective-permute-start(f32[2,3,16,64]{3,2,1,0:T(8,128)S(1)} %dynamic-slice_bitcast_fusion.1), channel_id=1, source_target_pairs={{0,2},{1,3},{2,0},{3,1},{4,6},{5,7},{6,4},{7,5},{8,10},{9,11},{10,... | collective-permute-start | bytes 73736 | tf_op jit(solution)/shard_map/ppermute | solution.py:320
  (16 other events, 218.9 us)
Sparse Core Ops, SparseCore 0:
  8.9 83.2 all-gather.2
